TPU v7x, 32 devices: a whole 2x2x4 slice. The times are simulated.
32 devices in a mesh: dp: 8 (over y, x, core), rows: 4 (over z).
Axes of the slice: x: 2, y: 2, z: 4, core: 2. Of those that a mesh axis runs over, the one named last changes fastest.
Arguments:
- tokens: bfloat16 [32768, 768], P(('dp', 'rows')), may hold values from -6 to 6
- segment_ids: int32 [32768], P(('dp', 'rows')), may hold values from 0 to 8, as said below
- true_counts: int32 [32], P(('dp', 'rows')), may hold values from 213 to 1024, as said below
- regroup: int32 [32], P(('dp', 'rows')), may hold values from 0 to 31, as said below
- cotangent: bfloat16 [32768, 768], P(('dp', 'rows')), may hold values from -12 to 12
- ln1_gain: float32 [768], replicated, may hold values from 0.5 to 1.5
- ln1_bias: float32 [768], replicated, may hold values from -1.75 to 1.75
- qkv_weight: bfloat16 [768, 2304], replicated, may hold values from -0.21875 to 0.21875
- qkv_bias: float32 [2304], replicated, may hold values from -1.75 to 1.75
- out_weight: bfloat16 [768, 768], replicated, may hold values from -1.5 to 1.5
- out_bias: float32 [768], replicated, may hold values from -1.75 to 1.75
- ln2_gain: float32 [768], replicated, may hold values from 0.5 to 1.5
- ln2_bias: float32 [768], replicated, may hold values from -1.75 to 1.75
- up_weight: bfloat16 [768, 3072], replicated, may hold values from -0.21875 to 0.21875
- up_bias: float32 [3072], replicated, may hold values from -1.75 to 1.75
- down_weight: bfloat16 [3072, 768], replicated, may hold values from -0.109375 to 0.109375
- down_bias: float32 [768], replicated, may hold values from -1.75 to 1.75
Outputs:
- out: bfloat16 [32768, 768], P(('dp', 'rows'))
- input_grad: bfloat16 [32768, 768], P(('dp', 'rows'))
- grad_ln1_gain: float32 [768], replicated
- grad_ln1_bias: float32 [768], replicated
- grad_qkv_weight: float32 [768, 2304], P('dp')
- grad_qkv_bias: float32 [2304], replicated
- grad_out_weight: float32 [768, 768], P('dp')
- grad_out_bias: float32 [768], replicated
- grad_ln2_gain: float32 [768], replicated
- grad_ln2_bias: float32 [768], replicated
- grad_up_weight: float32 [768, 3072], P('dp')
- grad_up_bias: float32 [3072], replicated
- grad_down_weight: float32 [3072, 768], P(None, 'dp')
- grad_down_bias: float32 [768], replicated
Inputs may be any that keep to these rules, and one draw needn't show every extreme that they name: `true_counts`: true tokens of each row; they fill its first positions, and some row is full. `segment_ids`: positions of a row carry cells 0 to 7 in order, each of 1 or more tokens, together filling the row's true count, then 8 on all padding positions. `regroup`: a permutation of the rows that maps every aligned block of 4 rows onto itself.
All inputs are finite; a program needn't handle non-finite values.
Results may differ from a plain program's by a relative error of at most 0.01.
Values may be sent and summed in bfloat16 or wider, within the bound.
A program may use at most 256 MiB of HBM per device.

v0:
```python
import jax
import jax.numpy as jnp
from jax import lax
from jax.sharding import PartitionSpec as P

HEAD_DIM = 64
ROT = 16


EPSILON = 1e-05
EXCLUDED = -1e30


def layer_norm(tensor, scales, shifts):
    centre = jnp.mean(tensor, axis=-1, keepdims=True)
    centred = tensor - centre
    spread = jnp.mean(centred * centred, axis=-1, keepdims=True)
    return centred * lax.rsqrt(spread + EPSILON) * scales + shifts


def rotate(tensor, cosine, sine_table):
    halfway = ROT // 2
    moving = tensor[..., :ROT]
    turned = jnp.concatenate([-moving[..., halfway:], moving[..., :halfway]], axis=-1)
    return jnp.concatenate([moving * cosine + turned * sine_table, tensor[..., ROT:]], axis=-1)


def angles(length):
    placed = jnp.arange(length, dtype=jnp.int32).astype(jnp.float32)
    rates = jnp.exp(
        jnp.arange(ROT // 2, dtype=jnp.float32) * (-2.0 / ROT) * jnp.log(jnp.float32(10000.0))
    )
    phases = placed[:, None] * rates[None, :]
    phases = jnp.concatenate([phases, phases], axis=1)
    return (jnp.cos(phases)[:, None, :], jnp.sin(phases)[:, None, :])


def contract(left, right, left_dim, right_dim):
    return lax.dot_general(
        left, right, (((left_dim,), (right_dim,)), ((), ())), preferred_element_type=jnp.float32
    )


def shards(
    tokens,
    segment_ids,
    true_counts,
    regroup,
    cotangent,
    ln1_gain,
    ln1_bias,
    qkv_weight,
    qkv_bias,
    out_weight,
    out_bias,
    ln2_gain,
    ln2_bias,
    up_weight,
    up_bias,
    down_weight,
    down_bias,
):
    length, model_width = cotangent.shape
    head_count = model_width // HEAD_DIM
    ff_width = up_weight.shape[1]
    source = regroup[0] % lax.axis_size("rows")
    piece = lax.all_gather(tokens, "rows", axis=0, tiled=True)
    offset = source * length
    inside = (offset >= 0) & (offset < piece.shape[0])
    bounded = jnp.clip(offset, 0, piece.shape[0] - length)
    taken = lax.dynamic_slice_in_dim(piece, bounded, length, 0)
    arrived = jnp.where(inside, taken, jnp.zeros_like(tokens))
    residual = arrived.astype(jnp.float32)
    cosine, sine_table = angles(length)
    live_rows = (jnp.arange(length, dtype=jnp.int32) < true_counts[0]).astype(jnp.float32)
    grad_out = cotangent.astype(jnp.float32) * live_rows[:, None]
    normed_one, pull_one = jax.vjp(layer_norm, residual, ln1_gain, ln1_bias)
    input_one = normed_one.astype(jnp.bfloat16)
    united_proj = jnp.dot(input_one, qkv_weight, preferred_element_type=jnp.float32) + qkv_bias
    head_shape = (length, head_count, HEAD_DIM)

    def rotate_both(query_pre, key_pre):
        return (rotate(query_pre, cosine, sine_table), rotate(key_pre, cosine, sine_table))

    (query_rot, key_rot), pull_rotate = jax.vjp(
        rotate_both,
        united_proj[:, :model_width].reshape(head_shape),
        united_proj[:, model_width : 2 * model_width].reshape(head_shape),
    )
    query_heads = query_rot.astype(jnp.bfloat16)
    key_heads = key_rot.astype(jnp.bfloat16)
    value_heads = united_proj[:, 2 * model_width :].reshape(head_shape).astype(jnp.bfloat16)
    span_rows = min(512, length)
    positions = jnp.arange(length, dtype=jnp.int32)
    scaling = HEAD_DIM ** (-0.5)

    def masked_scores(begin_row):
        ending = begin_row + span_rows
        products = (
            jnp.einsum(
                "qhe,khe->hqk",
                query_heads[begin_row:ending],
                key_heads,
                preferred_element_type=jnp.float32,
            )
            * scaling
        )
        allowed = (segment_ids[begin_row:ending, None] == segment_ids[None, :]) & (
            positions[None, :] <= positions[begin_row:ending, None]
        )
        return jnp.where(allowed[None], products, EXCLUDED)

    contexts = []
    log_sums = []
    for begin_row in range(0, length, span_rows):
        scores = masked_scores(begin_row)
        row_peak = jnp.max(scores, axis=-1, keepdims=True)
        log_sum = row_peak + jnp.log(jnp.sum(jnp.exp(scores - row_peak), axis=-1, keepdims=True))
        weights_low = jnp.exp(scores - log_sum).astype(jnp.bfloat16)
        contexts.append(
            jnp.einsum("hqk,khe->qhe", weights_low, value_heads, preferred_element_type=jnp.float32)
        )
        log_sums.append(log_sum)
    context = jnp.concatenate(contexts, axis=0).reshape(length, model_width).astype(jnp.bfloat16)
    attn_out = jnp.dot(context, out_weight, preferred_element_type=jnp.float32) + out_bias
    normed_two, pull_two = jax.vjp(layer_norm, residual, ln2_gain, ln2_bias)
    input_two = normed_two.astype(jnp.bfloat16)
    hidden = jnp.dot(input_two, up_weight, preferred_element_type=jnp.float32) + up_bias
    active_full, pull_gelu = jax.vjp(lambda inner: jax.nn.gelu(inner, approximate=False), hidden)
    active = active_full.astype(jnp.bfloat16)
    mlp_out = jnp.dot(active, down_weight, preferred_element_type=jnp.float32) + down_bias
    layer_out = (residual + attn_out + mlp_out).astype(jnp.bfloat16)
    grad_low = grad_out.astype(jnp.bfloat16)
    grad_active = contract(grad_low, down_weight, 1, 1)
    grad_hidden = pull_gelu(grad_active)[0].astype(jnp.bfloat16)
    grad_two = contract(grad_hidden, up_weight, 1, 1)
    grad_x_two, gain_two, shift_two = pull_two(grad_two)
    grad_context = contract(grad_low, out_weight, 1, 1).astype(jnp.bfloat16).reshape(head_shape)
    query_parts = []
    grad_keys = jnp.zeros(head_shape, jnp.float32)
    grad_values = jnp.zeros(head_shape, jnp.float32)
    for block_index, begin_row in enumerate(range(0, length, span_rows)):
        ending = begin_row + span_rows
        soft_full = jnp.exp(masked_scores(begin_row) - log_sums[block_index])
        soft_low = soft_full.astype(jnp.bfloat16)
        rows_grad = grad_context[begin_row:ending]
        probs_grad = jnp.einsum(
            "qhe,khe->hqk", rows_grad, value_heads, preferred_element_type=jnp.float32
        )
        inner_sum = jnp.sum(soft_full * probs_grad, axis=-1, keepdims=True)
        grad_scores = (soft_full * (probs_grad - inner_sum)).astype(jnp.bfloat16)
        query_parts.append(
            jnp.einsum("hqk,khe->qhe", grad_scores, key_heads, preferred_element_type=jnp.float32)
            * scaling
        )
        grad_keys = (
            grad_keys
            + jnp.einsum(
                "hqk,qhe->khe",
                grad_scores,
                query_heads[begin_row:ending],
                preferred_element_type=jnp.float32,
            )
            * scaling
        )
        grad_values = grad_values + jnp.einsum(
            "hqk,qhe->khe", soft_low, rows_grad, preferred_element_type=jnp.float32
        )
    grad_query = jnp.concatenate(query_parts, axis=0)
    query_back, key_back = pull_rotate((grad_query, grad_keys))
    grad_united = jnp.concatenate(
        [
            query_back.reshape(length, model_width),
            key_back.reshape(length, model_width),
            grad_values.reshape(length, model_width),
        ],
        axis=1,
    ).astype(jnp.bfloat16)
    grad_one = contract(grad_united, qkv_weight, 1, 1)
    grad_x_one, gain_one, shift_one = pull_one(grad_one)
    input_grad = (grad_out + grad_x_one + grad_x_two).astype(jnp.bfloat16)
    bias_qkv = jnp.sum(grad_united, axis=0, dtype=jnp.float32)
    bias_out = jnp.sum(grad_low, axis=0, dtype=jnp.float32)
    bias_up = jnp.sum(grad_hidden, axis=0, dtype=jnp.float32)
    own_count = true_counts[0].astype(jnp.float32)
    token_total = lax.psum(own_count, ("dp", "rows"))
    factor = 1.0 / token_total
    divisor = jnp.float32(1.0)
    vector_sums = lax.psum(
        (
            gain_one * factor,
            shift_one * factor,
            bias_qkv * factor,
            bias_out * factor,
            gain_two * factor,
            shift_two * factor,
            bias_up * factor,
        ),
        ("dp", "rows"),
    )
    partial_rows = lax.psum_scatter(
        jnp.concatenate(
            [
                contract(input_one, grad_united, 0, 0),
                contract(context, grad_low, 0, 0),
                contract(input_two, grad_hidden, 0, 0),
                contract(grad_low, active, 0, 0),
            ],
            axis=1,
        )
        * factor,
        "dp",
        scatter_dimension=0,
        tiled=True,
    )
    owned_rows = lax.psum_scatter(
        partial_rows.astype(jnp.bfloat16), "rows", scatter_dimension=0, tiled=True
    ).astype(jnp.float32)
    shard = lax.all_gather(owned_rows.astype(jnp.bfloat16), "rows", axis=0, tiled=True).astype(
        owned_rows.dtype
    )
    shard = shard / divisor
    grad_qkv_w = shard[:, : 3 * model_width]
    grad_out_w = shard[:, 3 * model_width : 4 * model_width]
    grad_up_w = shard[:, 4 * model_width : 4 * model_width + ff_width]
    grad_down_w = shard[:, 4 * model_width + ff_width :].T
    return (
        layer_out,
        input_grad,
        vector_sums[0],
        vector_sums[1],
        grad_qkv_w,
        vector_sums[2],
        grad_out_w,
        vector_sums[3],
        vector_sums[4],
        vector_sums[5],
        grad_up_w,
        vector_sums[6],
        grad_down_w,
        vector_sums[3],
    )


def solution(mesh):
    placed = (
        P(("dp", "rows"), None),
        P(("dp", "rows")),
        P(("dp", "rows")),
        P(("dp", "rows")),
        P(("dp", "rows"), None),
        P(),
        P(),
        P(),
        P(),
        P(),
        P(),
        P(),
        P(),
        P(),
        P(),
        P(),
        P(),
    )
    return jax.shard_map(
        shards,
        mesh=mesh,
        in_specs=placed,
        out_specs=(
            P(("dp", "rows"), None),
            P(("dp", "rows"), None),
            P(),
            P(),
            P("dp", None),
            P(),
            P("dp", None),
            P(),
            P(),
            P(),
            P("dp", None),
            P(),
            P(None, "dp"),
            P(),
        ),
        check_vma=False,
    )
```

profile of v0, /device:TPU:0, one launch (start us, length us, event | category | flops | bytes accessed | tf_op | source)
XLA Modules:
  0.0 793.1 jit_solution(7419020803447111221)
XLA Ops:
  8.9 45.5 %psum.56 = f32[]{:T(128)} all-reduce(f32[]{:T(128)S(6)} %convert_element_type.109), channel_id=1, replica_groups=mesh['dp'=8,'rows'=4] {'dp','rows'}, use_global_device_ids=true, to_apply=%region_13.14 | all-reduce | flops 1 | bytes 8 | tf_op jit(solution)/shard_map/psum | solution.py:186
  57.4 3.3 convolution_convert_fusion
  60.8 1.3 fusion.84
  62.0 2.0 fusion.33
  64.0 64.7 %all-gather.3.cloned.1.call-done = bf16[4096,768]{1,0:T(8,128)(2,1)} async-done(((bf16[1024,768]{1,0:T(8,128)(2,1)}), bf16[4096,768]{1,0:T(8,128)(2,1)}) %all-gather.3.cloned.1.call-update) | async-done | bytes 6291472 | tf_op jit(solution)/shard_map/all_gather | solution.py:67
  128.7 2.0 convert_reduce_fusion.2
  130.8 2.5 fusion.26
  134.4 5.9 convolution_add_fusion
  140.4 3.3 fusion.83
  143.7 2.2 copy-done.16
  146.0 3.6 copy.46
  149.5 2.1 slice_negate_fusion.2
  151.6 2.9 slice.161
  154.5 3.5 copy.45
  158.0 1.2 slice_negate_fusion.3
  159.2 1.9 slice.162
  161.2 3.6 slice.160
  164.8 1.8 fusion.39
  166.6 10.8 %fusion = (f32[12,512]{1,0:T(8,128)S(1)}, f32[12,512,1024]{2,1,0:T(8,128)}) fusion(pred[512,1024]{1,0:T(8,128)(4,1)S(1)} %copy-done.14, bf16[1024,12,48]{0,2,1:T(8,128)(2,1)S(1)} %copy-done.4, bf16[1024,12,16]{0,2,1:T(8,128)(2,1)S(1)} %get-tuple-element.49, bf16[1024,12,16]{0,2,1:T(8,128)(2,1)S(1)} %get-tuple-element.50, bf16[1024,12,48]{0,2,1:T(8,128)(2,1)S(1)} %slice.162), kind=kOutput, calls=%fused_computation.11 | convolution fusion | flops 828893184 | bytes 28860416 | tf_op jit(solution)/shard_map/qhe,khe->hqk/dot_general | solution.py:100
  177.4 11.8 %exponential_reduce_fusion.1 = f32[12,512]{1,0:T(8,128)S(1)} fusion(f32[12,512,1024]{2,1,0:T(8,128)} %get-tuple-element.66, f32[12,512]{1,0:T(8,128)S(1)} %get-tuple-element.65, pred[512,1024]{1,0:T(8,128)(4,1)S(1)} %copy-done.14), kind=kLoop, calls=%fused_computation.9 | loop fusion | flops 25159680 | bytes 25739264 | tf_op jit(solution)/shard_map/reduce_sum | solution.py:118
  189.8 2.6 copy.44
  192.4 12.3 %fusion.1 = (f32[12,512]{1,0:T(8,128)S(1)}, f32[12,512,1024]{2,1,0:T(8,128)}) fusion(pred[512,1024]{1,0:T(8,128)(4,1)} %get-tuple-element.59, bf16[1024,12,48]{0,2,1:T(8,128)(2,1)} %slice.161, bf16[1024,12,16]{0,2,1:T(8,128)(2,1)} %copy-done.19, bf16[1024,12,48]{0,2,1:T(8,128)(2,1)} %copy-done.2, bf16[1024,12,16]{0,2,1:T(8,128)(2,1)} %copy-done.17), kind=kOutput, calls=%fused_computation.12 | convolution fusion | flops 828893184 | bytes 28860416 | tf_op jit(solution)/shard_map/qhe,khe->hqk/dot_general | solution.py:100
  204.7 11.8 %exponential_reduce_fusion = f32[12,512]{1,0:T(8,128)S(1)} fusion(f32[12,512,1024]{2,1,0:T(8,128)} %get-tuple-element.64, f32[12,512]{1,0:T(8,128)S(1)} %get-tuple-element.63, pred[512,1024]{1,0:T(8,128)(4,1)S(1)} %copy-done.9), kind=kLoop, calls=%fused_computation.6 | loop fusion | flops 25159680 | bytes 25739264 | tf_op jit(solution)/shard_map/reduce_sum | solution.py:118
  217.2 18.9 %multiply_reduce_fusion.1 = (f32[12,512]{1,0:T(8,128)}, f32[12,512,1024]{2,1,0:T(8,128)}) fusion(f32[12,512,1024]{2,1,0:T(8,128)} %get-tuple-element.66, f32[12,512]{1,0:T(8,128)} %log_add_fusion.1, pred[512,1024]{1,0:T(8,128)(4,1)} %get-tuple-element.58, bf16[512,12,64]{0,2,1:T(8,128)(2,1)} %bitcast.74, bf16[1024,12,64]{0,2,1:T(8,128)(2,1)} %bitcast.56), kind=kOutput, calls=%fused_computation.4 | convolution fusion | flops 836757504 | bytes 53264384 | tf_op jit(solution)/shard_map/qhe,khe->hqk/dot_general | solution.py:147
  236.0 19.2 %multiply_reduce_fusion = (f32[12,512]{1,0:T(8,128)}, f32[12,512,1024]{2,1,0:T(8,128)}) fusion(f32[12,512,1024]{2,1,0:T(8,128)} %get-tuple-element.64, f32[12,512]{1,0:T(8,128)} %log_add_fusion, pred[512,1024]{1,0:T(8,128)(4,1)} %get-tuple-element.59, bf16[512,12,64]{0,2,1:T(8,128)(2,1)} %bitcast.72, bf16[1024,12,64]{0,2,1:T(8,128)(2,1)} %bitcast.57), kind=kOutput, calls=%fused_computation.2 | convolution fusion | flops 836757504 | bytes 53264384 | tf_op jit(solution)/shard_map/qhe,khe->hqk/dot_general | solution.py:147
  255.3 42.7 %multiply_convert_fusion = (bf16[12,512,1024]{2,1,0:T(8,128)(2,1)}, bf16[12,512,1024]{2,1,0:T(8,128)(2,1)}) fusion(f32[12,512,1024]{2,1,0:T(8,128)} %get-tuple-element.68, f32[12,512,1024]{2,1,0:T(8,128)} %get-tuple-element.64, f32[12,512]{1,0:T(8,128)} %get-tuple-element.67, f32[12,512]{1,0:T(8,128)} %log_add_fusion, ...), kind=kLoop, calls=%fused_computation.1 | loop fusion | flops 75497472 | bytes 126976000 | tf_op jit(solution)/shard_map/convert_element_type | solution.py:151
  298.0 10.2 %multiply_bitcast_fusion.2 = f32[512,12,64]{0,2,1:T(8,128)} fusion(bf16[12,512,1024]{2,1,0:T(8,128)(2,1)} %get-tuple-element.75, bf16[1024,12,48]{0,2,1:T(8,128)(2,1)} %slice.161, bf16[1024,12,16]{0,2,1:T(8,128)(2,1)} %copy-done.19), kind=kOutput, calls=%fused_computation.86 | convolution fusion | flops 808845312 | bytes 15728640 | tf_op jit(solution)/shard_map/hqk,khe->qhe/dot_general | solution.py:153
  308.3 7.0 fusion.63
  315.3 9.6 %multiply_bitcast_fusion.1 = f32[512,12,64]{0,2,1:T(8,128)} fusion(bf16[12,512,1024]{2,1,0:T(8,128)(2,1)} %get-tuple-element.74, bf16[1024,12,48]{0,2,1:T(8,128)(2,1)S(1)} %copy-done.5, bf16[1024,12,16]{0,2,1:T(8,128)(2,1)S(1)} %copy-done.20), kind=kOutput, calls=%fused_computation.85 | convolution fusion | flops 808845312 | bytes 15728640 | tf_op jit(solution)/shard_map/hqk,khe->qhe/dot_general | solution.py:153
  325.0 7.2 multiply_bitcast_fusion
  332.3 1.7 fusion.32
  334.0 1.6 broadcast_multiply_fusion
  336.9 13.3 %fusion.47 = f32[12,64,1024]{2,1,0:T(8,128)} fusion(bf16[512,12,64]{0,2,1:T(8,128)(2,1)S(1)} %bitcast.75, f32[12,512,1024]{2,1,0:T(8,128)} %get-tuple-element.66, f32[12,512]{1,0:T(8,128)S(1)} %copy-done.41, pred[512,1024]{1,0:T(8,128)(4,1)S(1)} %copy-done.15), kind=kOutput, calls=%fused_computation.116 | convolution fusion | flops 830472192 | bytes 29646848 | tf_op jit(solution)/shard_map/hqk,qhe->khe/dot_general | solution.py:166
  350.3 12.0 %fusion.35 = bf16[512,12,64]{0,2,1:T(8,128)(2,1)} fusion(bf16[1024,12,64]{0,2,1:T(8,128)(2,1)S(1)} %bitcast.58, f32[12,512,1024]{2,1,0:T(8,128)} %get-tuple-element.66, f32[12,512]{1,0:T(8,128)S(1)} %copy-done.41, pred[512,1024]{1,0:T(8,128)(4,1)S(1)} %copy-done.15), kind=kOutput, calls=%fused_computation.90 | convolution fusion | flops 830865408 | bytes 28073984 | tf_op jit(solution)/shard_map/hqk,khe->qhe/dot_general | solution.py:121
  362.2 12.0 %fusion.36 = bf16[512,12,64]{0,2,1:T(8,128)(2,1)} fusion(bf16[1024,12,64]{0,2,1:T(8,128)(2,1)S(1)} %bitcast.59, f32[12,512,1024]{2,1,0:T(8,128)} %get-tuple-element.64, f32[12,512]{1,0:T(8,128)S(1)} %copy-done.40, pred[512,1024]{1,0:T(8,128)(4,1)S(1)} %copy-done.10), kind=kOutput, calls=%fused_computation.91 | convolution fusion | flops 830865408 | bytes 28073984 | tf_op jit(solution)/shard_map/hqk,khe->qhe/dot_general | solution.py:121
  374.2 1.3 fusion.85
  375.6 13.9 %add_convert_fusion.2 = bf16[12,64,1024]{2,1,0:T(8,128)(2,1)} fusion(f32[12,64,1024]{2,1,0:T(8,128)} %fusion.47, bf16[512,12,64]{0,2,1:T(8,128)(2,1)S(1)} %bitcast.73, f32[12,512,1024]{2,1,0:T(8,128)} %get-tuple-element.64, f32[12,512]{1,0:T(8,128)S(1)} %copy-done.40, pred[512,1024]{1,0:T(8,128)(4,1)S(1)} %copy-done.10), kind=kOutput, calls=%fused_computation.67 | convolution fusion | flops 832045056 | bytes 31219712 | tf_op jit(solution)/shard_map/hqk,qhe->khe/dot_general | solution.py:166
  389.8 1.1 copy-done.29
  391.6 3.0 fusion.78
  394.6 38.3 %multiply_convert_fusion.2 = (bf16[1024,3072]{1,0:T(8,128)(2,1)S(1)}, f32[1024,3072]{1,0:T(8,128)}, f32[1024,3072]{1,0:T(8,128)}) fusion(f32[3072]{0:T(1024)S(1)} %copy-done.58, bf16[768,3072]{1,0:T(8,128)(2,1)} %param.30, f32[768]{0:T(1024)S(1)} %copy-done.59, f32[768]{0:T(1024)S(1)} %copy-done.48, f32[1024]{0:T(1024)S(1)} %copy-done.45, ...), kind=kOutput, calls=%fused_computation.19 | convolution fusion | flops 5044961280 | bytes 37775364 | tf_op jit(solution)/shard_map/dot_general | solution.py:128
  432.8 7.8 fusion.76
  441.0 1.3 copy-done.13
  442.4 1.4 add_convert_fusion.4
  443.8 1.4 add_convert_fusion.3
  445.2 19.3 %convert_reduce_fusion = (f32[3072]{0:T(1024)}, bf16[1024,3072]{1,0:T(8,128)(2,1)}) fusion(f32[1024,3072]{1,0:T(8,128)} %get-tuple-element.34, bf16[3072,768]{1,0:T(8,128)(2,1)} %param.32, bf16[1024,768]{1,0:T(8,128)(2,1)} %param.21, f32[1024]{0:T(1024)S(1)} %copy-done.53, f32[1024,3072]{1,0:T(8,128)} %get-tuple-element.62, f32[3072]{0:T(1024)} %param.31), kind=kOutput, calls=%fused_computation.17 | convolution fusion | flops 4887671808 | bytes 37777408 | tf_op jit(solution)/shard_map/dot_general | solution.py:39
  464.5 10.8 %fusion.66 = f32[768,3072]{1,0:T(8,128)} fusion(bf16[1024,3072]{1,0:T(8,128)(2,1)} %get-tuple-element.73, f32[768]{0:T(1024)} %param.29, f32[768]{0:T(1024)S(1)} %copy-done.48, f32[1024]{0:T(1024)S(1)} %copy-done.45, f32[1024]{0:T(1024)S(1)} %copy-done.43, bf16[4096,768]{1,0:T(8,128)(2,1)} %all-gather.3.cloned.1.call-done, s32[]{:T(128)S(6)} %min.4, ...), kind=kOutput, calls=%fused_computation.151 | convolution fusion | flops 4837343232 | bytes 17316868 | tf_op jit(solution)/shard_map/dot_general | solution.py:39
  475.3 8.9 %fusion.70 = f32[768,2304]{1,0:T(8,128)} fusion(f32[768]{0:T(1024)S(1)} %copy-done.61, f32[768]{0:T(1024)S(1)} %copy-done.50, f32[1024]{0:T(1024)S(1)} %copy-done.45, f32[1024]{0:T(1024)S(1)} %copy-done.43, bf16[1024,768]{0,1:T(8,128)(2,1)S(1)} %bitcast.80, bf16[1024,768]{0,1:T(8,128)(2,1)S(1)} %bitcast.71, bf16[1024,768]{0,1:T(8,128)(2,1)S(1)} %bitcast.68, ...), kind=kOutput, calls=%fused_computation.153 | convolution fusion | flops 3643539456 | bytes 13383685 | tf_op jit(solution)/shard_map/dot_general | solution.py:39
  484.2 20.0 %maximum_multiply_fusion = f32[768,9216]{1,0:T(8,128)} fusion(f32[768,3072]{1,0:T(8,128)} %fusion.76, f32[768,3072]{1,0:T(8,128)} %fusion.66, f32[768,768]{1,0:T(8,128)} %fusion.78, f32[768,2304]{1,0:T(8,128)} %fusion.70, f32[]{:T(128)S(6)} %div.41), kind=kLoop, calls=%fused_computation | loop fusion | flops 28311552 | bytes 56623108 | tf_op jit(solution)/shard_map/mul | solution.py:202
  504.3 9.8 %fusion.89 = f32[1024,768]{1,0:T(8,128)} fusion(bf16[1024,3072]{1,0:T(8,128)(2,1)} %get-tuple-element.73, bf16[768,3072]{1,0:T(8,128)(2,1)} %param.30), kind=kOutput, calls=%fused_computation.165 | convolution fusion | flops 4831838208 | bytes 14155776 | tf_op jit(solution)/shard_map/dot_general | solution.py:39
  514.1 161.8 %reduce-scatter.3.cloned.1.call-done = f32[96,9216]{1,0:T(8,128)} async-done(((f32[768,9216]{1,0:T(8,128)}), f32[96,9216]{1,0:T(8,128)}) %reduce-scatter.3.cloned.1.call-update) | async-done | bytes 3538960 | tf_op jit(solution)/shard_map/reduce_scatter | solution.py:201
  675.9 3.4 convert_element_type.110
  679.5 9.7 %fusion.27 = (f32[1024]{0:T(1024)S(1)}, f32[1024]{0:T(1024)S(1)}, f32[768]{0:T(1024)}, f32[1024,768]{1,0:T(8,128)S(1)}) fusion(f32[768]{0:T(1024)} %param.22, f32[1024]{0:T(1024)S(1)} %copy-done.43, bf16[4096,768]{1,0:T(8,128)(2,1)} %all-gather.3.cloned.1.call-done, s32[]{:T(128)S(6)} %min.4, pred[]{:T(512)S(6)} %and.25, f32[1024,768]{1,0:T(8,128)} %fusion.89, ...), kind=kOutput, calls=%fused_computation.58 | convolution fusion | flops 3645895936 | bytes 16143365 | tf_op jit(solution)/shard_map/dot_general | solution.py:39
  689.2 4.4 fusion.25
  693.6 4.9 convert_reduce_fusion.3
  700.3 17.6 %reduce-scatter.5.cloned.1.call-done = bf16[24,9216]{1,0:T(8,128)(2,1)} async-done(((bf16[96,9216]{1,0:T(8,128)(2,1)}), bf16[24,9216]{1,0:T(8,128)(2,1)}) %reduce-scatter.5.cloned.1.call-update) | async-done | bytes 442384 | tf_op jit(solution)/shard_map/reduce_scatter | solution.py:216
  717.9 1.3 broadcast_multiply_fusion.4
  719.2 2.7 convert_reduce_fusion.1
  721.9 1.3 broadcast_multiply_fusion.2
  723.3 43.2 %all-reduce.8 = (f32[768]{0:T(1024)}, f32[768]{0:T(1024)}, f32[2304]{0:T(1024)}, f32[768]{0:T(1024)}, f32[768]{0:T(1024)}, /*index=5*/f32[768]{0:T(1024)}, f32[3072]{0:T(1024)}) all-reduce(f32[768]{0:T(1024)} %broadcast_multiply_fusion.8, f32[768]{0:T(1024)} %broadcast_multiply_fusion.7, ...), channel_id=1, replica_groups=mesh['dp'=8,'rows'=4] {'dp','rows'}, use_global_device_ids=true, to_apply=%region_14.15 | all-reduce | flops 9216 | bytes 73728 | tf_op jit(solution)/shard_map/psum | solution.py:189
  766.4 8.7 %fusion.88 = f32[1024,768]{1,0:T(8,128)S(1)} fusion(bf16[1024,3072]{1,0:T(8,128)(2,1)} %copy-done.64, bf16[3072,768]{1,0:T(8,128)(2,1)} %param.32), kind=kOutput, calls=%fused_computation.164 | convolution fusion | flops 4831838208 | bytes 14155776 | tf_op jit(solution)/shard_map/dot_general | solution.py:131
  775.1 4.6 fusion.30
  779.7 1.9 convert_element_type.111
  781.7 1.1 slice_bitcast_fusion
  782.8 1.1 slice.132
  (166 shorter events, 11.9 us)
Async XLA Ops:
  7.2 127.2 %copy-start = (bf16[768,2304]{1,0:T(8,128)(2,1)S(1)}, bf16[768,2304]{1,0:T(8,128)(2,1)}, u32[]{:S(2)}) copy-start(bf16[768,2304]{1,0:T(8,128)(2,1)} %param.24) | copy-start | bytes 10616836
  7.2 121.5 %all-gather.3.cloned.1.call-start = ((), (), s32[]{:S(2)}) async-start(), calls=%async_computation.2 | async-start | bytes 7864320 | tf_op jit(solution)/shard_map/all_gather | solution.py:67
  7.9 668.0 %reduce-scatter.3.cloned.1.call-start = ((), (), s32[]{:S(2)}) async-start(), calls=%async_computation.3 | async-start | bytes 31850496 | tf_op jit(solution)/shard_map/reduce_scatter | solution.py:201
  55.8 4.9 copy-start.52
  60.7 1.3 copy-start.55
  60.7 73.7 %copy-start.49 = (f32[768]{0:T(1024)S(1)}, f32[768]{0:T(1024)}, u32[]{:S(2)}) copy-start(f32[768]{0:T(1024)} %param.22) | copy-start | bytes 9220
  60.7 73.7 %copy-start.60 = (f32[768]{0:T(1024)S(1)}, f32[768]{0:T(1024)}, u32[]{:S(2)}) copy-start(f32[768]{0:T(1024)} %param.23) | copy-start | bytes 9220
  130.7 3.1 copy-start.42
  140.4 5.6 copy-start.16
  159.2 5.6 copy-start.32
  159.2 5.6 copy-start.33
  159.2 5.6 copy-start.36
  159.2 5.6 copy-start.38
  161.1 5.5 copy-start.2
  161.2 5.5 copy-start.4
  161.2 5.5 copy-start.14
  166.6 10.8 %copy-start.17 = (bf16[1024,12,16]{0,2,1:T(8,128)(2,1)}, bf16[1024,12,16]{0,2,1:T(8,128)(2,1)S(1)}, u32[]{:S(2)}) copy-start(bf16[1024,12,16]{0,2,1:T(8,128)(2,1)S(1)} %get-tuple-element.50) | copy-start | bytes 1179652
  166.6 10.8 %copy-start.19 = (bf16[1024,12,16]{0,2,1:T(8,128)(2,1)}, bf16[1024,12,16]{0,2,1:T(8,128)(2,1)S(1)}, u32[]{:S(2)}) copy-start(bf16[1024,12,16]{0,2,1:T(8,128)(2,1)S(1)} %get-tuple-element.49) | copy-start | bytes 1179652
  192.4 12.3 %copy-start.9 = (pred[512,1024]{1,0:T(8,128)(4,1)S(1)}, pred[512,1024]{1,0:T(8,128)(4,1)}, u32[]{:S(2)}) copy-start(pred[512,1024]{1,0:T(8,128)(4,1)} %get-tuple-element.59) | copy-start | bytes 1572868
  298.0 10.3 %copy-start.3 = (bf16[1024,12,48]{0,2,1:T(8,128)(2,1)S(1)}, bf16[1024,12,48]{0,2,1:T(8,128)(2,1)}, u32[]{:S(2)}) copy-start(bf16[1024,12,48]{0,2,1:T(8,128)(2,1)} %copy-done.2) | copy-start | bytes 3538948
  298.0 10.3 %copy-start.18 = (bf16[1024,12,16]{0,2,1:T(8,128)(2,1)S(1)}, bf16[1024,12,16]{0,2,1:T(8,128)(2,1)}, u32[]{:S(2)}) copy-start(bf16[1024,12,16]{0,2,1:T(8,128)(2,1)} %copy-done.17) | copy-start | bytes 1179652
  308.3 7.0 copy-start.5
  308.3 7.0 copy-start.20
  325.0 7.2 copy-start.7
  325.0 7.3 copy-start.8
  332.2 108.4 %copy-start.1 = (f32[1024,12,64]{0,2,1:T(8,128)}, f32[1024,12,64]{0,2,1:T(8,128)S(1)}, u32[]{:S(2)}) copy-start(f32[1024,12,64]{0,2,1:T(8,128)S(1)} %multiply_bitcast_fusion) | copy-start | bytes 9437188
  332.2 1.7 copy-start.39
  336.9 13.3 %copy-start.6 = (bf16[1024,768]{0,1:T(8,128)(2,1)S(1)}, bf16[1024,768]{0,1:T(8,128)(2,1)}, u32[]{:S(2)}) copy-start(bf16[1024,768]{0,1:T(8,128)(2,1)} %copy.44) | copy-start | bytes 4718596
  350.2 12.0 %copy-start.10 = (pred[512,1024]{1,0:T(8,128)(4,1)S(1)}, pred[512,1024]{1,0:T(8,128)(4,1)}, u32[]{:S(2)}) copy-start(pred[512,1024]{1,0:T(8,128)(4,1)} %get-tuple-element.59) | copy-start | bytes 1572868
  350.2 12.0 %copy-start.40 = (f32[12,512]{1,0:T(8,128)S(1)}, f32[12,512]{1,0:T(8,128)}, u32[]{:S(2)}) copy-start(f32[12,512]{1,0:T(8,128)} %log_add_fusion) | copy-start | bytes 73732
  362.2 13.3 %copy-start.24 = (f32[1024,12,16]{0,2,1:T(8,128)S(1)}, f32[1024,12,16]{0,2,1:T(8,128)}, u32[]{:S(2)}) copy-start(f32[1024,12,16]{0,2,1:T(8,128)} %get-tuple-element.53) | copy-start | bytes 2359300
  374.2 1.4 copy-start.25
  375.6 13.9 %copy-start.34 = (bf16[512,12,64]{0,2,1:T(8,128)(2,1)S(1)}, bf16[512,12,64]{0,2,1:T(8,128)(2,1)}, u32[]{:S(2)}) copy-start(bf16[512,12,64]{0,2,1:T(8,128)(2,1)} %fusion.35) | copy-start | bytes 2359300
  375.6 13.9 %copy-start.35 = (bf16[512,12,64]{0,2,1:T(8,128)(2,1)S(1)}, bf16[512,12,64]{0,2,1:T(8,128)(2,1)}, u32[]{:S(2)}) copy-start(bf16[512,12,64]{0,2,1:T(8,128)(2,1)} %fusion.36) | copy-start | bytes 2359300
  389.5 2.0 copy-start.27
  389.5 2.0 copy-start.53
  391.5 3.0 copy-start.43
  391.5 3.0 copy-start.45
  391.5 3.0 copy-start.48
  391.5 3.0 copy-start.58
  391.5 3.0 copy-start.59
  432.8 7.9 copy-start.64
  432.8 7.9 copy-start.23
  432.8 7.9 copy-start.37
  440.7 1.7 copy-start.13
  441.0 2.7 slice-start
  464.5 10.8 %copy-start.21 = (bf16[1024,12,64]{0,2,1:T(8,128)(2,1)S(1)}, bf16[1024,12,64]{0,2,1:T(8,128)(2,1)}, u32[]{:S(2)}) copy-start(bf16[1024,12,64]{0,2,1:T(8,128)(2,1)} %add_convert_fusion.4) | copy-start | bytes 4718596
  464.5 10.8 %copy-start.22 = (bf16[1024,12,64]{0,2,1:T(8,128)(2,1)S(1)}, bf16[1024,12,64]{0,2,1:T(8,128)(2,1)}, u32[]{:S(2)}) copy-start(bf16[1024,12,64]{0,2,1:T(8,128)(2,1)} %add_convert_fusion.3) | copy-start | bytes 4718596
  464.5 10.8 %copy-start.31 = (bf16[12,64,1024]{2,1,0:T(8,128)(2,1)S(1)}, bf16[12,64,1024]{2,1,0:T(8,128)(2,1)}, u32[]{:S(2)}) copy-start(bf16[12,64,1024]{2,1,0:T(8,128)(2,1)} %add_convert_fusion.2) | copy-start | bytes 4718596
  464.5 10.8 %copy-start.50 = (f32[768]{0:T(1024)S(1)}, f32[768]{0:T(1024)}, u32[]{:S(2)}) copy-start(f32[768]{0:T(1024)} %param.22) | copy-start | bytes 9220
  464.5 10.8 %copy-start.61 = (f32[768]{0:T(1024)S(1)}, f32[768]{0:T(1024)}, u32[]{:S(2)}) copy-start(f32[768]{0:T(1024)} %param.23) | copy-start | bytes 9220
  504.3 213.6 %reduce-scatter.5.cloned.1.call-start = ((), (), s32[]{:S(2)}) async-start(), calls=%async_computation.4 | async-start | bytes 2211840 | tf_op jit(solution)/shard_map/reduce_scatter | solution.py:216
  679.4 9.8 %copy-start.47 = (f32[1024]{0:T(1024)S(1)}, f32[1024]{0:T(1024)}, u32[]{:S(2)}) copy-start(f32[1024]{0:T(1024)} %copy-done.46) | copy-start | bytes 12292
  679.4 100.3 %all-gather.5.cloned.1.call-start = ((), (), s32[]{:S(2)}) async-start(), calls=%async_computation.5 | async-start | bytes 2211840 | tf_op jit(solution)/shard_map/all_gather | solution.py:219
  679.4 9.7 %copy-start.11 = (f32[1024,768]{1,0:T(8,128)S(1)}, f32[1024,768]{1,0:T(8,128)}, u32[]{:S(2)}) copy-start(f32[1024,768]{1,0:T(8,128)} %fusion.89) | copy-start | bytes 9437188
  679.4 9.7 %copy-start.51 = (f32[768]{0:T(1024)S(1)}, f32[768]{0:T(1024)}, u32[]{:S(2)}) copy-start(f32[768]{0:T(1024)} %param.22) | copy-start | bytes 9220
  689.2 4.4 copy-start.28
  689.2 4.4 copy-start.54
  766.4 8.7 %copy-start.30 = (bf16[1024,12,64]{0,2,1:T(8,128)(2,1)S(1)}, bf16[1024,12,64]{0,2,1:T(8,128)(2,1)}, u32[]{:S(2)}) copy-start(bf16[1024,12,64]{0,2,1:T(8,128)(2,1)} %copy-done.29) | copy-start | bytes 4718596
  766.4 8.7 %copy-start.57 = (bf16[768,768]{1,0:T(8,128)(2,1)S(1)}, bf16[768,768]{1,0:T(8,128)(2,1)}, u32[]{:S(2)}) copy-start(bf16[768,768]{1,0:T(8,128)(2,1)} %param.26) | copy-start | bytes 3538948
  766.4 8.7 %copy-start.62 = (f32[768]{0:T(1024)S(1)}, f32[768]{0:T(1024)}, u32[]{:S(2)}) copy-start(f32[768]{0:T(1024)} %param.33) | copy-start | bytes 9220
  766.4 8.7 %copy-start.63 = (f32[768]{0:T(1024)S(1)}, f32[768]{0:T(1024)}, u32[]{:S(2)}) copy-start(f32[768]{0:T(1024)} %param.27) | copy-start | bytes 9220
  779.7 3.0 copy-start.12
  781.6 3.9 copy-start.56
  (6 other events, 6.0 us)
Sparse Core Ops, SparseCore 0:
  9.6 119.0 all-gather.2
  504.4 171.4 reduce-scatter.2
  679.5 38.3 reduce-scatter.4
  719.4 40.4 all-gather.4
where the time goes:
time: 802 us; the launch traced here: 793 us
  matrix products  277 us (35%)
  waiting for transfers between devices  245 us (31%)
  other arithmetic  130 us (16%)
  blocking collectives  88.6 us (11%)
  local copies, waits for them, and re-layouts  36 us (4%)
  between operations  17.3 us (2%)
    reduce_scatter x1, waiting for transfers between devices, shards(): lax.psum_scatter(jnp.concatenate([contract(input_one, grad_united, 0, 0),...  162 us
    dot_general x8, matrix products, contract(): lax.dot_general(left, right, (((left_dim,), (right_dim,)), ((), ())), pre...  72.6 us
    all_gather x1, waiting for transfers between devices, shards(): piece = lax.all_gather(tokens, 'rows', axis=0, tiled=True)  64.7 us
    psum x1, blocking collectives, shards(): token_total = lax.psum(own_count, ('dp', 'rows'))  45.5 us
    psum x1, blocking collectives, shards(): lax.psum((gain_one * factor, shift_one * factor, bias_qkv * factor, bias_...  43.2 us
    convert_element_type x1, other arithmetic, shards(): grad_scores = (soft_full * (probs_grad - inner_sum)).astype(jnp.bfloat16)  42.7 us
    dot_general x1, matrix products, shards(): jnp.dot(input_two, up_weight, preferred_element_type=jnp.float32) + up_bias  38.3 us
    dot_general x2, matrix products, shards(): jnp.einsum('qhe,khe->hqk', rows_grad, value_heads, preferred_element_type...  38.1 us
  transfers between devices with their start and end apart: 4, of which 3 were waited for; matrix products, arithmetic and copies ran while one was open for 7% of the time, Pallas kernels for 0%

commit v1 on v0

v1 whole, which is shorter than its diff:
```python
import functools
import numpy as np
import jax
import jax.numpy as jnp
from jax import lax
from jax.experimental import pallas as pl
from jax.experimental.pallas import tpu as pltpu
from jax.sharding import PartitionSpec as P

HEAD_DIM = 64
ROT = 16
PAIR = 128
EPSILON = 1e-05
EXCLUDED = -1e30
F32 = jnp.float32
BF16 = jnp.bfloat16


def nn(a, b):
    return lax.dot_general(a, b, (((1,), (0,)), ((), ())), preferred_element_type=F32)


def nt(a, b):
    return lax.dot_general(a, b, (((1,), (1,)), ((), ())), preferred_element_type=F32)


def tn(a, b):
    return lax.dot_general(a, b, (((0,), (0,)), ((), ())), preferred_element_type=F32)


def rotary_tables(length):
    half = ROT // 2
    placed = np.arange(length, dtype=np.float32)
    rates = np.exp(np.arange(half, dtype=np.float32) * np.float32(-2.0 / ROT) * np.log(np.float32(10000.0)))
    phases = placed[:, None] * rates[None, :].astype(np.float32)
    cosine = np.ones((length, HEAD_DIM), np.float32)
    sine = np.zeros((length, HEAD_DIM), np.float32)
    cosine[:, :half] = np.cos(phases)
    cosine[:, half:ROT] = np.cos(phases)
    sine[:, :half] = -np.sin(phases)
    sine[:, half:ROT] = np.sin(phases)
    return np.tile(cosine, (1, PAIR // HEAD_DIM)), np.tile(sine, (1, PAIR // HEAD_DIM))


def turned(u):
    lane = lax.broadcasted_iota(jnp.int32, u.shape, 1) % HEAD_DIM
    half = ROT // 2
    return jnp.where(lane < half, pltpu.roll(u, PAIR - half, 1), pltpu.roll(u, half, 1))


def gelu_parts(h):
    e = jnp.exp(h * h * -0.5)
    t = 1.0 / (1.0 + 0.2316418882 * jnp.abs(h))
    poly = t * (0.127414796 + t * (-0.142248368 + t * (0.7107068705 + t * (-0.7265760135 + t * 0.5307027145))))
    tail = poly * e
    phi = jnp.where(h >= 0, 1.0 - tail, tail)
    return h * phi, phi + h * (e * 0.3989422804014327)


def front_body(count_ref, x_ref, cot_ref, cos_ref, sin_ref, g1_ref, b1_ref, wqkv_ref, bqkv_ref, wout_ref, bout_ref,
               g2_ref, b2_ref, wup_ref, bup_ref, wdown_ref, bdown_ref,
               q_ref, k_ref, v_ref, gc_ref, n1_ref, n2_ref, gl_ref, act_ref, gh_ref, base_ref, t2_ref,
               gain2_ref, shift2_ref, bup_out, bout_out, *, tile):
    step = pl.program_id(0)
    rows, width = x_ref.shape
    pairs = width // PAIR
    ff = wup_ref.shape[1]
    x = x_ref[...].astype(F32)
    centred = x - jnp.mean(x, axis=1, keepdims=True)
    r = lax.rsqrt(jnp.mean(centred * centred, axis=1, keepdims=True) + EPSILON)
    n = centred * r
    n1 = (n * g1_ref[...] + b1_ref[...]).astype(BF16)
    n2 = (n * g2_ref[...] + b2_ref[...]).astype(BF16)
    n1_ref[...] = n1
    n2_ref[...] = n2
    place = step * rows + lax.broadcasted_iota(jnp.int32, (rows, 1), 0)
    gl = jnp.where(place < count_ref[0], cot_ref[...].astype(F32), 0.0)
    gl16 = gl.astype(BF16)
    gl_ref[...] = gl16

    @pl.when(step == 0)
    def _():
        gain2_ref[...] = jnp.zeros_like(gain2_ref)
        shift2_ref[...] = jnp.zeros_like(shift2_ref)
        bup_out[...] = jnp.zeros_like(bup_out)
        bout_out[...] = jnp.zeros_like(bout_out)

    bout_out[...] += jnp.sum(gl, axis=0, keepdims=True)
    cosine, sine = cos_ref[...], sin_ref[...]
    for p in range(pairs):
        cols = slice(p * PAIR, (p + 1) * PAIR)
        for which, ref in enumerate((q_ref, k_ref, v_ref)):
            wide = slice(which * width + p * PAIR, which * width + (p + 1) * PAIR)
            u = nn(n1, wqkv_ref[:, wide]) + bqkv_ref[:, wide]
            if which < 2:
                u = u * cosine + turned(u) * sine
            if which == 0:
                u = u * (HEAD_DIM ** -0.5)
            ref[p] = u.astype(BF16)
        gc_ref[p] = nt(gl16, wout_ref[cols, :]).astype(BF16)
    mlp = x + (bdown_ref[...] + bout_ref[...])
    grad_two = jnp.zeros((rows, width), F32)
    for f in range(0, ff, tile):
        cols = slice(f, f + tile)
        h = nn(n2, wup_ref[:, cols]) + bup_ref[:, cols]
        ga = nt(gl16, wdown_ref[cols, :])
        a, slope = gelu_parts(h)
        a16 = a.astype(BF16)
        gh = ga * slope
        gh16 = gh.astype(BF16)
        act_ref[:, cols] = a16
        gh_ref[:, cols] = gh16
        bup_out[:, cols] += jnp.sum(gh16.astype(F32), axis=0, keepdims=True)
        mlp = mlp + nn(a16, wdown_ref[cols, :])
        grad_two = grad_two + nt(gh16, wup_ref[:, cols])
    base_ref[...] = mlp
    t2_ref[...] = grad_two * g2_ref[...]
    gain2_ref[...] += jnp.sum(grad_two * n, axis=0, keepdims=True)
    shift2_ref[...] += jnp.sum(grad_two, axis=0, keepdims=True)


def front(count, x, cot, cosine, sine, g1, b1, wqkv, bqkv, wout, bout, g2, b2, wup, bup, wdown, bdown, rows=256, tile=512):
    length, width = x.shape
    ff = wup.shape[1]
    pairs = width // PAIR
    once = pl.Buffered(1)

    def row(cols):
        return pl.BlockSpec((rows, cols), lambda i: (i, 0))

    def whole(a):
        return pl.BlockSpec(a.shape, lambda i: (0,) * a.ndim, pipeline_mode=once)

    heads = pl.BlockSpec((pairs, rows, PAIR), lambda i: (0, i, 0))

    def vec(cols):
        return pl.BlockSpec((1, cols), lambda i: (0, 0))

    vectors = [v.reshape(1, -1) for v in (g1, b1, bqkv, bout, g2, b2, bup, bdown)]
    g1, b1, bqkv, bout, g2, b2, bup, bdown = vectors
    s = jax.ShapeDtypeStruct
    return pl.pallas_call(
        functools.partial(front_body, tile=tile),
        grid=(length // rows,),
        in_specs=[pl.BlockSpec(memory_space=pltpu.SMEM), row(width), row(width), row(PAIR), row(PAIR)]
        + [whole(a) for a in (g1, b1, wqkv, bqkv, wout, bout, g2, b2, wup, bup, wdown, bdown)],
        out_specs=[heads] * 4 + [row(width)] * 3 + [row(ff)] * 2 + [row(width)] * 2 + [vec(width), vec(width), vec(ff), vec(width)],
        out_shape=[s((pairs, length, PAIR), BF16)] * 4 + [s((length, width), BF16)] * 3 + [s((length, ff), BF16)] * 2
        + [s((length, width), F32)] * 2 + [s((1, width), F32), s((1, width), F32), s((1, ff), F32), s((1, width), F32)],
        compiler_params=pltpu.CompilerParams(vmem_limit_bytes=56 * 2**20),
        name="front",
    )(count, x, cot, cosine, sine, g1, b1, wqkv, bqkv, wout, bout, g2, b2, wup, bup, wdown, bdown)


def attention_body(first_ref, q_ref, k_ref, v_ref, gc_ref, segc_ref, segr_ref, cos_ref, sin_ref,
                   ctx_ref, gq_ref, gk_ref, gv_ref, dk_acc, dv_acc, *, rows):
    length = q_ref.shape[1]
    lane = lax.broadcasted_iota(jnp.int32, (rows, PAIR), 1)
    low = lane < HEAD_DIM
    dk_acc[...] = jnp.zeros_like(dk_acc)
    dv_acc[...] = jnp.zeros_like(dv_acc)

    def block(b, blocks):
        begin = pl.multiple_of(b * rows, rows)
        start = pl.multiple_of((b + 1 - blocks) * rows, rows)
        span = blocks * rows
        q = q_ref[0, pl.ds(begin, rows), :]
        g = gc_ref[0, pl.ds(begin, rows), :]
        zero = jnp.zeros_like(q)
        q2 = jnp.concatenate([jnp.where(low, q, zero), jnp.where(low, zero, q)], axis=0)
        g2 = jnp.concatenate([jnp.where(low, g, zero), jnp.where(low, zero, g)], axis=0)
        k = k_ref[0, pl.ds(start, span), :]
        v = v_ref[0, pl.ds(start, span), :]
        segt = segc_ref[pl.ds(begin, rows), :]
        segs = segr_ref[:, pl.ds(start, span)]
        t_at = begin + lax.broadcasted_iota(jnp.int32, (rows, span), 0)
        s_at = start + lax.broadcasted_iota(jnp.int32, (rows, span), 1)
        allowed = (segt == segs) & (s_at <= t_at)
        allowed = jnp.concatenate([allowed, allowed], axis=0)
        scores = jnp.where(allowed, nt(q2, k), EXCLUDED)
        peak = jnp.max(scores, axis=1, keepdims=True)
        e = jnp.exp(scores - peak)
        p = e * (1.0 / jnp.sum(e, axis=1, keepdims=True))
        p16 = p.astype(BF16)
        c2 = nn(p16, v)
        ctx_ref[pl.ds(begin, rows), :] = jnp.where(low, c2[:rows], c2[rows:]).astype(BF16)
        dp = nt(g2, v)
        inner = jnp.sum(p * dp, axis=1, keepdims=True)
        ds16 = (p * (dp - inner)).astype(BF16)
        d2 = nn(ds16, k)
        dq = jnp.where(low, d2[:rows], d2[rows:]) * (HEAD_DIM ** -0.5)
        cosine = cos_ref[pl.ds(begin, rows), :]
        sine = sin_ref[pl.ds(begin, rows), :]
        gq_ref[pl.ds(begin, rows), :] = (dq * cosine - turned(dq) * sine).astype(BF16)
        dk_acc[pl.ds(start, span), :] += tn(ds16, q2)
        dv_acc[pl.ds(start, span), :] += tn(p16, g2)

    total = length // rows

    def loop(b, carry):
        count = b + 1 - first_ref[b]
        for blocks in range(1, total + 1):
            @pl.when(count == blocks)
            def _():
                block(b, blocks)
        return carry

    lax.fori_loop(0, total, loop, 0)
    dk = dk_acc[...]
    gk_ref[...] = (dk * cos_ref[...] - turned(dk) * sin_ref[...]).astype(BF16)
    gv_ref[...] = dv_acc[...].astype(BF16)


def attention(q, k, v, gc, segment, cosine, sine, rows=128):
    pairs, length, _ = q.shape
    total = length // rows
    begins = jnp.sum((segment[None, :] < segment[::rows, None]).astype(jnp.int32), axis=1)
    first = begins // rows
    head = pl.BlockSpec((1, length, PAIR), lambda h, *_: (h, 0, 0))
    cols = pl.BlockSpec((length, PAIR), lambda h, *_: (0, h))
    s = jax.ShapeDtypeStruct((length, pairs * PAIR), BF16)

    def whole(shape):
        return pl.BlockSpec(shape, lambda h, *_: (0, 0), pipeline_mode=pl.Buffered(1))

    return pl.pallas_call(
        functools.partial(attention_body, rows=rows),
        grid_spec=pltpu.PrefetchScalarGridSpec(
            num_scalar_prefetch=1,
            grid=(pairs,),
            in_specs=[head] * 4 + [whole((length, 1)), whole((1, length)), whole((length, PAIR)), whole((length, PAIR))],
            out_specs=[cols] * 4,
            scratch_shapes=[pltpu.VMEM((length, PAIR), F32)] * 2,
        ),
        out_shape=[s] * 4,
        compiler_params=pltpu.CompilerParams(vmem_limit_bytes=56 * 2**20),
        name="attention",
    )(first, q, k, v, gc, segment.reshape(-1, 1), segment.reshape(1, -1), cosine, sine)


def shards(tokens, segment_ids, true_counts, regroup, cotangent, ln1_gain, ln1_bias, qkv_weight, qkv_bias, out_weight,
           out_bias, ln2_gain, ln2_bias, up_weight, up_bias, down_weight, down_bias):
    length, width = cotangent.shape
    source = regroup[0] % lax.axis_size("rows")
    piece = lax.all_gather(tokens, "rows", axis=0, tiled=True)
    arrived = lax.dynamic_slice_in_dim(piece, source * length, length, 0)
    cosine, sine = (jnp.asarray(t) for t in rotary_tables(length))
    (q, k, v, gc, n1, n2, gl, act, gh, base, t2, gain2, shift2, bias_up, bias_out) = front(
        true_counts, arrived, cotangent, cosine, sine, ln1_gain, ln1_bias, qkv_weight, qkv_bias, out_weight, out_bias,
        ln2_gain, ln2_bias, up_weight, up_bias, down_weight, down_bias)
    mlp_part = jnp.concatenate([tn(n2, gh), tn(gl, act)], axis=1).astype(BF16)
    mlp_rows = lax.psum(lax.psum_scatter(mlp_part, "dp", scatter_dimension=0, tiled=True), "rows")
    ctx, gq, gk, gv = attention(q, k, v, gc, segment_ids, cosine, sine, rows=256)
    out = (base + nn(ctx, out_weight)).astype(BF16)
    gu = jnp.concatenate([gq, gk, gv], axis=1)
    g1 = nt(gu, qkv_weight)
    x = arrived.astype(F32)
    centred = x - jnp.mean(x, axis=1, keepdims=True)
    r = lax.rsqrt(jnp.mean(centred * centred, axis=1, keepdims=True) + EPSILON)
    n = centred * r
    gain1 = jnp.sum(g1 * n, axis=0)
    shift1 = jnp.sum(g1, axis=0)
    t = g1 * ln1_gain + t2
    dx = r * (t - jnp.mean(t, axis=1, keepdims=True) - n * jnp.mean(t * n, axis=1, keepdims=True))
    input_grad = (gl.astype(F32) + dx).astype(BF16)
    attn_part = jnp.concatenate([tn(n1, gu), tn(ctx, gl)], axis=1).astype(BF16)
    attn_rows = lax.psum(lax.psum_scatter(attn_part, "dp", scatter_dimension=0, tiled=True), "rows")
    bias_qkv = jnp.sum(gu, axis=0, dtype=F32)
    packed = jnp.concatenate([gain1, shift1, bias_qkv, bias_out[0], gain2[0], shift2[0], bias_up[0], true_counts.astype(F32)])
    packed = lax.psum(packed, ("dp", "rows"))
    factor = 1.0 / packed[-1]
    cuts = np.cumsum([width, width, 3 * width, width, width, width, up_weight.shape[1]])
    vec = [part * factor for part in jnp.split(packed, cuts)[:-1]]
    mlp_rows = mlp_rows.astype(F32) * factor
    attn_rows = attn_rows.astype(F32) * factor
    ff = up_weight.shape[1]
    return (out, input_grad, vec[0], vec[1], attn_rows[:, : 3 * width], vec[2], attn_rows[:, 3 * width :], vec[3], vec[4], vec[5],
            mlp_rows[:, :ff], vec[6], mlp_rows[:, ff:].T, vec[3])


def solution(mesh):
    both = ("dp", "rows")
    placed = (P(both, None), P(both), P(both), P(both), P(both, None)) + (P(),) * 12
    return jax.shard_map(
        shards, mesh=mesh, in_specs=placed,
        out_specs=(P(both, None), P(both, None), P(), P(), P("dp", None), P(), P("dp", None), P(), P(), P(), P("dp", None), P(),
                   P(None, "dp"), P()),
        check_vma=False)
```

time: 802 us -> 462 us (0.58); the launches traced: 793 us -> 461 us
  matrix products: 277 us -> 36.3 us
  other arithmetic: 130 us -> 19.4 us
  Pallas kernels: 0 us -> 88.6 us
  blocking collectives: 88.6 us -> 44.5 us
  local copies, waits for them, and re-layouts: 36 us -> 23.4 us
  waiting for transfers between devices: 245 us -> 233 us
    dot_general x24 -> x6, matrix products: 277 us -> 36.3 us  [the longest x4 22.6 us: tn(): lax.dot_general(a, b, (((0,), (0,)), ((), ())), preferred_element_type=F32)]
    reduce_scatter x2, waiting for transfers between devices: 179 us -> 56.8 us  [the longest x1 56.8 us: shards(): lax.psum_scatter(mlp_part, 'dp', scatter_dimension=0, tiled=True)]
    pallas_call x0 -> x2, Pallas kernels: none -> 88.6 us  [the longest x1 48.3 us: front(): pl.pallas_call(functools.partial(front_body, tile=tile), grid=(length //...]
    psum x0 -> x1, waiting for transfers between devices: none -> 69.8 us  [shards(): lax.psum(lax.psum_scatter(attn_part, 'dp', scatter_dimension=0, tiled=Tru...]
    convert_element_type x5 -> x1, other arithmetic: 48 us -> 3.76 us  [shards(): input_grad = (gl.astype(F32) + dx).astype(BF16)]
    psum x2 -> x1, blocking collectives: 88.6 us -> 44.5 us  [shards(): packed = lax.psum(packed, ('dp', 'rows'))]
    all_gather x1, waiting for transfers between devices: 64.7 us -> 106 us  [shards(): piece = lax.all_gather(tokens, 'rows', axis=0, tiled=True)]
    reduce_sum x7 -> x4, other arithmetic: 40 us -> 4.92 us  [the longest x1 2.74 us: shards(): centred = x - jnp.mean(x, axis=1, keepdims=True)]
  transfers between devices with their start and end apart: 4 -> 4, of which waited for: 3 -> 3; matrix products, arithmetic and copies ran while one was open for 7% -> 12% of each run, Pallas kernels for 0% -> 0%
where the time goes in v1:
time: 462 us; the launch traced here: 461 us
  waiting for transfers between devices  233 us (50%)
  Pallas kernels  88.6 us (19%)
  blocking collectives  44.5 us (10%)
  matrix products  36.3 us (8%)
  local copies, waits for them, and re-layouts  23.4 us (5%)
  other arithmetic  19.4 us (4%)
  between operations  16.1 us (3%)
    all_gather x1, waiting for transfers between devices, shards(): piece = lax.all_gather(tokens, 'rows', axis=0, tiled=True)  106 us
    psum x1, waiting for transfers between devices, shards(): lax.psum(lax.psum_scatter(attn_part, 'dp', scatter_dimension=0, tiled=Tru...  69.8 us
    reduce_scatter x1, waiting for transfers between devices, shards(): lax.psum_scatter(mlp_part, 'dp', scatter_dimension=0, tiled=True)  56.8 us
    pallas_call x1, Pallas kernels, front(): pl.pallas_call(functools.partial(front_body, tile=tile), grid=(length //...  48.3 us
    psum x1, blocking collectives, shards(): packed = lax.psum(packed, ('dp', 'rows'))  44.5 us
    pallas_call x1, Pallas kernels, attention(): pl.pallas_call(functools.partial(attention_body, rows=rows), grid_spec=pl...  40.3 us
    dot_general x4, matrix products, tn(): lax.dot_general(a, b, (((0,), (0,)), ((), ())), preferred_element_type=F32)  22.6 us
    dot_general x1, matrix products, nt(): lax.dot_general(a, b, (((1,), (1,)), ((), ())), preferred_element_type=F32)  11.2 us
  transfers between devices with their start and end apart: 4, of which 3 were waited for; matrix products, arithmetic and copies ran while one was open for 12% of the time, Pallas kernels for 0%

profile of v1, /device:TPU:0, one launch (start us, length us, event | category | flops | bytes accessed | tf_op | source)
XLA Modules:
  0.0 461.4 jit_solution(4514374321124952708)
XLA Ops:
  7.2 0.0 all-gather.2.cloned.1.call-start
  7.2 0.7 all-gather.2.cloned.1.call-update
  7.9 0.0 reduce-scatter.3.cloned.1.call-start
  9.3 0.8 slice.18
  10.0 1.3 reshape.82.b1_ref
  11.3 1.3 reshape.84.bout_ref
  12.6 1.3 reshape.85.g2_ref
  13.8 1.3 reshape.86.b2_ref
  15.1 1.3 reshape.88.bdown_ref
  16.4 1.3 reshape.81.g1_ref
  17.6 1.3 reshape.83.bqkv_ref
  19.0 1.7 copy.36.segc_ref
  20.7 0.9 convert_reduce_fusion.2
  21.5 0.6 and_select_fusion.first_ref
  22.1 105.6 %all-gather.2.cloned.1.call-done = bf16[4096,768]{1,0:T(8,128)(2,1)} async-done(((bf16[1024,768]{1,0:T(8,128)(2,1)}), bf16[4096,768]{1,0:T(8,128)(2,1)}) %all-gather.2.cloned.1.call-update) | async-done | bytes 6291472 | tf_op jit(solution)/shard_map/all_gather | solution.py:245
  127.7 2.7 convert_reduce_fusion.1
  130.4 48.3 %front.1 = (bf16[6,1024,128]{2,1,0:T(8,128)(2,1)}, bf16[6,1024,128]{2,1,0:T(8,128)(2,1)}, bf16[6,1024,128]{2,1,0:T(8,128)(2,1)}, bf16[6,1024,128]{2,1,0:T(8,128)...) custom-call(s32[1]{0:T(128)S(6)} %copy.52.count_ref, ...), custom_call_target="tpu_custom_call" | custom-call | tf_op jit(solution)/shard_map/front/pallas_call | solution.py:142
  178.7 40.3 %attention.1 = (bf16[1024,768]{1,0:T(8,128)(2,1)}, bf16[1024,768]{1,0:T(8,128)(2,1)}, bf16[1024,768]{1,0:T(8,128)(2,1)}, bf16[1024,768]{1,0:T(8,128)(2,1)}) custom-call(s32[4]{0:T(128)} %and_select_fusion.first_ref, bf16[6,1024,128]{2,1,0:T(8,128)(2,1)} %get-tuple-element.34.q_ref, bf16[6,1024,128]{2,1,0:T(8,128)(2,1)} %get-tuple-element.35.k_ref, ...), custom_call_target="tpu_custom_call" | custom-call | tf_op jit(solution)/shard_map/attention/pallas_call | solution.py:226
  219.0 0.0 copy-start.4
  219.0 0.0 copy-start.14
  219.0 1.7 constant_dynamic-update-slice_fusion.2
  220.7 0.2 copy-done.4
  220.9 0.5 copy-done.14
  221.4 1.5 convolution_convert_fusion.3
  222.9 0.1 constant_dynamic-update-slice_fusion.1
  223.0 1.3 copy-done.2
  224.2 0.1 constant_dynamic-update-slice_fusion
  224.4 2.1 copy-done.1
  226.5 0.0 copy-done.17
  226.5 4.1 convolution_convert_fusion.2
  230.6 2.8 pad_maximum_fusion.1
  233.4 0.0 reduce-scatter.3.cloned.1.call-update
  233.4 0.0 reduce-scatter.5.cloned.1.call-start
  233.5 8.5 %convolution_convert_fusion = bf16[768,3072]{1,0:T(8,128)(2,1)S(1)} fusion(bf16[1024,768]{1,0:T(8,128)(2,1)S(1)} %copy-done.4, bf16[1024,3072]{1,0:T(8,128)(2,1)} %get-tuple-element.51), kind=kOutput, calls=%fused_computation.2 | convolution fusion | flops 4834197504 | bytes 12582912 | tf_op jit(solution)/shard_map/dot_general | solution.py:28
  242.0 8.5 %convolution_convert_fusion.1 = bf16[768,3072]{1,0:T(8,128)(2,1)S(1)} fusion(bf16[1024,768]{1,0:T(8,128)(2,1)S(1)} %copy-done.16, bf16[1024,3072]{1,0:T(8,128)(2,1)} %get-tuple-element.50), kind=kOutput, calls=%fused_computation.3 | convolution fusion | flops 4834197504 | bytes 12582912 | tf_op jit(solution)/shard_map/dot_general | solution.py:28
  250.5 4.0 pad_maximum_fusion
  254.6 0.0 copy-start.9
  254.6 0.0 reduce-scatter.5.cloned.1.call-update
  254.6 0.0 all-reduce.3.cloned.1.call-start
  254.7 0.6 copy-done.12
  255.3 0.7 copy-done
  256.0 0.6 fusion.11
  256.6 0.0 slice-start
  256.6 0.0 slice-start.1
  256.7 11.2 %fusion.12 = (f32[768]{0:T(1024)S(1)}, f32[768]{0:T(1024)S(1)}, f32[1024]{0:T(1024)S(1)}, f32[1024]{0:T(1024)S(1)}, f32[1024,768]{1,0:T(8,128)}) fusion(f32[1024]{0:T(1024)S(1)} %add_rsqrt_fusion, f32[1024]{0:T(1024)S(1)} %broadcast_multiply_fusion.2, bf16[1024,768]{1,0:T(8,128)(2,1)S(1)} %copy-done, f32[1024,768]{1,0:T(8,128)} %get-tuple-element.43, ...), kind=kOutput, calls=%fused_computation.54 | convolution fusion | flops 3632525824 | bytes 16147456 | tf_op jit(solution)/shard_map/dot_general | solution.py:24
  267.9 0.7 convert_reduce_fusion
  268.6 44.5 %psum.21 = f32[9217]{0:T(1024)S(1)} all-reduce(f32[9217]{0:T(1024)S(1)} %constant_dynamic-update-slice_fusion.6), channel_id=1, replica_groups=mesh['dp'=8,'rows'=4] {'dp','rows'}, use_global_device_ids=true, to_apply=%region_8.9 | all-reduce | flops 9217 | bytes 73736 | tf_op jit(solution)/shard_map/psum | solution.py:270
  313.1 0.5 slice.24
  314.3 0.0 reduce-scatter.3.cloned.1.call-done
  314.4 56.8 %reduce-scatter.5.cloned.1.call-done = bf16[96,6144]{1,0:T(8,128)(2,1)} async-done(((bf16[768,6144]{1,0:T(8,128)(2,1)}), bf16[96,6144]{1,0:T(8,128)(2,1)}) %reduce-scatter.5.cloned.1.call-update) | async-done | bytes 1179664 | tf_op jit(solution)/shard_map/reduce_scatter | solution.py:252
  371.1 0.0 all-reduce.3.cloned.1.call-update
  371.2 0.6 slice_multiply_fusion.2
  371.8 0.6 slice_multiply_fusion
  372.4 0.6 slice_multiply_fusion.1
  373.0 3.8 fusion.9
  376.8 0.4 copy-done.15
  377.2 2.6 add_convert_fusion
  379.7 69.8 %all-reduce.3.cloned.1.call-done = (bf16[96,3072]{1,0:T(8,128)(2,1)}, bf16[96,6144]{1,0:T(8,128)(2,1)}) async-done(((bf16[96,3072]{1,0:T(8,128)(2,1)}, bf16[96,6144]{1,0:T(8,128)(2,1)}), (bf16[96,3072]{1,0:T(8,128)(2,1)}, bf16[96,6144]{1,0:T(8,128)(2,1)})) %all-reduce.3.cloned.1.call-update) | async-done | bytes 1769488 | tf_op jit(solution)/shard_map/psum | solution.py:267
  449.5 1.3 convert_multiply_fusion.1
  450.8 0.7 slice.26
  451.5 1.0 slice.25
  452.5 0.2 convert_multiply_fusion
  452.7 1.6 slice_bitcast_fusion
  454.2 0.6 copy.54
  (43 shorter events, 0.2 us)
Async XLA Ops:
  7.2 120.5 %all-gather.2.cloned.1.call-start = ((), (), s32[]{:S(2)}) async-start(), calls=%async_computation.2 | async-start | bytes 7864320 | tf_op jit(solution)/shard_map/all_gather | solution.py:245
  7.9 306.4 %reduce-scatter.3.cloned.1.call-start = ((), (), s32[]{:S(2)}) async-start(), calls=%async_computation.3 | async-start | bytes 5308416 | tf_op jit(solution)/shard_map/reduce_scatter | solution.py:267
  219.0 1.9 copy-start.4
  219.0 2.3 copy-start.14
  221.4 1.5 copy-start.3
  222.8 1.4 copy-start.2
  222.9 3.6 copy-start.17
  224.4 2.1 copy-start.1
  233.4 137.7 %reduce-scatter.5.cloned.1.call-start = ((), (), s32[]{:S(2)}) async-start(), calls=%async_computation.4 | async-start | bytes 10616832 | tf_op jit(solution)/shard_map/reduce_scatter | solution.py:252
  233.5 8.5 %copy-start.16 = (bf16[1024,768]{1,0:T(8,128)(2,1)S(1)}, bf16[1024,768]{1,0:T(8,128)(2,1)}, u32[]{:S(2)}) copy-start(bf16[1024,768]{1,0:T(8,128)(2,1)} %get-tuple-element.49) | copy-start | bytes 4718596
  254.5 0.7 copy-start.12
  254.6 0.7 copy-start.11
  254.6 0.7 copy-start.10
  254.6 1.4 copy-start
  254.6 2.1 copy-start.9
  254.6 194.9 %all-reduce.3.cloned.1.call-start = ((), (), s32[]{:S(2)}) async-start(), calls=%async_computation.5 | async-start | bytes 3538944 | tf_op jit(solution)/shard_map/psum | solution.py:267
  256.6 11.2 %slice-start = ((s8[4718592]{0:T(1024)(128)(4,1)}), s8[4194304]{0:T(1024)(128)(4,1)S(1)}, s32[]{:S(2)}) async-start(s8[4718592]{0:T(1024)(128)(4,1)} %bitcast.23), calls=%async_computation.6 | async-start | bytes 8388608
  256.6 11.2 %slice-start.1 = ((s8[4718592]{0:T(1024)(128)(4,1)}), s8[524288]{0:T(1024)(128)(4,1)S(1)}, s32[]{:S(2)}) async-start(s8[4718592]{0:T(1024)(128)(4,1)} %bitcast.23), calls=%async_computation.7 | async-start | bytes 1048576
  267.8 0.8 copy-start.8
  371.8 82.5 %copy-start.7 = (f32[768]{0:T(1024)}, f32[768]{0:T(1024)S(1)}, u32[]{:S(2)}) copy-start(f32[768]{0:T(1024)S(1)} %get-tuple-element.100) | copy-start | bytes 9220
  373.0 3.8 copy-start.5
  373.0 3.8 copy-start.13
  373.0 4.2 copy-start.15
  449.5 3.0 copy-start.6
Sparse Core Ops, SparseCore 0:
  9.6 118.0 all-gather.1
  233.5 57.1 reduce-scatter.2
  294.6 76.4 reduce-scatter.4
  373.6 75.8 all-reduce.2

commit v2 on v1

--- a/solution.py
+++ b/solution.py
@@ -59,7 +59,7 @@
 
 def front_body(count_ref, x_ref, cot_ref, cos_ref, sin_ref, g1_ref, b1_ref, wqkv_ref, bqkv_ref, wout_ref, bout_ref,
                g2_ref, b2_ref, wup_ref, bup_ref, wdown_ref, bdown_ref,
-               q_ref, k_ref, v_ref, gc_ref, n1_ref, n2_ref, gl_ref, act_ref, gh_ref, base_ref, t2_ref,
+               q_ref, k_ref, v_ref, gc_ref, n1t_ref, n2t_ref, glt_ref, gl_ref, act_ref, gh_ref, base_ref, t2_ref,
                gain2_ref, shift2_ref, bup_out, bout_out, *, tile):
     step = pl.program_id(0)
     rows, width = x_ref.shape
@@ -71,12 +71,13 @@
     n = centred * r
     n1 = (n * g1_ref[...] + b1_ref[...]).astype(BF16)
     n2 = (n * g2_ref[...] + b2_ref[...]).astype(BF16)
-    n1_ref[...] = n1
-    n2_ref[...] = n2
+    n1t_ref[...] = n1.T
+    n2t_ref[...] = n2.T
     place = step * rows + lax.broadcasted_iota(jnp.int32, (rows, 1), 0)
     gl = jnp.where(place < count_ref[0], cot_ref[...].astype(F32), 0.0)
     gl16 = gl.astype(BF16)
     gl_ref[...] = gl16
+    glt_ref[...] = gl16.T
 
     @pl.when(step == 0)
     def _():
@@ -144,8 +145,8 @@
         grid=(length // rows,),
         in_specs=[pl.BlockSpec(memory_space=pltpu.SMEM), row(width), row(width), row(PAIR), row(PAIR)]
         + [whole(a) for a in (g1, b1, wqkv, bqkv, wout, bout, g2, b2, wup, bup, wdown, bdown)],
-        out_specs=[heads] * 4 + [row(width)] * 3 + [row(ff)] * 2 + [row(width)] * 2 + [vec(width), vec(width), vec(ff), vec(width)],
-        out_shape=[s((pairs, length, PAIR), BF16)] * 4 + [s((length, width), BF16)] * 3 + [s((length, ff), BF16)] * 2
+        out_specs=[heads] * 4 + [pl.BlockSpec((width, rows), lambda i: (0, i))] * 3 + [row(width)] + [row(ff)] * 2 + [row(width)] * 2 + [vec(width), vec(width), vec(ff), vec(width)],
+        out_shape=[s((pairs, length, PAIR), BF16)] * 4 + [s((width, length), BF16)] * 3 + [s((length, width), BF16)] + [s((length, ff), BF16)] * 2
         + [s((length, width), F32)] * 2 + [s((1, width), F32), s((1, width), F32), s((1, ff), F32), s((1, width), F32)],
         compiler_params=pltpu.CompilerParams(vmem_limit_bytes=56 * 2**20),
         name="front",
@@ -153,7 +154,7 @@
 
 
 def attention_body(first_ref, q_ref, k_ref, v_ref, gc_ref, segc_ref, segr_ref, cos_ref, sin_ref,
-                   ctx_ref, gq_ref, gk_ref, gv_ref, dk_acc, dv_acc, *, rows):
+                   ctx_ref, ctxt_ref, gu_ref, dk_acc, dv_acc, *, rows):
     length = q_ref.shape[1]
     lane = lax.broadcasted_iota(jnp.int32, (rows, PAIR), 1)
     low = lane < HEAD_DIM
@@ -183,7 +184,9 @@
         p = e * (1.0 / jnp.sum(e, axis=1, keepdims=True))
         p16 = p.astype(BF16)
         c2 = nn(p16, v)
-        ctx_ref[pl.ds(begin, rows), :] = jnp.where(low, c2[:rows], c2[rows:]).astype(BF16)
+        context = jnp.where(low, c2[:rows], c2[rows:]).astype(BF16)
+        ctx_ref[pl.ds(begin, rows), :] = context
+        ctxt_ref[:, pl.ds(begin, rows)] = context.T
         dp = nt(g2, v)
         inner = jnp.sum(p * dp, axis=1, keepdims=True)
         ds16 = (p * (dp - inner)).astype(BF16)
@@ -191,7 +194,7 @@
         dq = jnp.where(low, d2[:rows], d2[rows:]) * (HEAD_DIM ** -0.5)
         cosine = cos_ref[pl.ds(begin, rows), :]
         sine = sin_ref[pl.ds(begin, rows), :]
-        gq_ref[pl.ds(begin, rows), :] = (dq * cosine - turned(dq) * sine).astype(BF16)
+        gu_ref[0, pl.ds(begin, rows), :] = (dq * cosine - turned(dq) * sine).astype(BF16)
         dk_acc[pl.ds(start, span), :] += tn(ds16, q2)
         dv_acc[pl.ds(start, span), :] += tn(p16, g2)
 
@@ -207,8 +210,8 @@
 
     lax.fori_loop(0, total, loop, 0)
     dk = dk_acc[...]
-    gk_ref[...] = (dk * cos_ref[...] - turned(dk) * sin_ref[...]).astype(BF16)
-    gv_ref[...] = dv_acc[...].astype(BF16)
+    gu_ref[1] = (dk * cos_ref[...] - turned(dk) * sin_ref[...]).astype(BF16)
+    gu_ref[2] = dv_acc[...].astype(BF16)
 
 
 def attention(q, k, v, gc, segment, cosine, sine, rows=128):
@@ -218,7 +221,8 @@
     first = begins // rows
     head = pl.BlockSpec((1, length, PAIR), lambda h, *_: (h, 0, 0))
     cols = pl.BlockSpec((length, PAIR), lambda h, *_: (0, h))
-    s = jax.ShapeDtypeStruct((length, pairs * PAIR), BF16)
+    s = jax.ShapeDtypeStruct
+    width = pairs * PAIR
 
     def whole(shape):
         return pl.BlockSpec(shape, lambda h, *_: (0, 0), pipeline_mode=pl.Buffered(1))
@@ -229,53 +233,409 @@
             num_scalar_prefetch=1,
             grid=(pairs,),
             in_specs=[head] * 4 + [whole((length, 1)), whole((1, length)), whole((length, PAIR)), whole((length, PAIR))],
-            out_specs=[cols] * 4,
+            out_specs=[cols, pl.BlockSpec((PAIR, length), lambda h, *_: (h, 0)), pl.BlockSpec((3, length, PAIR), lambda h, *_: (0, 0, h))],
             scratch_shapes=[pltpu.VMEM((length, PAIR), F32)] * 2,
         ),
-        out_shape=[s] * 4,
+        out_shape=[s((length, width), BF16), s((width, length), BF16), s((3, length, width), BF16)],
         compiler_params=pltpu.CompilerParams(vmem_limit_bytes=56 * 2**20),
         name="attention",
     )(first, q, k, v, gc, segment.reshape(-1, 1), segment.reshape(1, -1), cosine, sine)
 
 
+MESH = pl.DeviceIdType.MESH
+CHUNK = 384
+
+
+class Line:
+    def __init__(self):
+        self.d = lax.axis_index("dp")
+        self.z = lax.axis_index("rows")
+        self.core = self.d % 2
+        self.x = (self.d // 2) % 2
+        self.y = self.d // 4
+        self.over_core = (self.d + 1 - 2 * self.core, self.z)
+        self.over_x = (self.d + 2 - 4 * self.x, self.z)
+        self.over_y = (self.d + 4 - 8 * self.y, self.z)
+        self.inner = (self.z + 1) // 2 % 2
+        self.near = (self.d, self.z + 1 - 2 * (self.z % 2))
+        self.far = (self.d, 3 - self.z)
+
+
+def remote(src, dst, send, recv, to):
+    return pltpu.make_async_remote_copy(src_ref=src, dst_ref=dst, send_sem=send, recv_sem=recv, device_id=to, device_id_type=MESH)
+
+
+class Everywhere:
+    HOPS = 7
+
+    def __init__(self, at, held, come, send, recv):
+        self.at, self.held, self.come, self.send, self.recv = at, held, come, send, recv
+
+    def copy(self, hop, to):
+        return remote(self.held.at[hop], self.come.at[hop], self.send.at[hop], self.recv.at[hop], to)
+
+    def take(self, hop, to):
+        self.copy(hop, to).wait()
+        self.held[hop + 1] = self.held[hop] + self.come[hop]
+
+    def hop(self, tick):
+        at = self.at
+        over = (at.over_core, at.over_x, at.over_y)
+
+        @pl.when(tick == 0)
+        def _():
+            self.copy(0, over[0]).start()
+
+        for j in (1, 2):
+            @pl.when(tick == j)
+            def _():
+                self.take(j - 1, over[j - 1])
+                self.copy(j, over[j]).start()
+
+        @pl.when(tick == 3)
+        def _():
+            self.take(2, over[2])
+
+            @pl.when(at.inner == 0)
+            def _():
+                self.copy(3, at.near).start()
+
+        @pl.when((tick == 4) & (at.inner == 1))
+        def _():
+            self.copy(3, at.near).wait_recv()
+            self.held[4] = self.held[3] + self.come[3]
+            self.copy(4, at.far).start()
+
+        @pl.when((tick == 4) & (at.inner == 0))
+        def _():
+            self.copy(3, at.near).wait_send()
+
+        @pl.when((tick == 5) & (at.inner == 1))
+        def _():
+            self.take(4, at.far)
+            self.copy(5, at.near).start()
+
+        @pl.when(tick == 6)
+        def _():
+            @pl.when(at.inner == 1)
+            def _():
+                self.copy(5, at.near).wait_send()
+
+            @pl.when(at.inner == 0)
+            def _():
+                self.copy(5, at.near).wait_recv()
+                self.held[5] = self.come[5]
+
+
+LAGS = dict(core=1, first=3, second=5, z=6, mid=8, back=9)
+
+
+def reduce_body(count_ref, n1t_ref, n2t_ref, glt_ref, ctxt_ref, gh_ref, act_ref, glc_ref, guc_ref,
+                x_ref, gl_ref, base_ref, t2_ref, ctx_ref, gu_ref, wqkv_ref, wout_ref, g1_ref,
+                gain2_ref, shift2_ref, bup_ref, bout_ref,
+                out_ref, ig_ref, grads_ref, vec_ref,
+                part, from_core, from_first, from_second, zsum, from_near, from_far,
+                c_send, c_recv, f_send, f_recv, s_send, s_recv, n_send, n_recv, m_send, m_recv,
+                held_n, come_n, held_v, come_v, n_s, n_r, v_s, v_r, gain1, shift1, bqkv, *, cuts, row_ticks):
+    tick = pl.program_id(0)
+    at = Line()
+    chunks = cuts[-1]
+    ring = part.shape[0]
+    width = wout_ref.shape[0]
+    block = width // 8
+
+    @pl.when(tick == 0)
+    def _():
+        barrier = pltpu.get_barrier_semaphore()
+        for to in (at.over_core, at.over_x, at.over_y, at.near):
+            pl.semaphore_signal(barrier, inc=1, device_id=to, device_id_type=MESH)
+
+        @pl.when(at.inner == 1)
+        def _():
+            pl.semaphore_signal(barrier, inc=1, device_id=at.far, device_id_type=MESH)
+            pl.semaphore_wait(barrier, 5)
+
+        @pl.when(at.inner == 0)
+        def _():
+            pl.semaphore_wait(barrier, 4)
+
+        held_n[0] = jnp.full(held_n.shape[1:], count_ref[0].astype(F32), F32)
+
+    def places(i):
+        even = 1 - i % 2
+        f = at.x * even + at.y * (1 - even)
+        s = at.y * even + at.x * (1 - even)
+        first = (at.d + even * (2 - 4 * at.x) + (1 - even) * (4 - 8 * at.y), at.z)
+        second = (at.d + even * (4 - 8 * at.y) + (1 - even) * (2 - 4 * at.x), at.z)
+        return even, f, s, first, second, i % ring
+
+    def core_copy(i):
+        slot = i % ring
+        return remote(part.at[slot, 1 - at.core], from_core.at[i], c_send.at[i], c_recv.at[i], at.over_core)
+
+    def first_copy(i):
+        even, f, s, first, second, slot = places(i)
+        return remote(part.at[slot, at.core, 1 - f], from_first.at[i], f_send.at[i], f_recv.at[i], first)
+
+    def second_copy(i):
+        even, f, s, first, second, slot = places(i)
+        return remote(part.at[slot, at.core, f, 1 - s], from_second.at[i], s_send.at[i], s_recv.at[i], second)
+
+    def out_copy(i):
+        return remote(zsum.at[i], from_near.at[i], n_send.at[i], n_recv.at[i], at.near)
+
+    def far_copy(i):
+        return remote(zsum.at[i], from_far.at[i], m_send.at[i], m_recv.at[i], at.far)
+
+    def back_copy(i):
+        return remote(from_far.at[i], from_near.at[i], n_send.at[i], n_recv.at[i], at.near)
+
+    def plus(a, b):
+        return (a.astype(F32) + b.astype(F32)).astype(BF16)
+
+    def product(left, right):
+        even = 1 - tick % 2
+        slot = tick % ring
+        half = width // 2
+        for h in range(2):
+            rows = nn(left[h * half : (h + 1) * half, :], right)
+            for j in range(4):
+                d = h * 4 + j
+                c, x, y = d % 2, (d // 2) % 2, d // 4
+                a = x * even + y * (1 - even)
+                b = y * even + x * (1 - even)
+                part[slot, c, a, b] = rows[j * block : (j + 1) * block].astype(BF16)
+        core_copy(tick).start()
+
+    starts = (0,) + cuts[:-1]
+    operands = ((n2t_ref, gh_ref), (glt_ref, act_ref), (ctxt_ref, glc_ref), (n1t_ref, guc_ref))
+    for (left, right), lo, hi in zip(operands, starts, cuts):
+        @pl.when((tick >= lo) & (tick < hi))
+        def _():
+            product(left[...], right[0] if right is guc_ref else right[...])
+
+    def when(lag, f):
+        i = tick - lag
+
+        @pl.when((i >= 0) & (i < chunks))
+        def _():
+            f(i)
+
+    def core_step(i):
+        even, f, s, first, second, slot = places(i)
+        core_copy(i).wait()
+        for a in range(2):
+            for b in range(2):
+                part[slot, at.core, a, b] = plus(part[slot, at.core, a, b], from_core[i, a, b])
+        first_copy(i).start()
+
+    def first_step(i):
+        even, f, s, first, second, slot = places(i)
+        first_copy(i).wait()
+        for b in range(2):
+            part[slot, at.core, f, b] = plus(part[slot, at.core, f, b], from_first[i, b])
+        second_copy(i).start()
+
+    def second_step(i):
+        even, f, s, first, second, slot = places(i)
+        second_copy(i).wait()
+        zsum[i] = plus(part[slot, at.core, f, s], from_second[i])
+
+        @pl.when(at.inner == 0)
+        def _():
+            out_copy(i).start()
+
+    def near_step(i):
+        @pl.when(at.inner == 1)
+        def _():
+            out_copy(i).wait_recv()
+            zsum[i] = plus(zsum[i], from_near[i])
+            far_copy(i).start()
+
+    def far_step(i):
+        @pl.when(at.inner == 1)
+        def _():
+            far_copy(i).wait()
+            total = plus(zsum[i], from_far[i])
+            from_far[i] = total
+            back_copy(i).start()
+            grads_ref[i] = total.astype(F32) / held_n[5, 0:1, 0:1]
+
+        @pl.when(at.inner == 0)
+        def _():
+            out_copy(i).wait_send()
+
+    def back_step(i):
+        @pl.when(at.inner == 0)
+        def _():
+            back_copy(i).wait_recv()
+            grads_ref[i] = from_near[i].astype(F32) / held_n[5, 0:1, 0:1]
+
+        @pl.when(at.inner == 1)
+        def _():
+            back_copy(i).wait_send()
+
+    when(LAGS["core"], core_step)
+
+    @pl.when(tick == 0)
+    def _():
+        gain1[...] = jnp.zeros_like(gain1)
+        shift1[...] = jnp.zeros_like(shift1)
+        bqkv[...] = jnp.zeros_like(bqkv)
+
+    @pl.when(tick < row_ticks)
+    def _():
+        out_ref[...] = (base_ref[...] + nn(ctx_ref[...], wout_ref[...])).astype(BF16)
+        g1 = nt(gu_ref[0], wqkv_ref[:, :width])
+        g1 = g1 + nt(gu_ref[1], wqkv_ref[:, width : 2 * width])
+        g1 = g1 + nt(gu_ref[2], wqkv_ref[:, 2 * width :])
+        x = x_ref[...].astype(F32)
+        centred = x - jnp.mean(x, axis=1, keepdims=True)
+        r = lax.rsqrt(jnp.mean(centred * centred, axis=1, keepdims=True) + EPSILON)
+        n = centred * r
+        gain1[...] += jnp.sum(g1 * n, axis=0, keepdims=True)
+        shift1[...] += jnp.sum(g1, axis=0, keepdims=True)
+        for j in range(3):
+            bqkv[:, j * width : (j + 1) * width] += jnp.sum(gu_ref[j].astype(F32), axis=0, keepdims=True)
+        t = g1 * g1_ref[...] + t2_ref[...]
+        dx = r * (t - jnp.mean(t, axis=1, keepdims=True) - n * jnp.mean(t * n, axis=1, keepdims=True))
+        ig_ref[...] = (gl_ref[...].astype(F32) + dx).astype(BF16)
+
+    when(LAGS["first"], first_step)
+    when(LAGS["second"], second_step)
+    when(LAGS["z"], near_step)
+    when(LAGS["mid"], far_step)
+    when(LAGS["back"], back_step)
+
+    Everywhere(at, held_n, come_n, n_s, n_r).hop(tick)
+
+    @pl.when(tick == row_ticks)
+    def _():
+        held_v[0] = jnp.zeros(held_v.shape[1:], F32)
+        held_v[0, 0:1, :] = bup_ref[...]
+        held_v[0, 1:2, : 3 * width] = bqkv[...]
+        held_v[0, 1:2, 3 * width :] = bout_ref[...]
+        held_v[0, 2:3, :width] = gain1[...]
+        held_v[0, 2:3, width : 2 * width] = shift1[...]
+        held_v[0, 2:3, 2 * width : 3 * width] = gain2_ref[...]
+        held_v[0, 2:3, 3 * width :] = shift2_ref[...]
+
+    Everywhere(at, held_v, come_v, v_s, v_r).hop(tick - row_ticks)
+
+    @pl.when(tick == row_ticks + 6)
+    def _():
+        vec_ref[...] = held_v[5] / held_n[5, 0:1, 0:1]
+
+
+def reduce(count, n1t, n2t, glt, ctxt, gh, act, gl, gu, x, base, t2, ctx, wqkv, wout, g1, gain2, shift2, bup, bout):
+    length, width = x.shape
+    ff = gh.shape[1]
+    block = width // 8
+    counts = (ff // CHUNK, ff // CHUNK, width // CHUNK, 3 * width // CHUNK)
+    cuts = tuple(int(c) for c in np.cumsum(counts))
+    chunks = cuts[-1]
+    per = width // CHUNK
+    rows = 128
+    row_ticks = length // rows
+    ticks = chunks + LAGS["back"]
+    ring = 8
+
+    def cols(array_chunks, begin):
+        return pl.BlockSpec((length, CHUNK), lambda t: (0, jnp.clip(t - begin, 0, array_chunks - 1)))
+
+    def row(cols):
+        return pl.BlockSpec((rows, cols), lambda t: (jnp.minimum(t, row_ticks - 1), 0))
+
+    def whole(a):
+        return pl.BlockSpec(a.shape, lambda t: (0,) * a.ndim, pipeline_mode=pl.Buffered(1))
+
+    def gu_cols(t):
+        j = jnp.clip(t - cuts[2], 0, counts[3] - 1)
+        return (j // per, 0, j % per)
+
+    g1 = g1.reshape(1, -1)
+    s = jax.ShapeDtypeStruct
+    dma = pltpu.SemaphoreType.DMA
+    hops = Everywhere.HOPS
+    return pl.pallas_call(
+        functools.partial(reduce_body, cuts=cuts, row_ticks=row_ticks),
+        grid=(ticks,),
+        in_specs=[pl.BlockSpec(memory_space=pltpu.SMEM), whole(n1t), whole(n2t), whole(glt), whole(ctxt),
+                  cols(counts[0], 0), cols(counts[1], cuts[0]), cols(counts[2], cuts[1]),
+                  pl.BlockSpec((1, length, CHUNK), gu_cols),
+                  row(width), row(width), row(width), row(width), row(width),
+                  pl.BlockSpec((3, rows, width), lambda t: (0, jnp.minimum(t, row_ticks - 1), 0)),
+                  whole(wqkv), whole(wout), whole(g1), whole(gain2), whole(shift2), whole(bup), whole(bout)],
+        out_specs=[row(width), row(width),
+                   pl.BlockSpec((chunks, block, CHUNK), lambda t: (0, 0, 0), pipeline_mode=pl.Buffered(1)),
+                   pl.BlockSpec((8, ff), lambda t: (0, 0), pipeline_mode=pl.Buffered(1))],
+        out_shape=[s((length, width), BF16), s((length, width), BF16), s((chunks, block, CHUNK), F32), s((8, ff), F32)],
+        scratch_shapes=[
+            pltpu.VMEM((ring, 2, 2, 2, block, CHUNK), BF16),
+            pltpu.VMEM((chunks, 2, 2, block, CHUNK), BF16),
+            pltpu.VMEM((chunks, 2, block, CHUNK), BF16),
+            pltpu.VMEM((chunks, block, CHUNK), BF16),
+            pltpu.VMEM((chunks, block, CHUNK), BF16),
+            pltpu.VMEM((chunks, block, CHUNK), BF16),
+            pltpu.VMEM((chunks, block, CHUNK), BF16),
+        ] + [dma((chunks,))] * 10 + [
+            pltpu.VMEM((hops, 8, 128), F32), pltpu.VMEM((hops, 8, 128), F32),
+            pltpu.VMEM((hops, 8, ff), F32), pltpu.VMEM((hops, 8, ff), F32),
+            dma((hops,)), dma((hops,)), dma((hops,)), dma((hops,)),
+            pltpu.VMEM((1, width), F32), pltpu.VMEM((1, width), F32), pltpu.VMEM((1, 3 * width), F32),
+        ],
+        compiler_params=pltpu.CompilerParams(vmem_limit_bytes=60 * 2**20, collective_id=0, has_side_effects=True),
+        name="reduce",
+    )(count, n1t, n2t, glt, ctxt, gh, act, gl, gu, x, gl, base, t2, ctx, gu, wqkv, wout, g1, gain2, shift2, bup, bout)
+
+
+def by_collectives(count, n1t, n2t, glt, ctxt, gh, act, gl, gu, x, base, t2, ctx, wqkv, wout, g1, gain2, shift2, bup, bout):
+    width = x.shape[1]
+    flat = jnp.concatenate([gu[0], gu[1], gu[2]], axis=1)
+    out = (base + nn(ctx, wout)).astype(BF16)
+    grad_one = nt(flat, wqkv)
+    x = x.astype(F32)
+    centred = x - jnp.mean(x, axis=1, keepdims=True)
+    r = lax.rsqrt(jnp.mean(centred * centred, axis=1, keepdims=True) + EPSILON)
+    n = centred * r
+    t = grad_one * g1 + t2
+    dx = r * (t - jnp.mean(t, axis=1, keepdims=True) - n * jnp.mean(t * n, axis=1, keepdims=True))
+    input_grad = (gl.astype(F32) + dx).astype(BF16)
+    packed = jnp.concatenate([bup[0], jnp.sum(flat, axis=0, dtype=F32), bout[0], jnp.sum(grad_one * n, axis=0),
+                              jnp.sum(grad_one, axis=0), gain2[0], shift2[0], count.astype(F32)])
+    packed = lax.psum(packed, ("dp", "rows"))
+    part = jnp.concatenate([nn(n2t, gh), nn(glt, act), nn(ctxt, gl), nn(n1t, flat)], axis=1).astype(BF16)
+    grads = lax.psum(lax.psum_scatter(part, "dp", scatter_dimension=0, tiled=True), "rows")
+    return out, input_grad, grads.astype(F32) / packed[-1], (packed[:-1] / packed[-1]).reshape(3, -1)
+
+
+def by_kernel(*operands):
+    out, input_grad, grads, vec = reduce(*operands)
+    grads = jnp.swapaxes(grads, 0, 1).reshape(grads.shape[1], -1)
+    return out, input_grad, grads, vec
+
+
 def shards(tokens, segment_ids, true_counts, regroup, cotangent, ln1_gain, ln1_bias, qkv_weight, qkv_bias, out_weight,
            out_bias, ln2_gain, ln2_bias, up_weight, up_bias, down_weight, down_bias):
     length, width = cotangent.shape
+    ff = up_weight.shape[1]
     source = regroup[0] % lax.axis_size("rows")
     piece = lax.all_gather(tokens, "rows", axis=0, tiled=True)
     arrived = lax.dynamic_slice_in_dim(piece, source * length, length, 0)
     cosine, sine = (jnp.asarray(t) for t in rotary_tables(length))
-    (q, k, v, gc, n1, n2, gl, act, gh, base, t2, gain2, shift2, bias_up, bias_out) = front(
+    (q, k, v, gc, n1t, n2t, glt, gl, act, gh, base, t2, gain2, shift2, bias_up, bias_out) = front(
         true_counts, arrived, cotangent, cosine, sine, ln1_gain, ln1_bias, qkv_weight, qkv_bias, out_weight, out_bias,
         ln2_gain, ln2_bias, up_weight, up_bias, down_weight, down_bias)
-    mlp_part = jnp.concatenate([tn(n2, gh), tn(gl, act)], axis=1).astype(BF16)
-    mlp_rows = lax.psum(lax.psum_scatter(mlp_part, "dp", scatter_dimension=0, tiled=True), "rows")
-    ctx, gq, gk, gv = attention(q, k, v, gc, segment_ids, cosine, sine, rows=256)
-    out = (base + nn(ctx, out_weight)).astype(BF16)
-    gu = jnp.concatenate([gq, gk, gv], axis=1)
-    g1 = nt(gu, qkv_weight)
-    x = arrived.astype(F32)
-    centred = x - jnp.mean(x, axis=1, keepdims=True)
-    r = lax.rsqrt(jnp.mean(centred * centred, axis=1, keepdims=True) + EPSILON)
-    n = centred * r
-    gain1 = jnp.sum(g1 * n, axis=0)
-    shift1 = jnp.sum(g1, axis=0)
-    t = g1 * ln1_gain + t2
-    dx = r * (t - jnp.mean(t, axis=1, keepdims=True) - n * jnp.mean(t * n, axis=1, keepdims=True))
-    input_grad = (gl.astype(F32) + dx).astype(BF16)
-    attn_part = jnp.concatenate([tn(n1, gu), tn(ctx, gl)], axis=1).astype(BF16)
-    attn_rows = lax.psum(lax.psum_scatter(attn_part, "dp", scatter_dimension=0, tiled=True), "rows")
-    bias_qkv = jnp.sum(gu, axis=0, dtype=F32)
-    packed = jnp.concatenate([gain1, shift1, bias_qkv, bias_out[0], gain2[0], shift2[0], bias_up[0], true_counts.astype(F32)])
-    packed = lax.psum(packed, ("dp", "rows"))
-    factor = 1.0 / packed[-1]
-    cuts = np.cumsum([width, width, 3 * width, width, width, width, up_weight.shape[1]])
-    vec = [part * factor for part in jnp.split(packed, cuts)[:-1]]
-    mlp_rows = mlp_rows.astype(F32) * factor
-    attn_rows = attn_rows.astype(F32) * factor
-    ff = up_weight.shape[1]
-    return (out, input_grad, vec[0], vec[1], attn_rows[:, : 3 * width], vec[2], attn_rows[:, 3 * width :], vec[3], vec[4], vec[5],
-            mlp_rows[:, :ff], vec[6], mlp_rows[:, ff:].T, vec[3])
+    ctx, ctxt, gu = attention(q, k, v, gc, segment_ids, cosine, sine, rows=256)
+    last = by_kernel if (lax.axis_size("dp"), lax.axis_size("rows")) == (8, 4) else by_collectives
+    out, input_grad, grads, vec = last(true_counts, n1t, n2t, glt, ctxt, gh, act, gl, gu, arrived, base, t2, ctx, qkv_weight,
+                                       out_weight, ln1_gain, gain2, shift2, bias_up, bias_out)
+    up, down = grads[:, :ff], grads[:, ff : 2 * ff].T
+    low, qkv = grads[:, 2 * ff : 2 * ff + width], grads[:, 2 * ff + width :]
+    gains = vec[2].reshape(4, width)
+    bias_out = vec[1, 3 * width :]
+    return (out, input_grad, gains[0], gains[1], qkv, vec[1, : 3 * width], low, bias_out, gains[2], gains[3], up, vec[0], down,
+            bias_out)
 
 
 def solution(mesh):

time: 462 us -> 354 us (0.77)
  waiting for transfers between devices: 233 us -> 113 us
  Pallas kernels: 88.6 us -> 202 us
  blocking collectives: 44.5 us -> 0 us
  matrix products: 36.3 us -> 0 us
  other arithmetic: 19.4 us -> 0.79 us
    pallas_call x0 -> x1, Pallas kernels: none -> 113 us  [reduce(): pl.pallas_call(functools.partial(reduce_body, cuts=cuts, row_ticks=row_ti...]
    psum x1 -> x0, waiting for transfers between devices: 69.8 us -> none  [shards(): lax.psum(lax.psum_scatter(attn_part, 'dp', scatter_dimension=0, tiled=Tru...]
    reduce_scatter x2 -> x0, waiting for transfers between devices: 56.8 us -> none  [the longest x1 56.8 us: shards(): lax.psum_scatter(mlp_part, 'dp', scatter_dimension=0, tiled=True)]
    psum x1 -> x0, blocking collectives: 44.5 us -> none  [shards(): packed = lax.psum(packed, ('dp', 'rows'))]
    dot_general x6 -> x0, matrix products: 36.3 us -> none  [the longest x4 22.6 us: tn(): lax.dot_general(a, b, (((0,), (0,)), ((), ())), preferred_element_type=F32)]
    all_gather x1, waiting for transfers between devices: 106 us -> 112 us  [shards(): piece = lax.all_gather(tokens, 'rows', axis=0, tiled=True)]
    concatenate x3 -> x0, other arithmetic: 6.84 us -> none  [the longest x1 4.03 us: shards(): mlp_part = jnp.concatenate([tn(n2, gh), tn(gl, act)], axis=1).astype(BF16)]
    reshape x7, local copies, waits for them, and re-layouts: 8.91 us -> 4.09 us  [front(): v.reshape(1, -1)]
  transfers between devices with their start and end apart: 4 -> 1, of which waited for: 3 -> 1; matrix products, arithmetic and copies ran while one was open for 12% -> 2% of each run, Pallas kernels for 0% -> 0%
where the time goes in v2:
time: 354 us; the launch traced here: 353 us
  Pallas kernels  202 us (57%)
  waiting for transfers between devices  113 us (32%)
  local copies, waits for them, and re-layouts  21.7 us (6%)
  between operations  15.5 us (4%)
    pallas_call x1, Pallas kernels, reduce(): pl.pallas_call(functools.partial(reduce_body, cuts=cuts, row_ticks=row_ti...  113 us
    all_gather x1, waiting for transfers between devices, shards(): piece = lax.all_gather(tokens, 'rows', axis=0, tiled=True)  112 us
    pallas_call x1, Pallas kernels, front(): pl.pallas_call(functools.partial(front_body, tile=tile), grid=(length //...  48.8 us
    pallas_call x1, Pallas kernels, attention(): pl.pallas_call(functools.partial(attention_body, rows=rows), grid_spec=pl...  40.4 us
  transfers between devices with their start and end apart: 1, of which 1 were waited for; matrix products, arithmetic and copies ran while one was open for 2% of the time, Pallas kernels for 0%

profile of v2, /device:TPU:0, one launch (start us, length us, event | category | flops | bytes accessed | tf_op | source)
XLA Modules:
  0.0 353.3 jit_solution(8198550549045862757)
XLA Ops:
  7.2 0.0 copy-start.2
  7.2 0.0 copy-start.5
  7.2 0.0 copy-start.6
  7.2 0.0 copy-start.7
  7.2 0.0 copy-start.8
  7.2 0.0 copy-start.9
  7.2 0.0 copy-start.10
  7.3 0.0 copy-start.4
  7.3 0.0 all-gather.2.cloned.1.call-start
  7.3 0.7 all-gather.2.cloned.1.call-update
  9.3 0.0 copy-done.2
  9.3 0.1 slice.45
  9.4 0.0 copy-done.5
  9.4 0.6 reshape.70.g1_ref
  10.0 0.0 copy-done.6
  10.0 0.6 reshape.71.b1_ref
  10.6 0.0 copy-done.7
  10.6 0.6 reshape.73.bout_ref
  11.2 0.0 copy-done.8
  11.2 0.6 reshape.74.g2_ref
  11.7 0.0 copy-done.9
  11.7 0.6 reshape.75.b2_ref
  12.3 0.0 copy-done.10
  12.3 0.6 reshape.77.bdown_ref
  12.9 0.0 copy-done.4
  12.9 0.6 reshape.72.bqkv_ref
  13.5 1.0 copy.35.segc_ref
  14.5 0.2 convert_reduce_fusion
  14.7 0.6 and_select_fusion.first_ref
  15.3 112.4 %all-gather.2.cloned.1.call-done = bf16[4096,768]{1,0:T(8,128)(2,1)} async-done(((bf16[1024,768]{1,0:T(8,128)(2,1)}), bf16[4096,768]{1,0:T(8,128)(2,1)}) %all-gather.2.cloned.1.call-update) | async-done | bytes 6291472 | tf_op jit(solution)/shard_map/all_gather | solution.py:623
  127.8 2.7 constant_dynamic-slice_fusion.x_ref
  130.4 48.8 %front.1 = (bf16[6,1024,128]{2,1,0:T(8,128)(2,1)}, bf16[6,1024,128]{2,1,0:T(8,128)(2,1)}, bf16[6,1024,128]{2,1,0:T(8,128)(2,1)}, bf16[6,1024,128]{2,1,0:T(8,128)...) custom-call(s32[1]{0:T(128)S(6)} %copy.41.count_ref, ...), custom_call_target="tpu_custom_call" | custom-call | tf_op jit(solution)/shard_map/front/pallas_call | solution.py:143
  179.2 40.4 %attention.1 = (bf16[1024,768]{1,0:T(8,128)(2,1)}, bf16[768,1024]{1,0:T(8,128)(2,1)}, bf16[3,1024,768]{2,1,0:T(8,128)(2,1)}) custom-call(s32[4]{0:T(128)} %and_select_fusion.first_ref, bf16[6,1024,128]{2,1,0:T(8,128)(2,1)} %get-tuple-element.40.q_ref, bf16[6,1024,128]{2,1,0:T(8,128)(2,1)} %get-tuple-element.41.k_ref, ...), custom_call_target="tpu_custom_call" | custom-call | tf_op jit(solution)/shard_map/attention/pallas_call | solution.py:230
  219.6 113.0 %reduce.13 = (bf16[1024,768]{1,0:T(8,128)(2,1)}, bf16[1024,768]{1,0:T(8,128)(2,1)}, f32[24,96,384]{2,1,0:T(8,128)}, f32[8,3072]{1,0:T(8,128)}) custom-call(s32[1]{0:T(128)S(6)} %copy.41.count_ref, bf16[768,1024]{1,0:T(8,128)(2,1)} %get-tuple-element.37.n1t_ref, bf16[768,1024]{1,0:T(8,128)(2,1)} %get-tuple-element.38.n2t_ref, ...), custom_call_target="tpu_custom_call" | custom-call | tf_op jit(solution)/shard_map/reduce/pallas_call | solution.py:560
  332.7 1.5 slice_reduce_fusion
  334.2 1.5 slice.55
  335.7 1.5 slice_reduce_fusion.1
  337.2 0.0 copy-start.3
  337.2 2.3 copy.37
  339.5 0.7 slice.58
  340.2 1.0 slice.57
  341.2 0.0 copy-start.1
  341.2 1.6 slice_bitcast_fusion
  342.8 0.0 copy-done.3
  342.8 0.6 copy.43
  343.4 0.0 copy-done.1
  343.4 0.0 copy-start
  343.4 1.1 copy.44
  344.5 0.8 copy-done
  345.3 1.1 copy.45
Async XLA Ops:
  7.2 2.1 copy-start.2
  7.2 2.2 copy-start.5
  7.2 2.8 copy-start.6
  7.2 3.4 copy-start.7
  7.2 3.9 %copy-start.8 = (f32[768]{0:T(1024)S(1)}, f32[768]{0:T(1024)}, u32[]{:S(2)}) copy-start(f32[768]{0:T(1024)} %param.30) | copy-start | bytes 9220
  7.2 4.5 %copy-start.9 = (f32[768]{0:T(1024)S(1)}, f32[768]{0:T(1024)}, u32[]{:S(2)}) copy-start(f32[768]{0:T(1024)} %param.31) | copy-start | bytes 9220
  7.2 5.1 %copy-start.10 = (f32[768]{0:T(1024)S(1)}, f32[768]{0:T(1024)}, u32[]{:S(2)}) copy-start(f32[768]{0:T(1024)} %param.35) | copy-start | bytes 9220
  7.3 5.7 %copy-start.4 = (f32[2304]{0:T(1024)S(1)}, f32[2304]{0:T(1024)}, u32[]{:S(2)}) copy-start(f32[2304]{0:T(1024)} %param.27) | copy-start | bytes 27652
  7.3 120.5 %all-gather.2.cloned.1.call-start = ((), (), s32[]{:S(2)}) async-start(), calls=%async_computation | async-start | bytes 7864320 | tf_op jit(solution)/shard_map/all_gather | solution.py:623
  337.2 5.6 %copy-start.3 = (f32[768]{0:T(1024)}, f32[768]{0:T(1024)S(1)}, u32[]{:S(2)}) copy-start(f32[768]{0:T(1024)S(1)} %get-tuple-element.116) | copy-start | bytes 9220
  341.2 2.2 copy-start.1
  343.4 2.0 copy-start
Sparse Core Ops, SparseCore 0:
  9.7 118.0 all-gather.1

commit v3 on v2

--- a/solution.py
+++ b/solution.py
@@ -14,6 +14,11 @@
 EXCLUDED = -1e30
 F32 = jnp.float32
 BF16 = jnp.bfloat16
+MESH = pl.DeviceIdType.MESH
+
+
+def remote(src, dst, send, recv, to):
+    return pltpu.make_async_remote_copy(src_ref=src, dst_ref=dst, send_sem=send, recv_sem=recv, device_id=to, device_id_type=MESH)
 
 
 def nn(a, b):
@@ -57,15 +62,107 @@
     return h * phi, phi + h * (e * 0.3989422804014327)
 
 
-def front_body(count_ref, x_ref, cot_ref, cos_ref, sin_ref, g1_ref, b1_ref, wqkv_ref, bqkv_ref, wout_ref, bout_ref,
-               g2_ref, b2_ref, wup_ref, bup_ref, wdown_ref, bdown_ref,
-               q_ref, k_ref, v_ref, gc_ref, n1t_ref, n2t_ref, glt_ref, gl_ref, act_ref, gh_ref, base_ref, t2_ref,
-               gain2_ref, shift2_ref, bup_out, bout_out, *, tile):
+def front_body(count_ref, want_ref, own_ref, cot_ref, cos_ref, sin_ref, g1_ref, b1_ref, bqkv_ref, bout_ref, g2_ref, b2_ref,
+               bup_ref, bdown_ref, wqkv_hbm, wout_hbm, wup_hbm, wdown_hbm,
+               x_ref, q_ref, k_ref, v_ref, gc_ref, n1t_ref, n2t_ref, glt_ref, gl_ref, act_ref, gh_ref, base_ref, t2_ref,
+               gain2_ref, shift2_ref, bup_out, bout_out,
+               wqkv_ref, wout_ref, wup_ref, wdown_ref, wants, from_near, from_half, to_inner, to_end,
+               w_sem, want_send, want_recv, near_send, near_recv, inner_send, end_send, half_recv, *, tile):
     step = pl.program_id(0)
-    rows, width = x_ref.shape
+    steps = pl.num_programs(0)
+    rows, width = cot_ref.shape
     pairs = width // PAIR
     ff = wup_ref.shape[1]
-    x = x_ref[...].astype(F32)
+    chunks = own_ref.shape[0] // rows
+    d, z = lax.axis_index("dp"), lax.axis_index("rows")
+    inner = (z + 1) // 2 % 2
+    near = z + 1 - 2 * (z % 2)
+    other_inner, other_end = 3 - z, 6 - 3 * z
+    loads = [pltpu.make_async_copy(src, dst, w_sem.at[j]) for j, (src, dst) in enumerate(
+        ((wqkv_hbm, wqkv_ref), (wout_hbm, wout_ref), (wup_hbm, wup_ref), (wdown_hbm, wdown_ref)))]
+
+    def span(i):
+        return pl.ds(pl.multiple_of(i * rows, rows), rows)
+
+    def want_copy(j):
+        to = lax.rem(z + j, 4)
+        return remote(wants.at[0], wants.at[j], want_send.at[j], want_recv.at[j], (d, to))
+
+    def near_copy(i):
+        return remote(own_ref.at[span(i)], from_near.at[span(i)], near_send.at[i], near_recv.at[i], (d, near))
+
+    def inner_copy(i):
+        return remote(to_inner.at[span(i)], from_half.at[span(i)], inner_send.at[i], half_recv.at[i], (d, other_inner))
+
+    def end_copy(i):
+        return remote(to_end.at[span(i)], from_half.at[span(i)], end_send.at[i], half_recv.at[i], (d, other_end))
+
+    def wanted(by):
+        return wants[lax.rem(z - by + 4, 4), 0:1, 0:1]
+
+    def relay(i):
+        @pl.when(inner == 1)
+        def _():
+            near_copy(i).wait_recv()
+            mine = own_ref[span(i), :].astype(F32)
+            theirs = from_near[span(i), :].astype(F32)
+            to_end[span(i), :] = jnp.where(wanted(other_end) == near, theirs, mine).astype(BF16)
+            end_copy(i).start()
+            to_inner[span(i), :] = jnp.where(wanted(other_inner) == near, theirs, mine).astype(BF16)
+            inner_copy(i).start()
+
+    @pl.when(step == 0)
+    def _():
+        barrier = pltpu.get_barrier_semaphore()
+        for j in (1, 2, 3):
+            pl.semaphore_signal(barrier, inc=1, device_id=(d, lax.rem(z + j, 4)), device_id_type=MESH)
+        wants[0] = want_ref[...]
+        pl.semaphore_wait(barrier, 3)
+        for j in (1, 2, 3):
+            want_copy(j).start()
+
+        def hand(i, carry):
+            near_copy(i).start()
+            return carry
+
+        lax.fori_loop(0, chunks, hand, 0)
+        for load in loads:
+            load.start()
+        for j in (1, 2, 3):
+            want_copy(j).wait()
+        relay(0)
+        gain2_ref[...] = jnp.zeros_like(gain2_ref)
+        shift2_ref[...] = jnp.zeros_like(shift2_ref)
+        bup_out[...] = jnp.zeros_like(bup_out)
+        bout_out[...] = jnp.zeros_like(bout_out)
+
+    @pl.when(step + 1 < chunks)
+    def _():
+        relay(step + 1)
+
+    @pl.when(step == 0)
+    def _():
+        for load in loads:
+            load.wait()
+
+    place = step * rows + lax.broadcasted_iota(jnp.int32, (rows, 1), 0)
+    gl = jnp.where(place < count_ref[0], cot_ref[...].astype(F32), 0.0)
+    gl16 = gl.astype(BF16)
+    gl_ref[...] = gl16
+    glt_ref[...] = gl16.T
+    bout_out[...] += jnp.sum(gl, axis=0, keepdims=True)
+    for p in range(pairs):
+        gc_ref[p] = nt(gl16, wout_ref[p * PAIR : (p + 1) * PAIR, :]).astype(BF16)
+
+    @pl.when(inner == 0)
+    def _():
+        near_copy(step).wait_recv()
+
+    inner_copy(step).wait_recv()
+    source = wanted(z)
+    x = jnp.where(source == near, from_near[span(step), :].astype(F32), from_half[span(step), :].astype(F32))
+    x = jnp.where(source == z, own_ref[span(step), :].astype(F32), x)
+    x_ref[...] = x.astype(BF16)
     centred = x - jnp.mean(x, axis=1, keepdims=True)
     r = lax.rsqrt(jnp.mean(centred * centred, axis=1, keepdims=True) + EPSILON)
     n = centred * r
@@ -73,23 +170,8 @@
     n2 = (n * g2_ref[...] + b2_ref[...]).astype(BF16)
     n1t_ref[...] = n1.T
     n2t_ref[...] = n2.T
-    place = step * rows + lax.broadcasted_iota(jnp.int32, (rows, 1), 0)
-    gl = jnp.where(place < count_ref[0], cot_ref[...].astype(F32), 0.0)
-    gl16 = gl.astype(BF16)
-    gl_ref[...] = gl16
-    glt_ref[...] = gl16.T
-
-    @pl.when(step == 0)
-    def _():
-        gain2_ref[...] = jnp.zeros_like(gain2_ref)
-        shift2_ref[...] = jnp.zeros_like(shift2_ref)
-        bup_out[...] = jnp.zeros_like(bup_out)
-        bout_out[...] = jnp.zeros_like(bout_out)
-
-    bout_out[...] += jnp.sum(gl, axis=0, keepdims=True)
     cosine, sine = cos_ref[...], sin_ref[...]
     for p in range(pairs):
-        cols = slice(p * PAIR, (p + 1) * PAIR)
         for which, ref in enumerate((q_ref, k_ref, v_ref)):
             wide = slice(which * width + p * PAIR, which * width + (p + 1) * PAIR)
             u = nn(n1, wqkv_ref[:, wide]) + bqkv_ref[:, wide]
@@ -98,7 +180,6 @@
             if which == 0:
                 u = u * (HEAD_DIM ** -0.5)
             ref[p] = u.astype(BF16)
-        gc_ref[p] = nt(gl16, wout_ref[cols, :]).astype(BF16)
     mlp = x + (bdown_ref[...] + bout_ref[...])
     grad_two = jnp.zeros((rows, width), F32)
     for f in range(0, ff, tile):
@@ -119,38 +200,58 @@
     gain2_ref[...] += jnp.sum(grad_two * n, axis=0, keepdims=True)
     shift2_ref[...] += jnp.sum(grad_two, axis=0, keepdims=True)
 
-
-def front(count, x, cot, cosine, sine, g1, b1, wqkv, bqkv, wout, bout, g2, b2, wup, bup, wdown, bdown, rows=256, tile=512):
-    length, width = x.shape
+    @pl.when(step == steps - 1)
+    def _():
+        def done(i, carry):
+            near_copy(i).wait_send()
+
+            @pl.when(inner == 1)
+            def _():
+                inner_copy(i).wait_send()
+                end_copy(i).wait_send()
+            return carry
+
+        lax.fori_loop(0, chunks, done, 0)
+
+
+def front(count, want, own, cot, cosine, sine, g1, b1, wqkv, bqkv, wout, bout, g2, b2, wup, bup, wdown, bdown, rows=128, tile=512):
+    length, width = own.shape
     ff = wup.shape[1]
     pairs = width // PAIR
-    once = pl.Buffered(1)
+    chunks = length // rows
 
     def row(cols):
         return pl.BlockSpec((rows, cols), lambda i: (i, 0))
 
     def whole(a):
-        return pl.BlockSpec(a.shape, lambda i: (0,) * a.ndim, pipeline_mode=once)
+        return pl.BlockSpec(a.shape, lambda i: (0,) * a.ndim, pipeline_mode=pl.Buffered(1))
 
     heads = pl.BlockSpec((pairs, rows, PAIR), lambda i: (0, i, 0))
+    down = pl.BlockSpec((width, rows), lambda i: (0, i))
 
     def vec(cols):
         return pl.BlockSpec((1, cols), lambda i: (0, 0))
 
     vectors = [v.reshape(1, -1) for v in (g1, b1, bqkv, bout, g2, b2, bup, bdown)]
-    g1, b1, bqkv, bout, g2, b2, bup, bdown = vectors
+    weights = (wqkv, wout, wup, wdown)
     s = jax.ShapeDtypeStruct
+    dma = pltpu.SemaphoreType.DMA
     return pl.pallas_call(
         functools.partial(front_body, tile=tile),
-        grid=(length // rows,),
-        in_specs=[pl.BlockSpec(memory_space=pltpu.SMEM), row(width), row(width), row(PAIR), row(PAIR)]
-        + [whole(a) for a in (g1, b1, wqkv, bqkv, wout, bout, g2, b2, wup, bup, wdown, bdown)],
-        out_specs=[heads] * 4 + [pl.BlockSpec((width, rows), lambda i: (0, i))] * 3 + [row(width)] + [row(ff)] * 2 + [row(width)] * 2 + [vec(width), vec(width), vec(ff), vec(width)],
-        out_shape=[s((pairs, length, PAIR), BF16)] * 4 + [s((width, length), BF16)] * 3 + [s((length, width), BF16)] + [s((length, ff), BF16)] * 2
+        grid=(chunks,),
+        in_specs=[pl.BlockSpec(memory_space=pltpu.SMEM), whole(want), whole(own), row(width), row(PAIR), row(PAIR)]
+        + [whole(a) for a in vectors] + [pl.BlockSpec(memory_space=pl.ANY)] * 4,
+        out_specs=[row(width)] + [heads] * 4 + [down] * 3 + [row(width)] + [row(ff)] * 2 + [row(width)] * 2
+        + [vec(width), vec(width), vec(ff), vec(width)],
+        out_shape=[s((length, width), BF16)] + [s((pairs, length, PAIR), BF16)] * 4 + [s((width, length), BF16)] * 3
+        + [s((length, width), BF16)] + [s((length, ff), BF16)] * 2
         + [s((length, width), F32)] * 2 + [s((1, width), F32), s((1, width), F32), s((1, ff), F32), s((1, width), F32)],
-        compiler_params=pltpu.CompilerParams(vmem_limit_bytes=56 * 2**20),
+        scratch_shapes=[pltpu.VMEM(w.shape, BF16) for w in weights]
+        + [pltpu.VMEM((4, 8, 128), jnp.int32)] + [pltpu.VMEM((length, width), BF16)] * 4
+        + [dma((4,)), dma((4,)), dma((4,))] + [dma((chunks,))] * 5,
+        compiler_params=pltpu.CompilerParams(vmem_limit_bytes=60 * 2**20, collective_id=1, has_side_effects=True),
         name="front",
-    )(count, x, cot, cosine, sine, g1, b1, wqkv, bqkv, wout, bout, g2, b2, wup, bup, wdown, bdown)
+    )(count, want, own, cot, cosine, sine, *vectors, *weights)
 
 
 def attention_body(first_ref, q_ref, k_ref, v_ref, gc_ref, segc_ref, segr_ref, cos_ref, sin_ref,
@@ -242,7 +343,6 @@
     )(first, q, k, v, gc, segment.reshape(-1, 1), segment.reshape(1, -1), cosine, sine)
 
 
-MESH = pl.DeviceIdType.MESH
 CHUNK = 384
 
 
@@ -259,10 +359,6 @@
         self.inner = (self.z + 1) // 2 % 2
         self.near = (self.d, self.z + 1 - 2 * (self.z % 2))
         self.far = (self.d, 3 - self.z)
-
-
-def remote(src, dst, send, recv, to):
-    return pltpu.make_async_remote_copy(src_ref=src, dst_ref=dst, send_sem=send, recv_sem=recv, device_id=to, device_id_type=MESH)
 
 
 class Everywhere:
@@ -619,12 +715,10 @@
            out_bias, ln2_gain, ln2_bias, up_weight, up_bias, down_weight, down_bias):
     length, width = cotangent.shape
     ff = up_weight.shape[1]
-    source = regroup[0] % lax.axis_size("rows")
-    piece = lax.all_gather(tokens, "rows", axis=0, tiled=True)
-    arrived = lax.dynamic_slice_in_dim(piece, source * length, length, 0)
+    want = jnp.full((8, 128), regroup[0] % lax.axis_size("rows"), jnp.int32)
     cosine, sine = (jnp.asarray(t) for t in rotary_tables(length))
-    (q, k, v, gc, n1t, n2t, glt, gl, act, gh, base, t2, gain2, shift2, bias_up, bias_out) = front(
-        true_counts, arrived, cotangent, cosine, sine, ln1_gain, ln1_bias, qkv_weight, qkv_bias, out_weight, out_bias,
+    (arrived, q, k, v, gc, n1t, n2t, glt, gl, act, gh, base, t2, gain2, shift2, bias_up, bias_out) = front(
+        true_counts, want, tokens, cotangent, cosine, sine, ln1_gain, ln1_bias, qkv_weight, qkv_bias, out_weight, out_bias,
         ln2_gain, ln2_bias, up_weight, up_bias, down_weight, down_bias)
     ctx, ctxt, gu = attention(q, k, v, gc, segment_ids, cosine, sine, rows=256)
     last = by_kernel if (lax.axis_size("dp"), lax.axis_size("rows")) == (8, 4) else by_collectives

time: 354 us -> 270 us (0.76)
  waiting for transfers between devices: 113 us -> 0 us
  Pallas kernels: 202 us -> 238 us
  between operations: 15.5 us -> 1.99 us
  local copies, waits for them, and re-layouts: 21.7 us -> 25.7 us
    all_gather x1 -> x0, waiting for transfers between devices: 112 us -> none  [shards(): piece = lax.all_gather(tokens, 'rows', axis=0, tiled=True)]
    pallas_call x1, Pallas kernels: 48.8 us -> 86.6 us  [front(): pl.pallas_call(functools.partial(front_body, tile=tile), grid=(chunks,),...]
    reshape x7, local copies, waits for them, and re-layouts: 4.09 us -> 8.91 us  [front(): v.reshape(1, -1)]
  transfers between devices with their start and end apart: 1 -> 0, of which waited for: 1 -> 0; matrix products, arithmetic and copies ran while one was open for 2% -> 0% of each run, Pallas kernels for 0% -> 0%
where the time goes in v3:
time: 270 us; the launch traced here: 267 us
  Pallas kernels  238 us (88%)
  local copies, waits for them, and re-layouts  25.7 us (10%)
    pallas_call x1, Pallas kernels, reduce(): pl.pallas_call(functools.partial(reduce_body, cuts=cuts, row_ticks=row_ti...  111 us
    pallas_call x1, Pallas kernels, front(): pl.pallas_call(functools.partial(front_body, tile=tile), grid=(chunks,),...  86.6 us
    pallas_call x1, Pallas kernels, attention(): pl.pallas_call(functools.partial(attention_body, rows=rows), grid_spec=pl...  40.4 us
    reshape x7, local copies, waits for them, and re-layouts, front(): v.reshape(1, -1)  8.91 us

profile of v3, /device:TPU:0, one launch (start us, length us, event | category | flops | bytes accessed | tf_op | source)
XLA Modules:
  0.0 266.8 jit_solution(10971377007678081877)
XLA Ops:
  2.0 0.8 slice.45
  2.7 0.9 convert_reduce_fusion
  3.6 0.5 and_select_fusion.first_ref
  4.1 1.3 reshape.70.g1_ref
  5.4 1.3 reshape.71.b1_ref
  6.7 1.3 reshape.73.bout_ref
  7.9 1.3 reshape.74.g2_ref
  9.2 1.3 reshape.75.b2_ref
  10.5 1.3 reshape.77.bdown_ref
  11.7 0.6 broadcast_in_dim.7.want_ref
  12.3 1.3 reshape.72.bqkv_ref
  13.6 1.7 copy.35.segc_ref
  15.3 86.6 %front.1 = (bf16[1024,768]{1,0:T(8,128)(2,1)}, bf16[6,1024,128]{2,1,0:T(8,128)(2,1)}, bf16[6,1024,128]{2,1,0:T(8,128)(2,1)}, bf16[6,1024,128]{2,1,0:T(8,128)(2,1...) custom-call(s32[1]{0:T(128)S(6)} %copy.41.count_ref, ...), custom_call_target="tpu_custom_call" | custom-call | tf_op jit(solution)/shard_map/front/pallas_call | solution.py:239
  101.9 40.4 %attention.1 = (bf16[1024,768]{1,0:T(8,128)(2,1)}, bf16[768,1024]{1,0:T(8,128)(2,1)}, bf16[3,1024,768]{2,1,0:T(8,128)(2,1)}) custom-call(s32[4]{0:T(128)} %and_select_fusion.first_ref, bf16[6,1024,128]{2,1,0:T(8,128)(2,1)} %get-tuple-element.41.q_ref, bf16[6,1024,128]{2,1,0:T(8,128)(2,1)} %get-tuple-element.42.k_ref, ...), custom_call_target="tpu_custom_call" | custom-call | tf_op jit(solution)/shard_map/attention/pallas_call | solution.py:331
  142.4 110.6 %reduce.13 = (bf16[1024,768]{1,0:T(8,128)(2,1)}, bf16[1024,768]{1,0:T(8,128)(2,1)}, f32[24,96,384]{2,1,0:T(8,128)}, f32[8,3072]{1,0:T(8,128)}) custom-call(s32[1]{0:T(128)S(6)} %copy.41.count_ref, bf16[768,1024]{1,0:T(8,128)(2,1)} %get-tuple-element.38.n1t_ref, bf16[768,1024]{1,0:T(8,128)(2,1)} %get-tuple-element.39.n2t_ref, ...), custom_call_target="tpu_custom_call" | custom-call | tf_op jit(solution)/shard_map/reduce/pallas_call | solution.py:656
  253.0 1.5 slice_reduce_fusion
  254.5 1.5 slice.55
  256.0 1.5 slice_reduce_fusion.1
  257.5 0.0 copy-start.2
  257.5 2.3 copy.37
  259.8 0.7 slice.58
  260.5 1.0 slice.57
  261.5 0.0 copy-start.1
  261.5 1.6 slice_bitcast_fusion
  263.1 0.0 copy-done.2
  263.1 0.6 copy.43
  263.7 0.0 copy-done.1
  263.7 0.0 copy-start
  263.7 1.1 copy.44
  264.8 0.8 copy-done
  265.6 1.1 copy.45
Async XLA Ops:
  257.5 5.6 %copy-start.2 = (f32[768]{0:T(1024)}, f32[768]{0:T(1024)S(1)}, u32[]{:S(2)}) copy-start(f32[768]{0:T(1024)S(1)} %get-tuple-element.118) | copy-start | bytes 9220
  261.5 2.2 copy-start.1
  263.7 2.0 copy-start

commit v4 on v3

--- a/solution.py
+++ b/solution.py
@@ -62,12 +62,12 @@
     return h * phi, phi + h * (e * 0.3989422804014327)
 
 
-def front_body(count_ref, want_ref, own_ref, cot_ref, cos_ref, sin_ref, g1_ref, b1_ref, bqkv_ref, bout_ref, g2_ref, b2_ref,
-               bup_ref, bdown_ref, wqkv_hbm, wout_hbm, wup_hbm, wdown_hbm,
+def front_body(count_ref, want_ref, own_ref, cot_ref, cos_ref, sin_ref, g1_vec, b1_vec, bqkv_vec, bout_vec, g2_vec, b2_vec,
+               bup_vec, bdown_vec, wqkv_hbm, wout_hbm, wup_hbm, wdown_hbm,
                x_ref, q_ref, k_ref, v_ref, gc_ref, n1t_ref, n2t_ref, glt_ref, gl_ref, act_ref, gh_ref, base_ref, t2_ref,
                gain2_ref, shift2_ref, bup_out, bout_out,
                wqkv_ref, wout_ref, wup_ref, wdown_ref, wants, from_near, from_half, to_inner, to_end,
-               w_sem, want_send, want_recv, near_send, near_recv, inner_send, end_send, half_recv, *, tile):
+               g1_ref, b1_ref, bqkv_ref, bout_ref, g2_ref, b2_ref, bup_ref, bdown_ref, w_sem, want_send, want_recv, near_send, near_recv, inner_send, end_send, half_recv, *, tile):
     step = pl.program_id(0)
     steps = pl.num_programs(0)
     rows, width = cot_ref.shape
@@ -116,7 +116,7 @@
         barrier = pltpu.get_barrier_semaphore()
         for j in (1, 2, 3):
             pl.semaphore_signal(barrier, inc=1, device_id=(d, lax.rem(z + j, 4)), device_id_type=MESH)
-        wants[0] = want_ref[...]
+        wants[0] = jnp.full(wants.shape[1:], want_ref[0] % 4, jnp.int32)
         pl.semaphore_wait(barrier, 3)
         for j in (1, 2, 3):
             want_copy(j).start()
@@ -131,6 +131,9 @@
         for j in (1, 2, 3):
             want_copy(j).wait()
         relay(0)
+        for vec, ref in ((g1_vec, g1_ref), (b1_vec, b1_ref), (bqkv_vec, bqkv_ref), (bout_vec, bout_ref), (g2_vec, g2_ref),
+                         (b2_vec, b2_ref), (bup_vec, bup_ref), (bdown_vec, bdown_ref)):
+            ref[...] = vec[...].reshape(1, -1)
         gain2_ref[...] = jnp.zeros_like(gain2_ref)
         shift2_ref[...] = jnp.zeros_like(shift2_ref)
         bup_out[...] = jnp.zeros_like(bup_out)
@@ -232,14 +235,14 @@
     def vec(cols):
         return pl.BlockSpec((1, cols), lambda i: (0, 0))
 
-    vectors = [v.reshape(1, -1) for v in (g1, b1, bqkv, bout, g2, b2, bup, bdown)]
+    vectors = (g1, b1, bqkv, bout, g2, b2, bup, bdown)
     weights = (wqkv, wout, wup, wdown)
     s = jax.ShapeDtypeStruct
     dma = pltpu.SemaphoreType.DMA
     return pl.pallas_call(
         functools.partial(front_body, tile=tile),
         grid=(chunks,),
-        in_specs=[pl.BlockSpec(memory_space=pltpu.SMEM), whole(want), whole(own), row(width), row(PAIR), row(PAIR)]
+        in_specs=[pl.BlockSpec(memory_space=pltpu.SMEM), pl.BlockSpec(memory_space=pltpu.SMEM), whole(own), row(width), row(PAIR), row(PAIR)]
         + [whole(a) for a in vectors] + [pl.BlockSpec(memory_space=pl.ANY)] * 4,
         out_specs=[row(width)] + [heads] * 4 + [down] * 3 + [row(width)] + [row(ff)] * 2 + [row(width)] * 2
         + [vec(width), vec(width), vec(ff), vec(width)],
@@ -248,58 +251,74 @@
         + [s((length, width), F32)] * 2 + [s((1, width), F32), s((1, width), F32), s((1, ff), F32), s((1, width), F32)],
         scratch_shapes=[pltpu.VMEM(w.shape, BF16) for w in weights]
         + [pltpu.VMEM((4, 8, 128), jnp.int32)] + [pltpu.VMEM((length, width), BF16)] * 4
-        + [dma((4,)), dma((4,)), dma((4,))] + [dma((chunks,))] * 5,
+        + [pltpu.VMEM((1, v.shape[0]), F32) for v in vectors] + [dma((4,)), dma((4,)), dma((4,))] + [dma((chunks,))] * 5,
         compiler_params=pltpu.CompilerParams(vmem_limit_bytes=60 * 2**20, collective_id=1, has_side_effects=True),
         name="front",
     )(count, want, own, cot, cosine, sine, *vectors, *weights)
 
 
-def attention_body(first_ref, q_ref, k_ref, v_ref, gc_ref, segc_ref, segr_ref, cos_ref, sin_ref,
-                   ctx_ref, ctxt_ref, gu_ref, dk_acc, dv_acc, *, rows):
-    length = q_ref.shape[1]
+def attention_body(q_ref, k_ref, v_ref, gc_ref, seg_ref, cos_ref, sin_ref,
+                   ctx_ref, ctxt_ref, gu_ref, dk_acc, dv_acc, segc_ref, segr_ref, first_ref, *, rows):
+    group, length, _ = q_ref.shape
+    total = length // rows
+    each = range(group)
+
+    @pl.when(pl.program_id(0) == 0)
+    def _():
+        seg = seg_ref[...].reshape(1, -1)
+        segr_ref[...] = seg
+        segc_ref[...] = jnp.broadcast_to(seg, (8, length)).T[:, :1]
+        wide = seg.astype(F32)
+        for b in range(total):
+            before = jnp.sum(jnp.where(wide < wide[:, b * rows : b * rows + 1], 1.0, 0.0))
+            first_ref[b] = before.astype(jnp.int32) // rows
+
     lane = lax.broadcasted_iota(jnp.int32, (rows, PAIR), 1)
     low = lane < HEAD_DIM
     dk_acc[...] = jnp.zeros_like(dk_acc)
     dv_acc[...] = jnp.zeros_like(dv_acc)
 
+    def both(ref, h, begin):
+        t = ref[h, pl.ds(begin, rows), :]
+        zero = jnp.zeros_like(t)
+        return jnp.concatenate([jnp.where(low, t, zero), jnp.where(low, zero, t)], axis=0)
+
     def block(b, blocks):
         begin = pl.multiple_of(b * rows, rows)
         start = pl.multiple_of((b + 1 - blocks) * rows, rows)
         span = blocks * rows
-        q = q_ref[0, pl.ds(begin, rows), :]
-        g = gc_ref[0, pl.ds(begin, rows), :]
-        zero = jnp.zeros_like(q)
-        q2 = jnp.concatenate([jnp.where(low, q, zero), jnp.where(low, zero, q)], axis=0)
-        g2 = jnp.concatenate([jnp.where(low, g, zero), jnp.where(low, zero, g)], axis=0)
-        k = k_ref[0, pl.ds(start, span), :]
-        v = v_ref[0, pl.ds(start, span), :]
+        q2 = [both(q_ref, h, begin) for h in each]
+        g2 = [both(gc_ref, h, begin) for h in each]
+        k = [k_ref[h, pl.ds(start, span), :] for h in each]
+        v = [v_ref[h, pl.ds(start, span), :] for h in each]
         segt = segc_ref[pl.ds(begin, rows), :]
         segs = segr_ref[:, pl.ds(start, span)]
         t_at = begin + lax.broadcasted_iota(jnp.int32, (rows, span), 0)
         s_at = start + lax.broadcasted_iota(jnp.int32, (rows, span), 1)
         allowed = (segt == segs) & (s_at <= t_at)
         allowed = jnp.concatenate([allowed, allowed], axis=0)
-        scores = jnp.where(allowed, nt(q2, k), EXCLUDED)
-        peak = jnp.max(scores, axis=1, keepdims=True)
-        e = jnp.exp(scores - peak)
-        p = e * (1.0 / jnp.sum(e, axis=1, keepdims=True))
-        p16 = p.astype(BF16)
-        c2 = nn(p16, v)
-        context = jnp.where(low, c2[:rows], c2[rows:]).astype(BF16)
-        ctx_ref[pl.ds(begin, rows), :] = context
-        ctxt_ref[:, pl.ds(begin, rows)] = context.T
-        dp = nt(g2, v)
-        inner = jnp.sum(p * dp, axis=1, keepdims=True)
-        ds16 = (p * (dp - inner)).astype(BF16)
-        d2 = nn(ds16, k)
-        dq = jnp.where(low, d2[:rows], d2[rows:]) * (HEAD_DIM ** -0.5)
+        scores = [jnp.where(allowed, nt(q2[h], k[h]), EXCLUDED) for h in each]
+        dp = [nt(g2[h], v[h]) for h in each]
+        e = [jnp.exp(scores[h] - jnp.max(scores[h], axis=1, keepdims=True)) for h in each]
+        p = [e[h] * (1.0 / jnp.sum(e[h], axis=1, keepdims=True)) for h in each]
+        p16 = [p[h].astype(BF16) for h in each]
+        c2 = [nn(p16[h], v[h]) for h in each]
+        for h in each:
+            dv_acc[h, pl.ds(start, span), :] += tn(p16[h], g2[h])
+        w = [p[h] * dp[h] for h in each]
+        ds16 = [(w[h] - p[h] * jnp.sum(w[h], axis=1, keepdims=True)).astype(BF16) for h in each]
+        d2 = [nn(ds16[h], k[h]) for h in each]
+        for h in each:
+            dk_acc[h, pl.ds(start, span), :] += tn(ds16[h], q2[h])
         cosine = cos_ref[pl.ds(begin, rows), :]
         sine = sin_ref[pl.ds(begin, rows), :]
-        gu_ref[0, pl.ds(begin, rows), :] = (dq * cosine - turned(dq) * sine).astype(BF16)
-        dk_acc[pl.ds(start, span), :] += tn(ds16, q2)
-        dv_acc[pl.ds(start, span), :] += tn(p16, g2)
-
-    total = length // rows
+        for h in each:
+            cols = slice(h * PAIR, (h + 1) * PAIR)
+            context = jnp.where(low, c2[h][:rows], c2[h][rows:]).astype(BF16)
+            ctx_ref[pl.ds(begin, rows), cols] = context
+            ctxt_ref[cols, pl.ds(begin, rows)] = context.T
+            dq = jnp.where(low, d2[h][:rows], d2[h][rows:]) * (HEAD_DIM ** -0.5)
+            gu_ref[0, pl.ds(begin, rows), cols] = (dq * cosine - turned(dq) * sine).astype(BF16)
 
     def loop(b, carry):
         count = b + 1 - first_ref[b]
@@ -310,37 +329,35 @@
         return carry
 
     lax.fori_loop(0, total, loop, 0)
-    dk = dk_acc[...]
-    gu_ref[1] = (dk * cos_ref[...] - turned(dk) * sin_ref[...]).astype(BF16)
-    gu_ref[2] = dv_acc[...].astype(BF16)
-
-
-def attention(q, k, v, gc, segment, cosine, sine, rows=128):
+    for h in each:
+        cols = slice(h * PAIR, (h + 1) * PAIR)
+        dk = dk_acc[h]
+        gu_ref[1, :, cols] = (dk * cos_ref[...] - turned(dk) * sin_ref[...]).astype(BF16)
+        gu_ref[2, :, cols] = dv_acc[h].astype(BF16)
+
+
+def attention(q, k, v, gc, segment, cosine, sine, rows=256, group=2):
     pairs, length, _ = q.shape
-    total = length // rows
-    begins = jnp.sum((segment[None, :] < segment[::rows, None]).astype(jnp.int32), axis=1)
-    first = begins // rows
-    head = pl.BlockSpec((1, length, PAIR), lambda h, *_: (h, 0, 0))
-    cols = pl.BlockSpec((length, PAIR), lambda h, *_: (0, h))
+    head = pl.BlockSpec((group, length, PAIR), lambda h: (h, 0, 0))
+    cols = pl.BlockSpec((length, group * PAIR), lambda h: (0, h))
     s = jax.ShapeDtypeStruct
     width = pairs * PAIR
 
-    def whole(shape):
-        return pl.BlockSpec(shape, lambda h, *_: (0, 0), pipeline_mode=pl.Buffered(1))
+    def whole(a):
+        return pl.BlockSpec(a.shape, lambda h: (0,) * a.ndim, pipeline_mode=pl.Buffered(1))
 
     return pl.pallas_call(
         functools.partial(attention_body, rows=rows),
-        grid_spec=pltpu.PrefetchScalarGridSpec(
-            num_scalar_prefetch=1,
-            grid=(pairs,),
-            in_specs=[head] * 4 + [whole((length, 1)), whole((1, length)), whole((length, PAIR)), whole((length, PAIR))],
-            out_specs=[cols, pl.BlockSpec((PAIR, length), lambda h, *_: (h, 0)), pl.BlockSpec((3, length, PAIR), lambda h, *_: (0, 0, h))],
-            scratch_shapes=[pltpu.VMEM((length, PAIR), F32)] * 2,
-        ),
+        grid=(pairs // group,),
+        in_specs=[head] * 4 + [whole(segment), whole(cosine), whole(sine)],
+        out_specs=[cols, pl.BlockSpec((group * PAIR, length), lambda h: (h, 0)),
+                   pl.BlockSpec((3, length, group * PAIR), lambda h: (0, 0, h))],
+        scratch_shapes=[pltpu.VMEM((group, length, PAIR), F32)] * 2
+        + [pltpu.VMEM((length, 1), jnp.int32), pltpu.VMEM((1, length), jnp.int32), pltpu.SMEM((length // rows,), jnp.int32)],
         out_shape=[s((length, width), BF16), s((width, length), BF16), s((3, length, width), BF16)],
         compiler_params=pltpu.CompilerParams(vmem_limit_bytes=56 * 2**20),
         name="attention",
-    )(first, q, k, v, gc, segment.reshape(-1, 1), segment.reshape(1, -1), cosine, sine)
+    )(q, k, v, gc, segment, cosine, sine)
 
 
 CHUNK = 384
@@ -374,7 +391,7 @@
         self.copy(hop, to).wait()
         self.held[hop + 1] = self.held[hop] + self.come[hop]
 
-    def hop(self, tick):
+    def hop(self, tick, spacing):
         at = self.at
         over = (at.over_core, at.over_x, at.over_y)
 
@@ -383,12 +400,12 @@
             self.copy(0, over[0]).start()
 
         for j in (1, 2):
-            @pl.when(tick == j)
+            @pl.when(tick == j * spacing)
             def _():
                 self.take(j - 1, over[j - 1])
                 self.copy(j, over[j]).start()
 
-        @pl.when(tick == 3)
+        @pl.when(tick == 3 * spacing)
         def _():
             self.take(2, over[2])
 
@@ -396,22 +413,22 @@
             def _():
                 self.copy(3, at.near).start()
 
-        @pl.when((tick == 4) & (at.inner == 1))
+        @pl.when((tick == 4 * spacing) & (at.inner == 1))
         def _():
             self.copy(3, at.near).wait_recv()
             self.held[4] = self.held[3] + self.come[3]
             self.copy(4, at.far).start()
 
-        @pl.when((tick == 4) & (at.inner == 0))
+        @pl.when((tick == 4 * spacing) & (at.inner == 0))
         def _():
             self.copy(3, at.near).wait_send()
 
-        @pl.when((tick == 5) & (at.inner == 1))
+        @pl.when((tick == 5 * spacing) & (at.inner == 1))
         def _():
             self.take(4, at.far)
             self.copy(5, at.near).start()
 
-        @pl.when(tick == 6)
+        @pl.when(tick == 6 * spacing)
         def _():
             @pl.when(at.inner == 1)
             def _():
@@ -423,16 +440,16 @@
                 self.held[5] = self.come[5]
 
 
-LAGS = dict(core=1, first=3, second=5, z=6, mid=8, back=9)
-
-
-def reduce_body(count_ref, n1t_ref, n2t_ref, glt_ref, ctxt_ref, gh_ref, act_ref, glc_ref, guc_ref,
-                x_ref, gl_ref, base_ref, t2_ref, ctx_ref, gu_ref, wqkv_ref, wout_ref, g1_ref,
-                gain2_ref, shift2_ref, bup_ref, bout_ref,
-                out_ref, ig_ref, grads_ref, vec_ref,
-                part, from_core, from_first, from_second, zsum, from_near, from_far,
+LAGS = dict(core=1, first=4, second=7, z=9, mid=11, back=13)
+SPACING = 3
+
+
+def reduce_body(count_ref, gh_ref, act_ref, glc_ref, guc_ref, x_ref, gl_ref, base_ref, t2_ref, ctx_ref, gu_ref, g1_ref,
+                gain2_ref, shift2_ref, bup_ref, bout_ref, n2t_hbm, wout_hbm, wqkv_hbm, glt_hbm, ctxt_hbm, n1t_hbm,
+                out_ref, ig_ref, total_ref, vec_ref,
+                n2t_ref, wout_ref, wqkv_ref, glt_ref, ctxt_ref, n1t_ref, load_sem, part, from_core, from_first, from_second, zsum, from_near, from_far,
                 c_send, c_recv, f_send, f_recv, s_send, s_recv, n_send, n_recv, m_send, m_recv,
-                held_n, come_n, held_v, come_v, n_s, n_r, v_s, v_r, gain1, shift1, bqkv, *, cuts, row_ticks):
+                held_v, come_v, v_s, v_r, gain1, shift1, bqkv, *, cuts, row_ticks):
     tick = pl.program_id(0)
     at = Line()
     chunks = cuts[-1]
@@ -440,8 +457,13 @@
     width = wout_ref.shape[0]
     block = width // 8
 
+    loads = [pltpu.make_async_copy(src, dst, load_sem.at[j]) for j, (src, dst) in enumerate(
+        ((n2t_hbm, n2t_ref), (wout_hbm, wout_ref), (wqkv_hbm, wqkv_ref), (glt_hbm, glt_ref), (ctxt_hbm, ctxt_ref),
+         (n1t_hbm, n1t_ref)))]
+
     @pl.when(tick == 0)
     def _():
+        loads[0].start()
         barrier = pltpu.get_barrier_semaphore()
         for to in (at.over_core, at.over_x, at.over_y, at.near):
             pl.semaphore_signal(barrier, inc=1, device_id=to, device_id_type=MESH)
@@ -455,7 +477,8 @@
         def _():
             pl.semaphore_wait(barrier, 4)
 
-        held_n[0] = jnp.full(held_n.shape[1:], count_ref[0].astype(F32), F32)
+        for load in loads[1:]:
+            load.start()
 
     def places(i):
         even = 1 - i % 2
@@ -503,6 +526,15 @@
                 part[slot, c, a, b] = rows[j * block : (j + 1) * block].astype(BF16)
         core_copy(tick).start()
 
+    @pl.when(tick == 0)
+    def _():
+        loads[0].wait()
+
+    @pl.when(tick == 1)
+    def _():
+        for load in loads[1:]:
+            load.wait()
+
     starts = (0,) + cuts[:-1]
     operands = ((n2t_ref, gh_ref), (glt_ref, act_ref), (ctxt_ref, glc_ref), (n1t_ref, guc_ref))
     for (left, right), lo, hi in zip(operands, starts, cuts):
@@ -555,7 +587,7 @@
             total = plus(zsum[i], from_far[i])
             from_far[i] = total
             back_copy(i).start()
-            grads_ref[i] = total.astype(F32) / held_n[5, 0:1, 0:1]
+            total_ref[i] = total
 
         @pl.when(at.inner == 0)
         def _():
@@ -565,7 +597,7 @@
         @pl.when(at.inner == 0)
         def _():
             back_copy(i).wait_recv()
-            grads_ref[i] = from_near[i].astype(F32) / held_n[5, 0:1, 0:1]
+            total_ref[i] = from_near[i]
 
         @pl.when(at.inner == 1)
         def _():
@@ -579,7 +611,7 @@
         shift1[...] = jnp.zeros_like(shift1)
         bqkv[...] = jnp.zeros_like(bqkv)
 
-    @pl.when(tick < row_ticks)
+    @pl.when((tick >= 1) & (tick <= row_ticks))
     def _():
         out_ref[...] = (base_ref[...] + nn(ctx_ref[...], wout_ref[...])).astype(BF16)
         g1 = nt(gu_ref[0], wqkv_ref[:, :width])
@@ -593,7 +625,7 @@
         shift1[...] += jnp.sum(g1, axis=0, keepdims=True)
         for j in range(3):
             bqkv[:, j * width : (j + 1) * width] += jnp.sum(gu_ref[j].astype(F32), axis=0, keepdims=True)
-        t = g1 * g1_ref[...] + t2_ref[...]
+        t = g1 * g1_ref[...].reshape(1, -1) + t2_ref[...]
         dx = r * (t - jnp.mean(t, axis=1, keepdims=True) - n * jnp.mean(t * n, axis=1, keepdims=True))
         ig_ref[...] = (gl_ref[...].astype(F32) + dx).astype(BF16)
 
@@ -603,9 +635,7 @@
     when(LAGS["mid"], far_step)
     when(LAGS["back"], back_step)
 
-    Everywhere(at, held_n, come_n, n_s, n_r).hop(tick)
-
-    @pl.when(tick == row_ticks)
+    @pl.when(tick == row_ticks + 1)
     def _():
         held_v[0] = jnp.zeros(held_v.shape[1:], F32)
         held_v[0, 0:1, :] = bup_ref[...]
@@ -615,12 +645,14 @@
         held_v[0, 2:3, width : 2 * width] = shift1[...]
         held_v[0, 2:3, 2 * width : 3 * width] = gain2_ref[...]
         held_v[0, 2:3, 3 * width :] = shift2_ref[...]
-
-    Everywhere(at, held_v, come_v, v_s, v_r).hop(tick - row_ticks)
-
-    @pl.when(tick == row_ticks + 6)
-    def _():
-        vec_ref[...] = held_v[5] / held_n[5, 0:1, 0:1]
+        held_v[0, 3:4, :] = jnp.full((1, held_v.shape[2]), count_ref[0].astype(F32), F32)
+
+    begin = row_ticks + 1
+    Everywhere(at, held_v, come_v, v_s, v_r).hop(tick - begin, SPACING)
+
+    @pl.when(tick == begin + 6 * SPACING)
+    def _():
+        vec_ref[...] = held_v[5]
 
 
 def reduce(count, n1t, n2t, glt, ctxt, gh, act, gl, gu, x, base, t2, ctx, wqkv, wout, g1, gain2, shift2, bup, bout):
@@ -634,13 +666,14 @@
     rows = 128
     row_ticks = length // rows
     ticks = chunks + LAGS["back"]
+    assert ticks > row_ticks + 1 + 6 * SPACING
     ring = 8
 
     def cols(array_chunks, begin):
         return pl.BlockSpec((length, CHUNK), lambda t: (0, jnp.clip(t - begin, 0, array_chunks - 1)))
 
     def row(cols):
-        return pl.BlockSpec((rows, cols), lambda t: (jnp.minimum(t, row_ticks - 1), 0))
+        return pl.BlockSpec((rows, cols), lambda t: (jnp.clip(t - 1, 0, row_ticks - 1), 0))
 
     def whole(a):
         return pl.BlockSpec(a.shape, lambda t: (0,) * a.ndim, pipeline_mode=pl.Buffered(1))
@@ -649,24 +682,25 @@
         j = jnp.clip(t - cuts[2], 0, counts[3] - 1)
         return (j // per, 0, j % per)
 
-    g1 = g1.reshape(1, -1)
+    loaded = (n2t, wout, wqkv, glt, ctxt, n1t)
     s = jax.ShapeDtypeStruct
     dma = pltpu.SemaphoreType.DMA
     hops = Everywhere.HOPS
     return pl.pallas_call(
         functools.partial(reduce_body, cuts=cuts, row_ticks=row_ticks),
         grid=(ticks,),
-        in_specs=[pl.BlockSpec(memory_space=pltpu.SMEM), whole(n1t), whole(n2t), whole(glt), whole(ctxt),
+        in_specs=[pl.BlockSpec(memory_space=pltpu.SMEM),
                   cols(counts[0], 0), cols(counts[1], cuts[0]), cols(counts[2], cuts[1]),
                   pl.BlockSpec((1, length, CHUNK), gu_cols),
                   row(width), row(width), row(width), row(width), row(width),
-                  pl.BlockSpec((3, rows, width), lambda t: (0, jnp.minimum(t, row_ticks - 1), 0)),
-                  whole(wqkv), whole(wout), whole(g1), whole(gain2), whole(shift2), whole(bup), whole(bout)],
+                  pl.BlockSpec((3, rows, width), lambda t: (0, jnp.clip(t - 1, 0, row_ticks - 1), 0)),
+                  whole(g1), whole(gain2), whole(shift2), whole(bup), whole(bout)] + [pl.BlockSpec(memory_space=pl.ANY)] * 6,
         out_specs=[row(width), row(width),
                    pl.BlockSpec((chunks, block, CHUNK), lambda t: (0, 0, 0), pipeline_mode=pl.Buffered(1)),
                    pl.BlockSpec((8, ff), lambda t: (0, 0), pipeline_mode=pl.Buffered(1))],
-        out_shape=[s((length, width), BF16), s((length, width), BF16), s((chunks, block, CHUNK), F32), s((8, ff), F32)],
-        scratch_shapes=[
+        out_shape=[s((length, width), BF16), s((length, width), BF16), s((chunks, block, CHUNK), BF16), s((8, ff), F32)],
+        scratch_shapes=[pltpu.VMEM(a.shape, BF16) for a in loaded] + [
+            dma((len(loaded),)),
             pltpu.VMEM((ring, 2, 2, 2, block, CHUNK), BF16),
             pltpu.VMEM((chunks, 2, 2, block, CHUNK), BF16),
             pltpu.VMEM((chunks, 2, block, CHUNK), BF16),
@@ -675,14 +709,62 @@
             pltpu.VMEM((chunks, block, CHUNK), BF16),
             pltpu.VMEM((chunks, block, CHUNK), BF16),
         ] + [dma((chunks,))] * 10 + [
-            pltpu.VMEM((hops, 8, 128), F32), pltpu.VMEM((hops, 8, 128), F32),
             pltpu.VMEM((hops, 8, ff), F32), pltpu.VMEM((hops, 8, ff), F32),
-            dma((hops,)), dma((hops,)), dma((hops,)), dma((hops,)),
+            dma((hops,)), dma((hops,)),
             pltpu.VMEM((1, width), F32), pltpu.VMEM((1, width), F32), pltpu.VMEM((1, 3 * width), F32),
         ],
         compiler_params=pltpu.CompilerParams(vmem_limit_bytes=60 * 2**20, collective_id=0, has_side_effects=True),
         name="reduce",
-    )(count, n1t, n2t, glt, ctxt, gh, act, gl, gu, x, gl, base, t2, ctx, gu, wqkv, wout, g1, gain2, shift2, bup, bout)
+    )(count, gh, act, gl, gu, x, gl, base, t2, ctx, gu, g1, gain2, shift2, bup, bout, *loaded)
+
+
+def finish_body(out_hbm, ig_hbm, total_ref, vec_ref, out_to, ig_to, up_ref, down_ref, low_ref, qkv_ref,
+                gain1_ref, shift1_ref, bqkv_ref, bout_ref, gain2_ref, shift2_ref, bup_ref, bdown_ref, sem):
+    copies = [pltpu.make_async_copy(out_hbm, out_to, sem.at[0]), pltpu.make_async_copy(ig_hbm, ig_to, sem.at[1])]
+    for copy in copies:
+        copy.start()
+    width, ff = gain1_ref.shape[0], bup_ref.shape[0]
+    factor = 1.0 / vec_ref[3:4, 0:1]
+    n_up, n_low = ff // CHUNK, width // CHUNK
+    for i in range(total_ref.shape[0]):
+        grad = total_ref[i].astype(F32) * factor
+        if i < n_up:
+            up_ref[:, i * CHUNK : (i + 1) * CHUNK] = grad
+        elif i < 2 * n_up:
+            down_ref[:, (i - n_up) * CHUNK : (i - n_up + 1) * CHUNK] = grad
+        elif i < 2 * n_up + n_low:
+            j = i - 2 * n_up
+            low_ref[:, j * CHUNK : (j + 1) * CHUNK] = grad
+        else:
+            j = i - 2 * n_up - n_low
+            qkv_ref[:, j * CHUNK : (j + 1) * CHUNK] = grad
+    vec = vec_ref[...] * factor
+    bup_ref[...] = vec[0]
+    bqkv_ref[...] = vec[1, : 3 * width]
+    bout_ref[...] = vec[1, 3 * width :]
+    bdown_ref[...] = vec[1, 3 * width :]
+    for j, ref in enumerate((gain1_ref, shift1_ref, gain2_ref, shift2_ref)):
+        ref[...] = vec[2, j * width : (j + 1) * width]
+    for copy in copies:
+        copy.wait()
+
+
+def finish(out, ig, total, vec):
+    length, width = out.shape
+    block, ff = total.shape[1], vec.shape[1]
+    s = jax.ShapeDtypeStruct
+    hbm, vmem = pl.BlockSpec(memory_space=pltpu.HBM), pl.BlockSpec(memory_space=pltpu.VMEM)
+    vectors = (width, width, 3 * width, width, width, width, ff, width)
+    return pl.pallas_call(
+        finish_body,
+        in_specs=[hbm, hbm, vmem, vmem],
+        out_specs=[hbm, hbm] + [vmem] * 12,
+        out_shape=[s(out.shape, BF16), s(ig.shape, BF16), s((block, ff), F32), s((block, ff), F32), s((block, width), F32),
+                   s((block, 3 * width), F32)] + [s((n,), F32) for n in vectors],
+        scratch_shapes=[pltpu.SemaphoreType.DMA((2,))],
+        compiler_params=pltpu.CompilerParams(vmem_limit_bytes=40 * 2**20),
+        name="finish",
+    )(out, ig, total, vec)
 
 
 def by_collectives(count, n1t, n2t, glt, ctxt, gh, act, gl, gu, x, base, t2, ctx, wqkv, wout, g1, gain2, shift2, bup, bout):
@@ -698,38 +780,30 @@
     dx = r * (t - jnp.mean(t, axis=1, keepdims=True) - n * jnp.mean(t * n, axis=1, keepdims=True))
     input_grad = (gl.astype(F32) + dx).astype(BF16)
     packed = jnp.concatenate([bup[0], jnp.sum(flat, axis=0, dtype=F32), bout[0], jnp.sum(grad_one * n, axis=0),
-                              jnp.sum(grad_one, axis=0), gain2[0], shift2[0], count.astype(F32)])
+                              jnp.sum(grad_one, axis=0), gain2[0], shift2[0],
+                              jnp.full(bup.shape[1], count[0].astype(F32))])
     packed = lax.psum(packed, ("dp", "rows"))
     part = jnp.concatenate([nn(n2t, gh), nn(glt, act), nn(ctxt, gl), nn(n1t, flat)], axis=1).astype(BF16)
     grads = lax.psum(lax.psum_scatter(part, "dp", scatter_dimension=0, tiled=True), "rows")
-    return out, input_grad, grads.astype(F32) / packed[-1], (packed[:-1] / packed[-1]).reshape(3, -1)
-
-
-def by_kernel(*operands):
-    out, input_grad, grads, vec = reduce(*operands)
-    grads = jnp.swapaxes(grads, 0, 1).reshape(grads.shape[1], -1)
-    return out, input_grad, grads, vec
+    total = jnp.swapaxes(grads.reshape(grads.shape[0], -1, CHUNK), 0, 1)
+    return out, input_grad, total, packed.reshape(4, -1)
 
 
 def shards(tokens, segment_ids, true_counts, regroup, cotangent, ln1_gain, ln1_bias, qkv_weight, qkv_bias, out_weight,
            out_bias, ln2_gain, ln2_bias, up_weight, up_bias, down_weight, down_bias):
     length, width = cotangent.shape
     ff = up_weight.shape[1]
-    want = jnp.full((8, 128), regroup[0] % lax.axis_size("rows"), jnp.int32)
     cosine, sine = (jnp.asarray(t) for t in rotary_tables(length))
     (arrived, q, k, v, gc, n1t, n2t, glt, gl, act, gh, base, t2, gain2, shift2, bias_up, bias_out) = front(
-        true_counts, want, tokens, cotangent, cosine, sine, ln1_gain, ln1_bias, qkv_weight, qkv_bias, out_weight, out_bias,
+        true_counts, regroup, tokens, cotangent, cosine, sine, ln1_gain, ln1_bias, qkv_weight, qkv_bias, out_weight, out_bias,
         ln2_gain, ln2_bias, up_weight, up_bias, down_weight, down_bias)
-    ctx, ctxt, gu = attention(q, k, v, gc, segment_ids, cosine, sine, rows=256)
-    last = by_kernel if (lax.axis_size("dp"), lax.axis_size("rows")) == (8, 4) else by_collectives
-    out, input_grad, grads, vec = last(true_counts, n1t, n2t, glt, ctxt, gh, act, gl, gu, arrived, base, t2, ctx, qkv_weight,
+    ctx, ctxt, gu = attention(q, k, v, gc, segment_ids, cosine, sine)
+    last = reduce if (lax.axis_size("dp"), lax.axis_size("rows")) == (8, 4) else by_collectives
+    out, input_grad, total, vec = last(true_counts, n1t, n2t, glt, ctxt, gh, act, gl, gu, arrived, base, t2, ctx, qkv_weight,
                                        out_weight, ln1_gain, gain2, shift2, bias_up, bias_out)
-    up, down = grads[:, :ff], grads[:, ff : 2 * ff].T
-    low, qkv = grads[:, 2 * ff : 2 * ff + width], grads[:, 2 * ff + width :]
-    gains = vec[2].reshape(4, width)
-    bias_out = vec[1, 3 * width :]
-    return (out, input_grad, gains[0], gains[1], qkv, vec[1, : 3 * width], low, bias_out, gains[2], gains[3], up, vec[0], down,
-            bias_out)
+    (out, input_grad, up, down, low, qkv, gain1, shift1, bias_qkv, bias_out, gain2, shift2, bias_up, bias_down) = finish(
+        out, input_grad, total, vec)
+    return (out, input_grad, gain1, shift1, qkv, bias_qkv, low, bias_out, gain2, shift2, up, bias_up, down.T, bias_down)
 
 
 def solution(mesh):

time: 270 us -> 235 us (0.87)
  local copies, waits for them, and re-layouts: 25.7 us -> 5.18 us
  Pallas kernels: 238 us -> 225 us
    reshape x9 -> x0, local copies, waits for them, and re-layouts: 12.9 us -> none  [the longest x7 8.91 us: front(): v.reshape(1, -1)]
    pallas_call x1, Pallas kernels: 111 us -> 98.2 us  [reduce(): pl.pallas_call(functools.partial(reduce_body, cuts=cuts, row_ticks=row_ti...]
    slice x6 -> x0, local copies, waits for them, and re-layouts: 6.95 us -> none  [the longest x2 1.7 us: shards(): low, qkv = (grads[:, 2 * ff:2 * ff + width], grads[:, 2 * ff + width:])]
    pallas_call x1 -> x2, Pallas kernels: 40.4 us -> 39.8 us  [the longest x1 36.3 us: attention(): pl.pallas_call(functools.partial(attention_body, rows=rows), grid=(pairs...]
where the time goes in v4:
time: 235 us; the launch traced here: 232 us
  Pallas kernels  225 us (96%)
  local copies, waits for them, and re-layouts  5.18 us (2%)
    pallas_call x1, Pallas kernels, reduce(): pl.pallas_call(functools.partial(reduce_body, cuts=cuts, row_ticks=row_ti...  98.2 us
    pallas_call x1, Pallas kernels, front(): pl.pallas_call(functools.partial(front_body, tile=tile), grid=(chunks,),...  86.8 us
    pallas_call x1, Pallas kernels, attention(): pl.pallas_call(functools.partial(attention_body, rows=rows), grid=(pairs...  36.3 us
    unnamed x8, local copies, waits for them, and re-layouts  5.18 us

profile of v4, /device:TPU:0, one launch (start us, length us, event | category | flops | bytes accessed | tf_op | source)
XLA Modules:
  0.0 232.1 jit_solution(16580839236441567601)
XLA Ops:
  1.9 86.8 %front.1 = (bf16[1024,768]{1,0:T(8,128)(2,1)}, bf16[6,1024,128]{2,1,0:T(8,128)(2,1)}, bf16[6,1024,128]{2,1,0:T(8,128)(2,1)}, bf16[6,1024,128]{2,1,0:T(8,128)(2,1...) custom-call(s32[1]{0:T(128)S(6)} %copy.33.count_ref, ...), custom_call_target="tpu_custom_call" | custom-call | tf_op jit(solution)/shard_map/front/pallas_call | solution.py:242
  88.8 36.3 %attention.1 = (bf16[1024,768]{1,0:T(8,128)(2,1)}, bf16[768,1024]{1,0:T(8,128)(2,1)}, bf16[3,1024,768]{2,1,0:T(8,128)(2,1)}) custom-call(bf16[6,1024,128]{2,1,0:T(8,128)(2,1)} %get-tuple-element.55.q_ref, bf16[6,1024,128]{2,1,0:T(8,128)(2,1)} %get-tuple-element.56.k_ref, bf16[6,1024,128]{2,1,0:T(8,128)(2,1)} %get-tuple-element.57.v_ref, ...), custom_call_target="tpu_custom_call" | custom-call | tf_op jit(solution)/shard_map/attention/pallas_call | solution.py:349
  125.1 98.2 %reduce.1 = (bf16[1024,768]{1,0:T(8,128)(2,1)}, bf16[1024,768]{1,0:T(8,128)(2,1)}, bf16[24,96,384]{2,1,0:T(8,128)(2,1)}, f32[8,3072]{1,0:T(8,128)}) custom-call(s32[1]{0:T(128)S(6)} %copy.33.count_ref, bf16[1024,3072]{1,0:T(8,128)(2,1)} %get-tuple-element.52.gh_ref, bf16[1024,3072]{1,0:T(8,128)(2,1)} %get-tuple-element.53.act_ref, ...), custom_call_target="tpu_custom_call" | custom-call | tf_op jit(solution)/shard_map/reduce/pallas_call | solution.py:689
  223.3 0.0 copy-start
  223.3 1.5 copy-done
  224.7 0.0 copy-start.1
  224.7 1.4 copy-done.1
  226.2 0.0 copy-start.2
  226.2 1.4 copy-done.2
  227.6 0.0 copy-start.3
  227.6 0.9 copy-done.3
  228.5 3.5 %finish.1 = (bf16[1024,768]{1,0:T(8,128)(2,1)}, bf16[1024,768]{1,0:T(8,128)(2,1)}, f32[96,3072]{1,0:T(8,128)}, f32[96,3072]{1,0:T(8,128)}, f32[96,768]{1,0:T(8,1...) custom-call(bf16[1024,768]{1,0:T(8,128)(2,1)S(1)} %copy-done.1, ...), custom_call_target="tpu_custom_call" | custom-call | tf_op jit(solution)/shard_map/finish/pallas_call | solution.py:758
Async XLA Ops:
  223.3 1.5 copy-start
  224.7 1.4 copy-start.1
  226.2 1.4 copy-start.2
  227.6 0.9 copy-start.3

commit v5 on v4

--- a/solution.py
+++ b/solution.py
@@ -64,7 +64,7 @@
 
 def front_body(count_ref, want_ref, own_ref, cot_ref, cos_ref, sin_ref, g1_vec, b1_vec, bqkv_vec, bout_vec, g2_vec, b2_vec,
                bup_vec, bdown_vec, wqkv_hbm, wout_hbm, wup_hbm, wdown_hbm,
-               x_ref, q_ref, k_ref, v_ref, gc_ref, n1t_ref, n2t_ref, glt_ref, gl_ref, act_ref, gh_ref, base_ref, t2_ref,
+               x_ref, q_ref, k_ref, v_ref, gc_ref, n1t_ref, n2t_ref, glt_ref, gl_ref, mlp_ref, base_ref, t2_ref,
                gain2_ref, shift2_ref, bup_out, bout_out,
                wqkv_ref, wout_ref, wup_ref, wdown_ref, wants, from_near, from_half, to_inner, to_end,
                g1_ref, b1_ref, bqkv_ref, bout_ref, g2_ref, b2_ref, bup_ref, bdown_ref, w_sem, want_send, want_recv, near_send, near_recv, inner_send, end_send, half_recv, *, tile):
@@ -151,7 +151,8 @@
     place = step * rows + lax.broadcasted_iota(jnp.int32, (rows, 1), 0)
     gl = jnp.where(place < count_ref[0], cot_ref[...].astype(F32), 0.0)
     gl16 = gl.astype(BF16)
-    gl_ref[...] = gl16
+    for j in range(gl_ref.shape[0]):
+        gl_ref[j] = gl16[:, j * PIECE : (j + 1) * PIECE]
     glt_ref[...] = gl16.T
     bout_out[...] += jnp.sum(gl, axis=0, keepdims=True)
     for p in range(pairs):
@@ -193,8 +194,8 @@
         a16 = a.astype(BF16)
         gh = ga * slope
         gh16 = gh.astype(BF16)
-        act_ref[:, cols] = a16
-        gh_ref[:, cols] = gh16
+        mlp_ref[:, cols] = gh16
+        mlp_ref[:, ff + f : ff + f + tile] = a16
         bup_out[:, cols] += jnp.sum(gh16.astype(F32), axis=0, keepdims=True)
         mlp = mlp + nn(a16, wdown_ref[cols, :])
         grad_two = grad_two + nt(gh16, wup_ref[:, cols])
@@ -244,10 +245,11 @@
         grid=(chunks,),
         in_specs=[pl.BlockSpec(memory_space=pltpu.SMEM), pl.BlockSpec(memory_space=pltpu.SMEM), whole(own), row(width), row(PAIR), row(PAIR)]
         + [whole(a) for a in vectors] + [pl.BlockSpec(memory_space=pl.ANY)] * 4,
-        out_specs=[row(width)] + [heads] * 4 + [down] * 3 + [row(width)] + [row(ff)] * 2 + [row(width)] * 2
+        out_specs=[row(width)] + [heads] * 4 + [down] * 3
+        + [pl.BlockSpec((width // PIECE, rows, PIECE), lambda i: (0, i, 0)), row(2 * ff)] + [row(width)] * 2
         + [vec(width), vec(width), vec(ff), vec(width)],
         out_shape=[s((length, width), BF16)] + [s((pairs, length, PAIR), BF16)] * 4 + [s((width, length), BF16)] * 3
-        + [s((length, width), BF16)] + [s((length, ff), BF16)] * 2
+        + [s((width // PIECE, length, PIECE), BF16), s((length, 2 * ff), BF16)]
         + [s((length, width), F32)] * 2 + [s((1, width), F32), s((1, width), F32), s((1, ff), F32), s((1, width), F32)],
         scratch_shapes=[pltpu.VMEM(w.shape, BF16) for w in weights]
         + [pltpu.VMEM((4, 8, 128), jnp.int32)] + [pltpu.VMEM((length, width), BF16)] * 4
@@ -360,7 +362,9 @@
     )(q, k, v, gc, segment, cosine, sine)
 
 
-CHUNK = 384
+CHUNK = 512
+PIECE = 256
+GROUP = 2
 
 
 class Line:
@@ -439,31 +443,43 @@
                 self.copy(5, at.near).wait_recv()
                 self.held[5] = self.come[5]
 
-
-LAGS = dict(core=1, first=4, second=7, z=9, mid=11, back=13)
-SPACING = 3
-
-
-def reduce_body(count_ref, gh_ref, act_ref, glc_ref, guc_ref, x_ref, gl_ref, base_ref, t2_ref, ctx_ref, gu_ref, g1_ref,
-                gain2_ref, shift2_ref, bup_ref, bout_ref, n2t_hbm, wout_hbm, wqkv_hbm, glt_hbm, ctxt_hbm, n1t_hbm,
-                out_ref, ig_ref, total_ref, vec_ref,
-                n2t_ref, wout_ref, wqkv_ref, glt_ref, ctxt_ref, n1t_ref, load_sem, part, from_core, from_first, from_second, zsum, from_near, from_far,
-                c_send, c_recv, f_send, f_recv, s_send, s_recv, n_send, n_recv, m_send, m_recv,
-                held_v, come_v, v_s, v_r, gain1, shift1, bqkv, *, cuts, row_ticks):
+LAGS = dict(core=1, first=3, second=5, z=7, mid=9, back=10)
+RING, CORE_RING, LINK_RING = 7, 6, 8
+
+
+def chunk_columns(i, groups, per_group):
+    period = per_group + 1
+    if i < groups * period and i % period < per_group:
+        return "mlp", per_group * (i // period) + i % period
+    j = i // period if i < groups * period else i - groups * per_group
+    return "rest", 2 * j, 2 * j + 1
+
+
+def back_body(count_ref, seg_ref, mlp_ref, q_ref, k_ref, v_ref, gc_ref, x_ref, base_ref, t2_ref, cos_ref, sin_ref, g1_ref,
+              gain2_ref, shift2_ref, bup_ref, bout_ref, n2t_hbm, glt_hbm, n1t_hbm, gl_hbm, wout_hbm, wqkv_hbm,
+              out_ref, ig_ref, total_ref, vec_ref,
+              left_mlp, left_rest, rhs, wout_ref, wqkv_ref, load_sem, ctx, dk_acc, dv_acc, begin_ref,
+              part, from_core, from_first, from_second, from_near, from_far,
+              c_send, c_recv, f_send, f_recv, s_send, s_recv, n_send, n_recv, m_send, m_recv,
+              held_v, come_v, v_s, v_r, gain1, shift1, bqkv, *, rows, row_ticks):
     tick = pl.program_id(0)
     at = Line()
-    chunks = cuts[-1]
-    ring = part.shape[0]
-    width = wout_ref.shape[0]
-    block = width // 8
-
-    loads = [pltpu.make_async_copy(src, dst, load_sem.at[j]) for j, (src, dst) in enumerate(
-        ((n2t_hbm, n2t_ref), (wout_hbm, wout_ref), (wqkv_hbm, wqkv_ref), (glt_hbm, glt_ref), (ctxt_hbm, ctxt_ref),
-         (n1t_hbm, n1t_ref)))]
+    chunks, block = total_ref.shape[0], total_ref.shape[1]
+    length, width = seg_ref.shape[0], wout_ref.shape[0]
+    groups = width // PIECE
+    per_group = length // rows
+    period = per_group + 1
+    busy = groups * period
+    g = jnp.minimum(tick // period, groups - 1)
+    spot = tick % period
+    first_need = (pltpu.make_async_copy(n2t_hbm, left_mlp.at[0], load_sem.at[0]),)
+    later_need = [pltpu.make_async_copy(src, dst, load_sem.at[1 + j]) for j, (src, dst) in enumerate(
+        ((glt_hbm, left_mlp.at[1]), (n1t_hbm, left_rest.at[0]), (gl_hbm, rhs.at[pl.ds(3 * groups, groups)]),
+         (wout_hbm, wout_ref), (wqkv_hbm, wqkv_ref)))]
 
     @pl.when(tick == 0)
     def _():
-        loads[0].start()
+        first_need[0].start()
         barrier = pltpu.get_barrier_semaphore()
         for to in (at.over_core, at.over_x, at.over_y, at.near):
             pl.semaphore_signal(barrier, inc=1, device_id=to, device_id_type=MESH)
@@ -477,8 +493,22 @@
         def _():
             pl.semaphore_wait(barrier, 4)
 
-        for load in loads[1:]:
+        for load in later_need:
             load.start()
+        wide = jnp.broadcast_to(seg_ref[...].reshape(1, -1), (8, length)).astype(F32)
+        tall = wide.T[:, :1]
+        for b in range(0, length, PAIR):
+            earlier = jnp.where(wide[:1] < tall[b : b + PAIR], 1.0, 0.0)
+            begin_ref[b : b + PAIR, :] = jnp.sum(earlier, axis=1, keepdims=True).astype(jnp.int32)
+        gain1[...] = jnp.zeros_like(gain1)
+        shift1[...] = jnp.zeros_like(shift1)
+        bqkv[...] = jnp.zeros_like(bqkv)
+        first_need[0].wait()
+
+    @pl.when(tick == 1)
+    def _():
+        for load in later_need:
+            load.wait()
 
     def places(i):
         even = 1 - i % 2
@@ -486,61 +516,56 @@
         s = at.y * even + at.x * (1 - even)
         first = (at.d + even * (2 - 4 * at.x) + (1 - even) * (4 - 8 * at.y), at.z)
         second = (at.d + even * (4 - 8 * at.y) + (1 - even) * (2 - 4 * at.x), at.z)
-        return even, f, s, first, second, i % ring
+        return f, s, first, second, i % RING
 
     def core_copy(i):
-        slot = i % ring
-        return remote(part.at[slot, 1 - at.core], from_core.at[i], c_send.at[i], c_recv.at[i], at.over_core)
+        return remote(part.at[i % RING, 1 - at.core], from_core.at[i % CORE_RING], c_send.at[i], c_recv.at[i], at.over_core)
 
     def first_copy(i):
-        even, f, s, first, second, slot = places(i)
-        return remote(part.at[slot, at.core, 1 - f], from_first.at[i], f_send.at[i], f_recv.at[i], first)
+        f, s, first, second, slot = places(i)
+        return remote(part.at[slot, at.core, 1 - f], from_first.at[i % LINK_RING], f_send.at[i], f_recv.at[i], first)
 
     def second_copy(i):
-        even, f, s, first, second, slot = places(i)
-        return remote(part.at[slot, at.core, f, 1 - s], from_second.at[i], s_send.at[i], s_recv.at[i], second)
+        f, s, first, second, slot = places(i)
+        return remote(part.at[slot, at.core, f, 1 - s], from_second.at[i % LINK_RING], s_send.at[i], s_recv.at[i], second)
 
     def out_copy(i):
-        return remote(zsum.at[i], from_near.at[i], n_send.at[i], n_recv.at[i], at.near)
+        return remote(total_ref.at[i], from_near.at[i % LINK_RING], n_send.at[i], n_recv.at[i], at.near)
 
     def far_copy(i):
-        return remote(zsum.at[i], from_far.at[i], m_send.at[i], m_recv.at[i], at.far)
-
-    def back_copy(i):
-        return remote(from_far.at[i], from_near.at[i], n_send.at[i], n_recv.at[i], at.near)
+        return remote(total_ref.at[i], from_far.at[i % LINK_RING], m_send.at[i], m_recv.at[i], at.far)
 
     def plus(a, b):
         return (a.astype(F32) + b.astype(F32)).astype(BF16)
 
-    def product(left, right):
+    def put(h, half, cols, rows_of):
         even = 1 - tick % 2
-        slot = tick % ring
-        half = width // 2
+        for j in range(4):
+            d = h * 4 + j
+            c, x, y = d % 2, (d // 2) % 2, d // 4
+            a = x * even + y * (1 - even)
+            b = y * even + x * (1 - even)
+            part[tick % RING, c, a, b, :, cols] = rows_of[j * block : (j + 1) * block].astype(BF16)
+
+    half = width // 2
+    is_mlp = (tick < busy) & (spot < per_group)
+
+    @pl.when(is_mlp)
+    def _():
+        left = (per_group * g + spot) // (groups * per_group // 2)
         for h in range(2):
-            rows = nn(left[h * half : (h + 1) * half, :], right)
-            for j in range(4):
-                d = h * 4 + j
-                c, x, y = d % 2, (d // 2) % 2, d // 4
-                a = x * even + y * (1 - even)
-                b = y * even + x * (1 - even)
-                part[slot, c, a, b] = rows[j * block : (j + 1) * block].astype(BF16)
+            put(h, half, slice(0, CHUNK), nn(left_mlp[left, h * half : (h + 1) * half, :], mlp_ref[...]))
         core_copy(tick).start()
 
-    @pl.when(tick == 0)
-    def _():
-        loads[0].wait()
-
-    @pl.when(tick == 1)
-    def _():
-        for load in loads[1:]:
-            load.wait()
-
-    starts = (0,) + cuts[:-1]
-    operands = ((n2t_ref, gh_ref), (glt_ref, act_ref), (ctxt_ref, glc_ref), (n1t_ref, guc_ref))
-    for (left, right), lo, hi in zip(operands, starts, cuts):
-        @pl.when((tick >= lo) & (tick < hi))
-        def _():
-            product(left[...], right[0] if right is guc_ref else right[...])
+    @pl.when((tick < chunks) & jnp.logical_not(is_mlp))
+    def _():
+        j = (tick // period) * (1 - tick // busy) + (tick - groups * per_group) * (tick // busy)
+        for e in range(2):
+            s = 2 * j + e
+            for h in range(2):
+                put(h, half, slice(e * PIECE, (e + 1) * PIECE),
+                    nn(left_rest[s // (3 * groups), h * half : (h + 1) * half, :], rhs[s]))
+        core_copy(tick).start()
 
     def when(lag, f):
         i = tick - lag
@@ -550,24 +575,24 @@
             f(i)
 
     def core_step(i):
-        even, f, s, first, second, slot = places(i)
+        f, s, first, second, slot = places(i)
         core_copy(i).wait()
         for a in range(2):
             for b in range(2):
-                part[slot, at.core, a, b] = plus(part[slot, at.core, a, b], from_core[i, a, b])
+                part[slot, at.core, a, b] = plus(part[slot, at.core, a, b], from_core[i % CORE_RING, a, b])
         first_copy(i).start()
 
     def first_step(i):
-        even, f, s, first, second, slot = places(i)
+        f, s, first, second, slot = places(i)
         first_copy(i).wait()
         for b in range(2):
-            part[slot, at.core, f, b] = plus(part[slot, at.core, f, b], from_first[i, b])
+            part[slot, at.core, f, b] = plus(part[slot, at.core, f, b], from_first[i % LINK_RING, b])
         second_copy(i).start()
 
     def second_step(i):
-        even, f, s, first, second, slot = places(i)
+        f, s, first, second, slot = places(i)
         second_copy(i).wait()
-        zsum[i] = plus(part[slot, at.core, f, s], from_second[i])
+        total_ref[i] = plus(part[slot, at.core, f, s], from_second[i % LINK_RING])
 
         @pl.when(at.inner == 0)
         def _():
@@ -577,17 +602,15 @@
         @pl.when(at.inner == 1)
         def _():
             out_copy(i).wait_recv()
-            zsum[i] = plus(zsum[i], from_near[i])
+            total_ref[i] = plus(total_ref[i], from_near[i % LINK_RING])
             far_copy(i).start()
 
     def far_step(i):
         @pl.when(at.inner == 1)
         def _():
             far_copy(i).wait()
-            total = plus(zsum[i], from_far[i])
-            from_far[i] = total
-            back_copy(i).start()
-            total_ref[i] = total
+            total_ref[i] = plus(total_ref[i], from_far[i % LINK_RING])
+            out_copy(i).start()
 
         @pl.when(at.inner == 0)
         def _():
@@ -596,46 +619,107 @@
     def back_step(i):
         @pl.when(at.inner == 0)
         def _():
-            back_copy(i).wait_recv()
-            total_ref[i] = from_near[i]
+            out_copy(i).wait_recv()
+            total_ref[i] = from_near[i % LINK_RING]
 
         @pl.when(at.inner == 1)
         def _():
-            back_copy(i).wait_send()
+            out_copy(i).wait_send()
 
     when(LAGS["core"], core_step)
-
-    @pl.when(tick == 0)
-    def _():
-        gain1[...] = jnp.zeros_like(gain1)
-        shift1[...] = jnp.zeros_like(shift1)
-        bqkv[...] = jnp.zeros_like(bqkv)
-
-    @pl.when((tick >= 1) & (tick <= row_ticks))
-    def _():
-        out_ref[...] = (base_ref[...] + nn(ctx_ref[...], wout_ref[...])).astype(BF16)
-        g1 = nt(gu_ref[0], wqkv_ref[:, :width])
-        g1 = g1 + nt(gu_ref[1], wqkv_ref[:, width : 2 * width])
-        g1 = g1 + nt(gu_ref[2], wqkv_ref[:, 2 * width :])
+    when(LAGS["first"], first_step)
+    when(LAGS["second"], second_step)
+    when(LAGS["z"], near_step)
+    when(LAGS["mid"], far_step)
+    when(LAGS["back"], back_step)
+
+    each = range(GROUP)
+    low = lax.broadcasted_iota(jnp.int32, (rows, PAIR), 1) < HEAD_DIM
+
+    def unit(b):
+        span = (b + 1) * rows
+        mine = slice(b * rows, span)
+
+        def both(ref, h):
+            t = ref[h, mine, :]
+            zero = jnp.zeros_like(t)
+            return jnp.concatenate([jnp.where(low, t, zero), jnp.where(low, zero, t)], axis=0)
+
+        q2 = [both(q_ref, h) for h in each]
+        g2 = [both(gc_ref, h) for h in each]
+        k = [k_ref[h, :span, :] for h in each]
+        v = [v_ref[h, :span, :] for h in each]
+        s_at = lax.broadcasted_iota(jnp.int32, (rows, span), 1)
+        t_at = b * rows + lax.broadcasted_iota(jnp.int32, (rows, span), 0)
+        allowed = (s_at >= begin_ref[mine, :]) & (s_at <= t_at)
+        allowed = jnp.concatenate([allowed, allowed], axis=0)
+        scores = [jnp.where(allowed, nt(q2[h], k[h]), EXCLUDED) for h in each]
+        dp = [nt(g2[h], v[h]) for h in each]
+        e = [jnp.exp(scores[h] - jnp.max(scores[h], axis=1, keepdims=True)) for h in each]
+        p = [e[h] * (1.0 / jnp.sum(e[h], axis=1, keepdims=True)) for h in each]
+        p16 = [p[h].astype(BF16) for h in each]
+        c2 = [nn(p16[h], v[h]) for h in each]
+        for h in each:
+            dv_acc[h, :span, :] += tn(p16[h], g2[h])
+        w = [p[h] * dp[h] for h in each]
+        ds16 = [(w[h] - p[h] * jnp.sum(w[h], axis=1, keepdims=True)).astype(BF16) for h in each]
+        d2 = [nn(ds16[h], k[h]) for h in each]
+        for h in each:
+            dk_acc[h, :span, :] += tn(ds16[h], q2[h])
+        for h in each:
+            cols = slice(h * PAIR, (h + 1) * PAIR)
+            context = jnp.where(low, c2[h][:rows], c2[h][rows:]).astype(BF16)
+            ctx[g, mine, cols] = context
+            left_rest[1, pl.ds(pl.multiple_of(g * PIECE + h * PAIR, PAIR), PAIR), mine] = context.T
+            dq = jnp.where(low, d2[h][:rows], d2[h][rows:]) * (HEAD_DIM ** -0.5)
+            rhs[3 * g, mine, cols] = (dq * cos_ref[mine, :] - turned(dq) * sin_ref[mine, :]).astype(BF16)
+
+    @pl.when((tick < busy) & (spot == 0))
+    def _():
+        dk_acc[...] = jnp.zeros_like(dk_acc)
+        dv_acc[...] = jnp.zeros_like(dv_acc)
+
+    for b in range(per_group):
+        @pl.when((tick < busy) & (spot == b))
+        def _():
+            unit(b)
+
+    @pl.when((tick < busy) & (spot == per_group - 1))
+    def _():
+        for h in each:
+            cols = slice(h * PAIR, (h + 1) * PAIR)
+            dk = dk_acc[h]
+            rhs[3 * g + 1, :, cols] = (dk * cos_ref[...] - turned(dk) * sin_ref[...]).astype(BF16)
+            rhs[3 * g + 2, :, cols] = dv_acc[h].astype(BF16)
+
+    @pl.when((tick >= busy) & (tick < busy + row_ticks))
+    def _():
+        n_rows = x_ref.shape[0]
+        here = pl.ds(pl.multiple_of((tick - busy) * n_rows, n_rows), n_rows)
+        attn = base_ref[...]
+        for j in range(groups):
+            attn = attn + nn(ctx[j, here, :], wout_ref[j * PIECE : (j + 1) * PIECE, :])
+        out_ref[...] = attn.astype(BF16)
+        g1 = jnp.zeros(attn.shape, F32)
+        for s in range(3 * groups):
+            cols = slice((s % 3) * width + (s // 3) * PIECE, (s % 3) * width + (s // 3 + 1) * PIECE)
+            grads = rhs[s, here, :]
+            g1 = g1 + nt(grads, wqkv_ref[:, cols])
+            bqkv[:, cols] += jnp.sum(grads.astype(F32), axis=0, keepdims=True)
         x = x_ref[...].astype(F32)
         centred = x - jnp.mean(x, axis=1, keepdims=True)
         r = lax.rsqrt(jnp.mean(centred * centred, axis=1, keepdims=True) + EPSILON)
         n = centred * r
         gain1[...] += jnp.sum(g1 * n, axis=0, keepdims=True)
         shift1[...] += jnp.sum(g1, axis=0, keepdims=True)
-        for j in range(3):
-            bqkv[:, j * width : (j + 1) * width] += jnp.sum(gu_ref[j].astype(F32), axis=0, keepdims=True)
         t = g1 * g1_ref[...].reshape(1, -1) + t2_ref[...]
         dx = r * (t - jnp.mean(t, axis=1, keepdims=True) - n * jnp.mean(t * n, axis=1, keepdims=True))
-        ig_ref[...] = (gl_ref[...].astype(F32) + dx).astype(BF16)
-
-    when(LAGS["first"], first_step)
-    when(LAGS["second"], second_step)
-    when(LAGS["z"], near_step)
-    when(LAGS["mid"], far_step)
-    when(LAGS["back"], back_step)
-
-    @pl.when(tick == row_ticks + 1)
+        gl = jnp.concatenate([rhs[3 * groups + j, here, :] for j in range(groups)], axis=1)
+        ig_ref[...] = (gl.astype(F32) + dx).astype(BF16)
+
+    begin = busy + row_ticks
+
+    @pl.when(tick == begin)
     def _():
         held_v[0] = jnp.zeros(held_v.shape[1:], F32)
         held_v[0, 0:1, :] = bup_ref[...]
@@ -647,75 +731,75 @@
         held_v[0, 2:3, 3 * width :] = shift2_ref[...]
         held_v[0, 3:4, :] = jnp.full((1, held_v.shape[2]), count_ref[0].astype(F32), F32)
 
-    begin = row_ticks + 1
-    Everywhere(at, held_v, come_v, v_s, v_r).hop(tick - begin, SPACING)
-
-    @pl.when(tick == begin + 6 * SPACING)
+    Everywhere(at, held_v, come_v, v_s, v_r).hop(tick - begin, 1)
+
+    @pl.when(tick == begin + 6)
     def _():
         vec_ref[...] = held_v[5]
 
 
-def reduce(count, n1t, n2t, glt, ctxt, gh, act, gl, gu, x, base, t2, ctx, wqkv, wout, g1, gain2, shift2, bup, bout):
+def back(count, segment, mlp, q, k, v, gc, x, base, t2, cosine, sine, g1, gain2, shift2, bup, bout, n2t, glt, n1t, gl, wout, wqkv,
+         rows=256):
     length, width = x.shape
-    ff = gh.shape[1]
+    ff = bup.shape[1]
     block = width // 8
-    counts = (ff // CHUNK, ff // CHUNK, width // CHUNK, 3 * width // CHUNK)
-    cuts = tuple(int(c) for c in np.cumsum(counts))
-    chunks = cuts[-1]
-    per = width // CHUNK
-    rows = 128
+    groups = width // PIECE
+    chunks = (2 * ff + 4 * width) // CHUNK
+    period = length // rows + 1
+    busy = groups * period
     row_ticks = length // rows
-    ticks = chunks + LAGS["back"]
-    assert ticks > row_ticks + 1 + 6 * SPACING
-    ring = 8
-
-    def cols(array_chunks, begin):
-        return pl.BlockSpec((length, CHUNK), lambda t: (0, jnp.clip(t - begin, 0, array_chunks - 1)))
+    ticks = max(chunks + LAGS["back"], busy + row_ticks + 7)
+    n_mlp = 2 * ff // CHUNK
 
     def row(cols):
-        return pl.BlockSpec((rows, cols), lambda t: (jnp.clip(t - 1, 0, row_ticks - 1), 0))
+        return pl.BlockSpec((rows, cols), lambda t: (jnp.clip(t - busy, 0, row_ticks - 1), 0))
 
     def whole(a):
         return pl.BlockSpec(a.shape, lambda t: (0,) * a.ndim, pipeline_mode=pl.Buffered(1))
 
-    def gu_cols(t):
-        j = jnp.clip(t - cuts[2], 0, counts[3] - 1)
-        return (j // per, 0, j % per)
-
-    loaded = (n2t, wout, wqkv, glt, ctxt, n1t)
+    def mlp_cols(t):
+        return (0, jnp.minimum((period - 1) * (t // period) + jnp.minimum(t % period, period - 2), n_mlp - 1))
+
+    heads = pl.BlockSpec((GROUP, length, PAIR), lambda t: (jnp.minimum(t // period, groups - 1), 0, 0))
     s = jax.ShapeDtypeStruct
     dma = pltpu.SemaphoreType.DMA
     hops = Everywhere.HOPS
+    loaded = (n2t, glt, n1t, gl, wout, wqkv)
     return pl.pallas_call(
-        functools.partial(reduce_body, cuts=cuts, row_ticks=row_ticks),
+        functools.partial(back_body, rows=rows, row_ticks=row_ticks),
         grid=(ticks,),
-        in_specs=[pl.BlockSpec(memory_space=pltpu.SMEM),
-                  cols(counts[0], 0), cols(counts[1], cuts[0]), cols(counts[2], cuts[1]),
-                  pl.BlockSpec((1, length, CHUNK), gu_cols),
-                  row(width), row(width), row(width), row(width), row(width),
-                  pl.BlockSpec((3, rows, width), lambda t: (0, jnp.clip(t - 1, 0, row_ticks - 1), 0)),
-                  whole(g1), whole(gain2), whole(shift2), whole(bup), whole(bout)] + [pl.BlockSpec(memory_space=pl.ANY)] * 6,
+        in_specs=[pl.BlockSpec(memory_space=pltpu.SMEM), whole(segment), pl.BlockSpec((length, CHUNK), mlp_cols)]
+        + [heads] * 4 + [row(width)] * 3
+        + [whole(a) for a in (cosine, sine, g1, gain2, shift2, bup, bout)] + [pl.BlockSpec(memory_space=pl.ANY)] * 6,
         out_specs=[row(width), row(width),
                    pl.BlockSpec((chunks, block, CHUNK), lambda t: (0, 0, 0), pipeline_mode=pl.Buffered(1)),
                    pl.BlockSpec((8, ff), lambda t: (0, 0), pipeline_mode=pl.Buffered(1))],
         out_shape=[s((length, width), BF16), s((length, width), BF16), s((chunks, block, CHUNK), BF16), s((8, ff), F32)],
-        scratch_shapes=[pltpu.VMEM(a.shape, BF16) for a in loaded] + [
-            dma((len(loaded),)),
-            pltpu.VMEM((ring, 2, 2, 2, block, CHUNK), BF16),
-            pltpu.VMEM((chunks, 2, 2, block, CHUNK), BF16),
-            pltpu.VMEM((chunks, 2, block, CHUNK), BF16),
-            pltpu.VMEM((chunks, block, CHUNK), BF16),
-            pltpu.VMEM((chunks, block, CHUNK), BF16),
-            pltpu.VMEM((chunks, block, CHUNK), BF16),
-            pltpu.VMEM((chunks, block, CHUNK), BF16),
+        scratch_shapes=[
+            pltpu.VMEM((2, width, length), BF16),
+            pltpu.VMEM((2, width, length), BF16),
+            pltpu.VMEM((4 * groups, length, PIECE), BF16),
+            pltpu.VMEM(wout.shape, BF16),
+            pltpu.VMEM(wqkv.shape, BF16),
+            dma((6,)),
+            pltpu.VMEM((groups, length, PIECE), BF16),
+            pltpu.VMEM((GROUP, length, PAIR), F32),
+            pltpu.VMEM((GROUP, length, PAIR), F32),
+            pltpu.VMEM((length, 1), jnp.int32),
+            pltpu.VMEM((RING, 2, 2, 2, block, CHUNK), BF16),
+            pltpu.VMEM((CORE_RING, 2, 2, block, CHUNK), BF16),
+            pltpu.VMEM((LINK_RING, 2, block, CHUNK), BF16),
+            pltpu.VMEM((LINK_RING, block, CHUNK), BF16),
+            pltpu.VMEM((LINK_RING, block, CHUNK), BF16),
+            pltpu.VMEM((LINK_RING, block, CHUNK), BF16),
         ] + [dma((chunks,))] * 10 + [
             pltpu.VMEM((hops, 8, ff), F32), pltpu.VMEM((hops, 8, ff), F32),
             dma((hops,)), dma((hops,)),
             pltpu.VMEM((1, width), F32), pltpu.VMEM((1, width), F32), pltpu.VMEM((1, 3 * width), F32),
         ],
         compiler_params=pltpu.CompilerParams(vmem_limit_bytes=60 * 2**20, collective_id=0, has_side_effects=True),
-        name="reduce",
-    )(count, gh, act, gl, gu, x, gl, base, t2, ctx, gu, g1, gain2, shift2, bup, bout, *loaded)
+        name="back",
+    )(count, segment, mlp, q, k, v, gc, x, base, t2, cosine, sine, g1, gain2, shift2, bup, bout, *loaded)
 
 
 def finish_body(out_hbm, ig_hbm, total_ref, vec_ref, out_to, ig_to, up_ref, down_ref, low_ref, qkv_ref,
@@ -725,19 +809,18 @@
         copy.start()
     width, ff = gain1_ref.shape[0], bup_ref.shape[0]
     factor = 1.0 / vec_ref[3:4, 0:1]
-    n_up, n_low = ff // CHUNK, width // CHUNK
+    groups = width // PIECE
+    n_up = ff // CHUNK
     for i in range(total_ref.shape[0]):
         grad = total_ref[i].astype(F32) * factor
-        if i < n_up:
-            up_ref[:, i * CHUNK : (i + 1) * CHUNK] = grad
-        elif i < 2 * n_up:
-            down_ref[:, (i - n_up) * CHUNK : (i - n_up + 1) * CHUNK] = grad
-        elif i < 2 * n_up + n_low:
-            j = i - 2 * n_up
-            low_ref[:, j * CHUNK : (j + 1) * CHUNK] = grad
-        else:
-            j = i - 2 * n_up - n_low
-            qkv_ref[:, j * CHUNK : (j + 1) * CHUNK] = grad
+        kind, *what = chunk_columns(i, groups, 2 * n_up // groups)
+        if kind == "mlp":
+            ref, j = (up_ref, what[0]) if what[0] < n_up else (down_ref, what[0] - n_up)
+            ref[:, j * CHUNK : (j + 1) * CHUNK] = grad
+            continue
+        for e, s in enumerate(what):
+            ref, col = (qkv_ref, (s % 3) * width + (s // 3) * PIECE) if s < 3 * groups else (low_ref, (s - 3 * groups) * PIECE)
+            ref[:, col : col + PIECE] = grad[:, e * PIECE : (e + 1) * PIECE]
     vec = vec_ref[...] * factor
     bup_ref[...] = vec[0]
     bqkv_ref[...] = vec[1, : 3 * width]
@@ -767,9 +850,12 @@
     )(out, ig, total, vec)
 
 
-def by_collectives(count, n1t, n2t, glt, ctxt, gh, act, gl, gu, x, base, t2, ctx, wqkv, wout, g1, gain2, shift2, bup, bout):
-    width = x.shape[1]
+def by_collectives(count, segment, mlp, q, k, v, gc, x, base, t2, cosine, sine, g1, gain2, shift2, bup, bout, n2t, glt, n1t, gl,
+                   wout, wqkv):
+    width, ff = x.shape[1], bup.shape[1]
+    ctx, ctxt, gu = attention(q, k, v, gc, segment, cosine, sine)
     flat = jnp.concatenate([gu[0], gu[1], gu[2]], axis=1)
+    low = jnp.concatenate(list(gl), axis=1)
     out = (base + nn(ctx, wout)).astype(BF16)
     grad_one = nt(flat, wqkv)
     x = x.astype(F32)
@@ -778,15 +864,21 @@
     n = centred * r
     t = grad_one * g1 + t2
     dx = r * (t - jnp.mean(t, axis=1, keepdims=True) - n * jnp.mean(t * n, axis=1, keepdims=True))
-    input_grad = (gl.astype(F32) + dx).astype(BF16)
+    input_grad = (low.astype(F32) + dx).astype(BF16)
     packed = jnp.concatenate([bup[0], jnp.sum(flat, axis=0, dtype=F32), bout[0], jnp.sum(grad_one * n, axis=0),
-                              jnp.sum(grad_one, axis=0), gain2[0], shift2[0],
-                              jnp.full(bup.shape[1], count[0].astype(F32))])
+                              jnp.sum(grad_one, axis=0), gain2[0], shift2[0], jnp.full(ff, count[0].astype(F32))])
     packed = lax.psum(packed, ("dp", "rows"))
-    part = jnp.concatenate([nn(n2t, gh), nn(glt, act), nn(ctxt, gl), nn(n1t, flat)], axis=1).astype(BF16)
+    mlp_part = jnp.concatenate([nn(n2t, mlp[:, :ff]), nn(glt, mlp[:, ff:])], axis=1)
+    rest = [nn(n1t, gu[s % 3, :, (s // 3) * PIECE : (s // 3 + 1) * PIECE]) for s in range(3 * width // PIECE)]
+    rest = jnp.concatenate(rest + [nn(ctxt, low)], axis=1)
+    columns = []
+    for i in range((mlp_part.shape[1] + rest.shape[1]) // CHUNK):
+        kind, j, *_ = chunk_columns(i, width // PIECE, 2 * ff // CHUNK * PIECE // width)
+        begin = j * (CHUNK if kind == "mlp" else PIECE)
+        columns.append((mlp_part if kind == "mlp" else rest)[:, begin : begin + CHUNK])
+    part = jnp.stack(columns, axis=1).astype(BF16)
     grads = lax.psum(lax.psum_scatter(part, "dp", scatter_dimension=0, tiled=True), "rows")
-    total = jnp.swapaxes(grads.reshape(grads.shape[0], -1, CHUNK), 0, 1)
-    return out, input_grad, total, packed.reshape(4, -1)
+    return out, input_grad, jnp.swapaxes(grads, 0, 1), packed.reshape(4, -1)
 
 
 def shards(tokens, segment_ids, true_counts, regroup, cotangent, ln1_gain, ln1_bias, qkv_weight, qkv_bias, out_weight,
@@ -794,13 +886,12 @@
     length, width = cotangent.shape
     ff = up_weight.shape[1]
     cosine, sine = (jnp.asarray(t) for t in rotary_tables(length))
-    (arrived, q, k, v, gc, n1t, n2t, glt, gl, act, gh, base, t2, gain2, shift2, bias_up, bias_out) = front(
+    (arrived, q, k, v, gc, n1t, n2t, glt, gl, mlp, base, t2, gain2, shift2, bias_up, bias_out) = front(
         true_counts, regroup, tokens, cotangent, cosine, sine, ln1_gain, ln1_bias, qkv_weight, qkv_bias, out_weight, out_bias,
         ln2_gain, ln2_bias, up_weight, up_bias, down_weight, down_bias)
-    ctx, ctxt, gu = attention(q, k, v, gc, segment_ids, cosine, sine)
-    last = reduce if (lax.axis_size("dp"), lax.axis_size("rows")) == (8, 4) else by_collectives
-    out, input_grad, total, vec = last(true_counts, n1t, n2t, glt, ctxt, gh, act, gl, gu, arrived, base, t2, ctx, qkv_weight,
-                                       out_weight, ln1_gain, gain2, shift2, bias_up, bias_out)
+    last = back if (lax.axis_size("dp"), lax.axis_size("rows")) == (8, 4) else by_collectives
+    out, input_grad, total, vec = last(true_counts, segment_ids, mlp, q, k, v, gc, arrived, base, t2, cosine, sine, ln1_gain, gain2,
+                                       shift2, bias_up, bias_out, n2t, glt, n1t, gl, out_weight, qkv_weight)
     (out, input_grad, up, down, low, qkv, gain1, shift1, bias_qkv, bias_out, gain2, shift2, bias_up, bias_down) = finish(
         out, input_grad, total, vec)
     return (out, input_grad, gain1, shift1, qkv, bias_qkv, low, bias_out, gain2, shift2, up, bias_up, down.T, bias_down)

time: 235 us -> 214 us (0.911); the launches traced: 232 us -> 214 us
  Pallas kernels: 225 us -> 207 us
    pallas_call x2 -> x1, Pallas kernels: 135 us -> 116 us  [back(): pl.pallas_call(functools.partial(back_body, rows=rows, row_ticks=row_tick...]
where the time goes in v5:
time: 214 us
  Pallas kernels  207 us (97%)
  local copies, waits for them, and re-layouts  5.18 us (2%)
    pallas_call x1, Pallas kernels, back(): pl.pallas_call(functools.partial(back_body, rows=rows, row_ticks=row_tick...  116 us
    pallas_call x1, Pallas kernels, front(): pl.pallas_call(functools.partial(front_body, tile=tile), grid=(chunks,),...  86.8 us
    unnamed x8, local copies, waits for them, and re-layouts  5.18 us

profile of v5, /device:TPU:0, one launch (start us, length us, event | category | flops | bytes accessed | tf_op | source)
XLA Modules:
  0.0 214.0 jit_solution(10569452828409543311)
XLA Ops:
  1.9 86.8 %front.1 = (bf16[1024,768]{1,0:T(8,128)(2,1)}, bf16[6,1024,128]{2,1,0:T(8,128)(2,1)}, bf16[6,1024,128]{2,1,0:T(8,128)(2,1)}, bf16[6,1024,128]{2,1,0:T(8,128)(2,1...) custom-call(s32[1]{0:T(128)S(6)} %copy.33.count_ref, ...), custom_call_target="tpu_custom_call" | custom-call | tf_op jit(solution)/shard_map/front/pallas_call | solution.py:243
  88.7 116.5 %back.1 = (bf16[1024,768]{1,0:T(8,128)(2,1)}, bf16[1024,768]{1,0:T(8,128)(2,1)}, bf16[18,96,512]{2,1,0:T(8,128)(2,1)}, f32[8,3072]{1,0:T(8,128)}) custom-call(s32[1]{0:T(128)S(6)} %copy.33.count_ref, s32[1024]{0:T(1024)} %seg_ref.1, bf16[1024,6144]{1,0:T(8,128)(2,1)} %get-tuple-element.48.mlp_ref, bf16[6,1024,128]{2,1,0:T(8,128)(2,1)} %get-tuple-element.49.q_ref, ...), custom_call_target="tpu_custom_call" | custom-call | tf_op jit(solution)/shard_map/back/pallas_call | solution.py:768
  205.2 0.0 copy-start
  205.2 1.5 copy-done
  206.7 0.0 copy-start.1
  206.7 1.4 copy-done.1
  208.1 0.0 copy-start.2
  208.1 1.4 copy-done.2
  209.5 0.0 copy-start.3
  209.5 0.9 copy-done.3
  210.4 3.5 %finish.1 = (bf16[1024,768]{1,0:T(8,128)(2,1)}, bf16[1024,768]{1,0:T(8,128)(2,1)}, f32[96,3072]{1,0:T(8,128)}, f32[96,3072]{1,0:T(8,128)}, f32[96,768]{1,0:T(8,1...) custom-call(bf16[1024,768]{1,0:T(8,128)(2,1)S(1)} %copy-done.1, ...), custom_call_target="tpu_custom_call" | custom-call | tf_op jit(solution)/shard_map/finish/pallas_call | solution.py:841
Async XLA Ops:
  205.2 1.5 copy-start
  206.7 1.4 copy-start.1
  208.1 1.4 copy-start.2
  209.5 0.9 copy-start.3

commit v6 on v5

--- a/solution.py
+++ b/solution.py
@@ -10,6 +10,10 @@
 HEAD_DIM = 64
 ROT = 16
 PAIR = 128
+CHUNK = 512
+PIECE = 256
+GROUP = 2
+SPAN = 256
 EPSILON = 1e-05
 EXCLUDED = -1e30
 F32 = jnp.float32
@@ -62,40 +66,75 @@
     return h * phi, phi + h * (e * 0.3989422804014327)
 
 
+def attend(q, k, v, gc, begins, t_first):
+    each, rows, span = range(len(q)), q[0].shape[0], k[0].shape[0]
+    low = lax.broadcasted_iota(jnp.int32, (rows, PAIR), 1) < HEAD_DIM
+
+    def both(t):
+        zero = jnp.zeros_like(t)
+        return jnp.concatenate([jnp.where(low, t, zero), jnp.where(low, zero, t)], axis=0)
+
+    q2, g2 = [both(t) for t in q], [both(t) for t in gc]
+    s_at = lax.broadcasted_iota(jnp.int32, (rows, span), 1)
+    t_at = t_first + lax.broadcasted_iota(jnp.int32, (rows, span), 0)
+    allowed = (s_at >= begins) & (s_at <= t_at)
+    allowed = jnp.concatenate([allowed, allowed], axis=0)
+    scores = [jnp.where(allowed, nt(q2[h], k[h]), EXCLUDED) for h in each]
+    dp = [nt(g2[h], v[h]) for h in each]
+    e = [jnp.exp(scores[h] - jnp.max(scores[h], axis=1, keepdims=True)) for h in each]
+    p = [e[h] * (1.0 / jnp.sum(e[h], axis=1, keepdims=True)) for h in each]
+    p16 = [p[h].astype(BF16) for h in each]
+    c2 = [nn(p16[h], v[h]) for h in each]
+    dv = [tn(p16[h], g2[h]) for h in each]
+    w = [p[h] * dp[h] for h in each]
+    ds16 = [(w[h] - p[h] * jnp.sum(w[h], axis=1, keepdims=True)).astype(BF16) for h in each]
+    d2 = [nn(ds16[h], k[h]) for h in each]
+    dk = [tn(ds16[h], q2[h]) for h in each]
+    context = [jnp.where(low, c2[h][:rows], c2[h][rows:]).astype(BF16) for h in each]
+    dq = [jnp.where(low, d2[h][:rows], d2[h][rows:]) * (HEAD_DIM ** -0.5) for h in each]
+    return context, dq, dk, dv
+
+
 def front_body(count_ref, want_ref, own_ref, cot_ref, cos_ref, sin_ref, g1_vec, b1_vec, bqkv_vec, bout_vec, g2_vec, b2_vec,
                bup_vec, bdown_vec, wqkv_hbm, wout_hbm, wup_hbm, wdown_hbm,
                x_ref, q_ref, k_ref, v_ref, gc_ref, n1t_ref, n2t_ref, glt_ref, gl_ref, mlp_ref, base_ref, t2_ref,
                gain2_ref, shift2_ref, bup_out, bout_out,
                wqkv_ref, wout_ref, wup_ref, wdown_ref, wants, from_near, from_half, to_inner, to_end,
-               g1_ref, b1_ref, bqkv_ref, bout_ref, g2_ref, b2_ref, bup_ref, bdown_ref, w_sem, want_send, want_recv, near_send, near_recv, inner_send, end_send, half_recv, *, tile):
+               g1_ref, b1_ref, bqkv_ref, bout_ref, g2_ref, b2_ref, bup_ref, bdown_ref, gl_all, ga_all, gc_all, w_sem, want_send, want_recv, near_send, near_recv, inner_send, end_send, half_recv, *, tile):
     step = pl.program_id(0)
     steps = pl.num_programs(0)
-    rows, width = cot_ref.shape
+    length, width = cot_ref.shape
+    rows = x_ref.shape[0]
     pairs = width // PAIR
     ff = wup_ref.shape[1]
-    chunks = own_ref.shape[0] // rows
+    chunks = length // rows
+    part = rows // 2
+    parts = length // part
     d, z = lax.axis_index("dp"), lax.axis_index("rows")
     inner = (z + 1) // 2 % 2
     near = z + 1 - 2 * (z % 2)
     other_inner, other_end = 3 - z, 6 - 3 * z
     loads = [pltpu.make_async_copy(src, dst, w_sem.at[j]) for j, (src, dst) in enumerate(
-        ((wqkv_hbm, wqkv_ref), (wout_hbm, wout_ref), (wup_hbm, wup_ref), (wdown_hbm, wdown_ref)))]
+        ((wdown_hbm, wdown_ref), (wout_hbm, wout_ref), (wqkv_hbm, wqkv_ref), (wup_hbm, wup_ref)))]
 
     def span(i):
         return pl.ds(pl.multiple_of(i * rows, rows), rows)
+
+    def bit(i):
+        return pl.ds(pl.multiple_of(i * part, part), part)
 
     def want_copy(j):
         to = lax.rem(z + j, 4)
         return remote(wants.at[0], wants.at[j], want_send.at[j], want_recv.at[j], (d, to))
 
     def near_copy(i):
-        return remote(own_ref.at[span(i)], from_near.at[span(i)], near_send.at[i], near_recv.at[i], (d, near))
+        return remote(own_ref.at[bit(i)], from_near.at[bit(i)], near_send.at[i], near_recv.at[i], (d, near))
 
     def inner_copy(i):
-        return remote(to_inner.at[span(i)], from_half.at[span(i)], inner_send.at[i], half_recv.at[i], (d, other_inner))
+        return remote(to_inner.at[bit(i)], from_half.at[bit(i)], inner_send.at[i], half_recv.at[i], (d, other_inner))
 
     def end_copy(i):
-        return remote(to_end.at[span(i)], from_half.at[span(i)], end_send.at[i], half_recv.at[i], (d, other_end))
+        return remote(to_end.at[bit(i)], from_half.at[bit(i)], end_send.at[i], half_recv.at[i], (d, other_end))
 
     def wanted(by):
         return wants[lax.rem(z - by + 4, 4), 0:1, 0:1]
@@ -104,11 +143,11 @@
         @pl.when(inner == 1)
         def _():
             near_copy(i).wait_recv()
-            mine = own_ref[span(i), :].astype(F32)
-            theirs = from_near[span(i), :].astype(F32)
-            to_end[span(i), :] = jnp.where(wanted(other_end) == near, theirs, mine).astype(BF16)
+            mine = own_ref[bit(i), :].astype(F32)
+            theirs = from_near[bit(i), :].astype(F32)
+            to_end[bit(i), :] = jnp.where(wanted(other_end) == near, theirs, mine).astype(BF16)
             end_copy(i).start()
-            to_inner[span(i), :] = jnp.where(wanted(other_inner) == near, theirs, mine).astype(BF16)
+            to_inner[bit(i), :] = jnp.where(wanted(other_inner) == near, theirs, mine).astype(BF16)
             inner_copy(i).start()
 
     @pl.when(step == 0)
@@ -125,44 +164,61 @@
             near_copy(i).start()
             return carry
 
-        lax.fori_loop(0, chunks, hand, 0)
+        lax.fori_loop(0, parts, hand, 0)
         for load in loads:
             load.start()
-        for j in (1, 2, 3):
-            want_copy(j).wait()
-        relay(0)
         for vec, ref in ((g1_vec, g1_ref), (b1_vec, b1_ref), (bqkv_vec, bqkv_ref), (bout_vec, bout_ref), (g2_vec, g2_ref),
                          (b2_vec, b2_ref), (bup_vec, bup_ref), (bdown_vec, bdown_ref)):
             ref[...] = vec[...].reshape(1, -1)
         gain2_ref[...] = jnp.zeros_like(gain2_ref)
         shift2_ref[...] = jnp.zeros_like(shift2_ref)
         bup_out[...] = jnp.zeros_like(bup_out)
-        bout_out[...] = jnp.zeros_like(bout_out)
-
-    @pl.when(step + 1 < chunks)
-    def _():
-        relay(step + 1)
-
-    @pl.when(step == 0)
-    def _():
-        for load in loads:
+        place = lax.broadcasted_iota(jnp.int32, (length, 1), 0)
+        masked = jnp.where(place < count_ref[0], cot_ref[...].astype(F32), 0.0)
+        gl_all[...] = masked.astype(BF16)
+        bout_out[...] = jnp.sum(masked, axis=0, keepdims=True)
+
+        def active(f):
+            ga_all[f] = nt(gl_all[...], wdown_ref[f * tile : (f + 1) * tile, :])
+
+        tiles = ff // tile
+        loads[0].wait()
+        for f in range(2):
+            active(f)
+        for j in (1, 2, 3):
+            want_copy(j).wait()
+        relay(0)
+        relay(1)
+        for f in range(2, tiles - 1):
+            active(f)
+        relay(2)
+        relay(3)
+        active(tiles - 1)
+        loads[1].wait()
+        for p in range(pairs):
+            gc_all[p] = nt(gl_all[...], wout_ref[p * PAIR : (p + 1) * PAIR, :]).astype(BF16)
+        for load in loads[2:]:
             load.wait()
 
-    place = step * rows + lax.broadcasted_iota(jnp.int32, (rows, 1), 0)
-    gl = jnp.where(place < count_ref[0], cot_ref[...].astype(F32), 0.0)
-    gl16 = gl.astype(BF16)
+    @pl.when((step > 0) & (step + 1 < chunks))
+    def _():
+        relay(2 * step + 2)
+        relay(2 * step + 3)
+
+    gl16 = gl_all[span(step), :]
     for j in range(gl_ref.shape[0]):
         gl_ref[j] = gl16[:, j * PIECE : (j + 1) * PIECE]
     glt_ref[...] = gl16.T
-    bout_out[...] += jnp.sum(gl, axis=0, keepdims=True)
     for p in range(pairs):
-        gc_ref[p] = nt(gl16, wout_ref[p * PAIR : (p + 1) * PAIR, :]).astype(BF16)
+        gc_ref[p] = gc_all[p, span(step), :]
 
     @pl.when(inner == 0)
     def _():
-        near_copy(step).wait_recv()
-
-    inner_copy(step).wait_recv()
+        for j in range(2):
+            near_copy(2 * step + j).wait_recv()
+
+    for j in range(2):
+        inner_copy(2 * step + j).wait_recv()
     source = wanted(z)
     x = jnp.where(source == near, from_near[span(step), :].astype(F32), from_half[span(step), :].astype(F32))
     x = jnp.where(source == z, own_ref[span(step), :].astype(F32), x)
@@ -189,7 +245,7 @@
     for f in range(0, ff, tile):
         cols = slice(f, f + tile)
         h = nn(n2, wup_ref[:, cols]) + bup_ref[:, cols]
-        ga = nt(gl16, wdown_ref[cols, :])
+        ga = ga_all[f // tile, span(step), :]
         a, slope = gelu_parts(h)
         a16 = a.astype(BF16)
         gh = ga * slope
@@ -215,7 +271,7 @@
                 end_copy(i).wait_send()
             return carry
 
-        lax.fori_loop(0, chunks, done, 0)
+        lax.fori_loop(0, parts, done, 0)
 
 
 def front(count, want, own, cot, cosine, sine, g1, b1, wqkv, bqkv, wout, bout, g2, b2, wup, bup, wdown, bdown, rows=128, tile=512):
@@ -243,7 +299,7 @@
     return pl.pallas_call(
         functools.partial(front_body, tile=tile),
         grid=(chunks,),
-        in_specs=[pl.BlockSpec(memory_space=pltpu.SMEM), pl.BlockSpec(memory_space=pltpu.SMEM), whole(own), row(width), row(PAIR), row(PAIR)]
+        in_specs=[pl.BlockSpec(memory_space=pltpu.SMEM), pl.BlockSpec(memory_space=pltpu.SMEM), whole(own), whole(cot), row(PAIR), row(PAIR)]
         + [whole(a) for a in vectors] + [pl.BlockSpec(memory_space=pl.ANY)] * 4,
         out_specs=[row(width)] + [heads] * 4 + [down] * 3
         + [pl.BlockSpec((width // PIECE, rows, PIECE), lambda i: (0, i, 0)), row(2 * ff)] + [row(width)] * 2
@@ -253,7 +309,9 @@
         + [s((length, width), F32)] * 2 + [s((1, width), F32), s((1, width), F32), s((1, ff), F32), s((1, width), F32)],
         scratch_shapes=[pltpu.VMEM(w.shape, BF16) for w in weights]
         + [pltpu.VMEM((4, 8, 128), jnp.int32)] + [pltpu.VMEM((length, width), BF16)] * 4
-        + [pltpu.VMEM((1, v.shape[0]), F32) for v in vectors] + [dma((4,)), dma((4,)), dma((4,))] + [dma((chunks,))] * 5,
+        + [pltpu.VMEM((1, v.shape[0]), F32) for v in vectors]
+        + [pltpu.VMEM((length, width), BF16), pltpu.VMEM((ff // tile, length, tile), F32), pltpu.VMEM((pairs, length, PAIR), BF16)]
+        + [dma((4,)), dma((4,)), dma((4,))] + [dma((2 * chunks,))] * 5,
         compiler_params=pltpu.CompilerParams(vmem_limit_bytes=60 * 2**20, collective_id=1, has_side_effects=True),
         name="front",
     )(count, want, own, cot, cosine, sine, *vectors, *weights)
@@ -362,11 +420,6 @@
     )(q, k, v, gc, segment, cosine, sine)
 
 
-CHUNK = 512
-PIECE = 256
-GROUP = 2
-
-
 class Line:
     def __init__(self):
         self.d = lax.axis_index("dp")
@@ -383,76 +436,56 @@
 
 
 class Everywhere:
-    HOPS = 7
-
-    def __init__(self, at, held, come, send, recv):
-        self.at, self.held, self.come, self.send, self.recv = at, held, come, send, recv
-
-    def copy(self, hop, to):
-        return remote(self.held.at[hop], self.come.at[hop], self.send.at[hop], self.recv.at[hop], to)
-
-    def take(self, hop, to):
-        self.copy(hop, to).wait()
-        self.held[hop + 1] = self.held[hop] + self.come[hop]
-
-    def hop(self, tick, spacing):
+    def __init__(self, at, of_dp, of_rows, send, recv):
+        self.at, self.of_dp, self.of_rows, self.send, self.recv = at, of_dp, of_rows, send, recv
+        self.devices, self.lines = of_dp.shape[0], of_rows.shape[0]
+
+    def over_dp(self, j):
         at = self.at
-        over = (at.over_core, at.over_x, at.over_y)
-
-        @pl.when(tick == 0)
-        def _():
-            self.copy(0, over[0]).start()
-
-        for j in (1, 2):
-            @pl.when(tick == j * spacing)
-            def _():
-                self.take(j - 1, over[j - 1])
-                self.copy(j, over[j]).start()
-
-        @pl.when(tick == 3 * spacing)
-        def _():
-            self.take(2, over[2])
-
-            @pl.when(at.inner == 0)
-            def _():
-                self.copy(3, at.near).start()
-
-        @pl.when((tick == 4 * spacing) & (at.inner == 1))
-        def _():
-            self.copy(3, at.near).wait_recv()
-            self.held[4] = self.held[3] + self.come[3]
-            self.copy(4, at.far).start()
-
-        @pl.when((tick == 4 * spacing) & (at.inner == 0))
-        def _():
-            self.copy(3, at.near).wait_send()
-
-        @pl.when((tick == 5 * spacing) & (at.inner == 1))
-        def _():
-            self.take(4, at.far)
-            self.copy(5, at.near).start()
-
-        @pl.when(tick == 6 * spacing)
-        def _():
-            @pl.when(at.inner == 1)
-            def _():
-                self.copy(5, at.near).wait_send()
-
-            @pl.when(at.inner == 0)
-            def _():
-                self.copy(5, at.near).wait_recv()
-                self.held[5] = self.come[5]
+        mine = self.of_dp.at[at.d]
+        return remote(mine, mine, self.send.at[j], self.recv.at[j], (lax.rem(at.d + j, self.devices), at.z))
+
+    def over_rows(self, j):
+        at, sem = self.at, self.devices + j
+        mine = self.of_rows.at[at.z]
+        return remote(mine, mine, self.send.at[sem], self.recv.at[sem], (at.d, lax.rem(at.z + j, self.lines)))
+
+    def begin(self, rows):
+        self.of_dp[self.at.d] = jnp.concatenate(rows, axis=0)
+        for j in range(1, self.devices):
+            self.over_dp(j).start()
+
+    def turn(self):
+        for j in range(1, self.devices):
+            self.over_dp(j).wait()
+        total = self.of_dp[0]
+        for j in range(1, self.devices):
+            total = total + self.of_dp[j]
+        self.of_rows[self.at.z] = total
+        for j in range(1, self.lines):
+            self.over_rows(j).start()
+
+    def end(self):
+        for j in range(1, self.lines):
+            self.over_rows(j).wait()
+        total = self.of_rows[0]
+        for j in range(1, self.lines):
+            total = total + self.of_rows[j]
+        return total
+
 
 LAGS = dict(core=1, first=3, second=5, z=7, mid=9, back=10)
 RING, CORE_RING, LINK_RING = 7, 6, 8
 
 
-def chunk_columns(i, groups, per_group):
+def chunk_columns(i, n_mlp, pieces, per_group):
     period = per_group + 1
-    if i < groups * period and i % period < per_group:
+    busy = n_mlp // per_group * period
+    if i < busy and i % period < per_group:
         return "mlp", per_group * (i // period) + i % period
-    j = i // period if i < groups * period else i - groups * per_group
-    return "rest", 2 * j, 2 * j + 1
+    j = i // period if i < busy else i - n_mlp
+    wide = pieces // 3
+    return ("rest", 2 * j, 2 * j + 1) if j < wide else ("rest", j + wide)
 
 
 def back_body(count_ref, seg_ref, mlp_ref, q_ref, k_ref, v_ref, gc_ref, x_ref, base_ref, t2_ref, cos_ref, sin_ref, g1_ref,
@@ -461,17 +494,19 @@
               left_mlp, left_rest, rhs, wout_ref, wqkv_ref, load_sem, ctx, dk_acc, dv_acc, begin_ref,
               part, from_core, from_first, from_second, from_near, from_far,
               c_send, c_recv, f_send, f_recv, s_send, s_recv, n_send, n_recv, m_send, m_recv,
-              held_v, come_v, v_s, v_r, gain1, shift1, bqkv, *, rows, row_ticks):
+              dp_e, rows_e, dp_l, rows_l, e_send, e_recv, l_send, l_recv, gain1, shift1, bqkv, *, rows, row_ticks):
     tick = pl.program_id(0)
     at = Line()
     chunks, block = total_ref.shape[0], total_ref.shape[1]
     length, width = seg_ref.shape[0], wout_ref.shape[0]
     groups = width // PIECE
     per_group = length // rows
+    n_mlp, pieces = 2 * bup_ref.shape[1] // CHUNK, 4 * groups
+    n_wide = n_mlp + pieces // 3
     period = per_group + 1
     busy = groups * period
-    g = jnp.minimum(tick // period, groups - 1)
-    spot = tick % period
+    g, spot = jnp.minimum(tick // period, groups - 1), tick % period
+    attending = (tick < busy) & (spot < per_group)
     first_need = (pltpu.make_async_copy(n2t_hbm, left_mlp.at[0], load_sem.at[0]),)
     later_need = [pltpu.make_async_copy(src, dst, load_sem.at[1 + j]) for j, (src, dst) in enumerate(
         ((glt_hbm, left_mlp.at[1]), (n1t_hbm, left_rest.at[0]), (gl_hbm, rhs.at[pl.ds(3 * groups, groups)]),
@@ -481,18 +516,11 @@
     def _():
         first_need[0].start()
         barrier = pltpu.get_barrier_semaphore()
-        for to in (at.over_core, at.over_x, at.over_y, at.near):
-            pl.semaphore_signal(barrier, inc=1, device_id=to, device_id_type=MESH)
-
-        @pl.when(at.inner == 1)
-        def _():
-            pl.semaphore_signal(barrier, inc=1, device_id=at.far, device_id_type=MESH)
-            pl.semaphore_wait(barrier, 5)
-
-        @pl.when(at.inner == 0)
-        def _():
-            pl.semaphore_wait(barrier, 4)
-
+        for j in range(1, 8):
+            pl.semaphore_signal(barrier, inc=1, device_id=(lax.rem(at.d + j, 8), at.z), device_id_type=MESH)
+        for j in range(1, 4):
+            pl.semaphore_signal(barrier, inc=1, device_id=(at.d, lax.rem(at.z + j, 4)), device_id_type=MESH)
+        pl.semaphore_wait(barrier, 10)
         for load in later_need:
             load.start()
         wide = jnp.broadcast_to(seg_ref[...].reshape(1, -1), (8, length)).astype(F32)
@@ -518,22 +546,30 @@
         second = (at.d + even * (4 - 8 * at.y) + (1 - even) * (2 - 4 * at.x), at.z)
         return f, s, first, second, i % RING
 
-    def core_copy(i):
-        return remote(part.at[i % RING, 1 - at.core], from_core.at[i % CORE_RING], c_send.at[i], c_recv.at[i], at.over_core)
-
-    def first_copy(i):
+    def core_copy(i, w):
+        lanes = pl.ds(0, w)
+        return remote(part.at[i % RING, 1 - at.core, :, :, :, lanes], from_core.at[i % CORE_RING, :, :, :, lanes],
+                      c_send.at[i], c_recv.at[i], at.over_core)
+
+    def first_copy(i, w):
         f, s, first, second, slot = places(i)
-        return remote(part.at[slot, at.core, 1 - f], from_first.at[i % LINK_RING], f_send.at[i], f_recv.at[i], first)
-
-    def second_copy(i):
+        lanes = pl.ds(0, w)
+        return remote(part.at[slot, at.core, 1 - f, :, :, lanes], from_first.at[i % LINK_RING, :, :, lanes],
+                      f_send.at[i], f_recv.at[i], first)
+
+    def second_copy(i, w):
         f, s, first, second, slot = places(i)
-        return remote(part.at[slot, at.core, f, 1 - s], from_second.at[i % LINK_RING], s_send.at[i], s_recv.at[i], second)
-
-    def out_copy(i):
-        return remote(total_ref.at[i], from_near.at[i % LINK_RING], n_send.at[i], n_recv.at[i], at.near)
-
-    def far_copy(i):
-        return remote(total_ref.at[i], from_far.at[i % LINK_RING], m_send.at[i], m_recv.at[i], at.far)
+        lanes = pl.ds(0, w)
+        return remote(part.at[slot, at.core, f, 1 - s, :, lanes], from_second.at[i % LINK_RING, :, lanes],
+                      s_send.at[i], s_recv.at[i], second)
+
+    def out_copy(i, w):
+        lanes = pl.ds(0, w)
+        return remote(total_ref.at[i, :, lanes], from_near.at[i % LINK_RING, :, lanes], n_send.at[i], n_recv.at[i], at.near)
+
+    def far_copy(i, w):
+        lanes = pl.ds(0, w)
+        return remote(total_ref.at[i, :, lanes], from_far.at[i % LINK_RING, :, lanes], m_send.at[i], m_recv.at[i], at.far)
 
     def plus(a, b):
         return (a.astype(F32) + b.astype(F32)).astype(BF16)
@@ -548,83 +584,94 @@
             part[tick % RING, c, a, b, :, cols] = rows_of[j * block : (j + 1) * block].astype(BF16)
 
     half = width // 2
-    is_mlp = (tick < busy) & (spot < per_group)
-
-    @pl.when(is_mlp)
-    def _():
-        left = (per_group * g + spot) // (groups * per_group // 2)
+
+    @pl.when(attending)
+    def _():
+        left = (per_group * g + spot) // (n_mlp // 2)
         for h in range(2):
             put(h, half, slice(0, CHUNK), nn(left_mlp[left, h * half : (h + 1) * half, :], mlp_ref[...]))
-        core_copy(tick).start()
-
-    @pl.when((tick < chunks) & jnp.logical_not(is_mlp))
-    def _():
-        j = (tick // period) * (1 - tick // busy) + (tick - groups * per_group) * (tick // busy)
+        core_copy(tick, CHUNK).start()
+
+    def rest(s, e):
+        for h in range(2):
+            put(h, half, slice(e * PIECE, (e + 1) * PIECE),
+                nn(left_rest[s // (3 * groups), h * half : (h + 1) * half, :], rhs[s]))
+
+    @pl.when((tick < n_wide) & jnp.logical_not(attending))
+    def _():
+        late = tick // busy
+        j = (tick // period) * (1 - late) + (tick - n_mlp) * late
         for e in range(2):
-            s = 2 * j + e
-            for h in range(2):
-                put(h, half, slice(e * PIECE, (e + 1) * PIECE),
-                    nn(left_rest[s // (3 * groups), h * half : (h + 1) * half, :], rhs[s]))
-        core_copy(tick).start()
+            rest(2 * j + e, e)
+        core_copy(tick, CHUNK).start()
+
+    @pl.when((tick >= n_wide) & (tick < chunks))
+    def _():
+        rest(tick - n_wide + 2 * (n_wide - n_mlp), 0)
+        core_copy(tick, PIECE).start()
 
     def when(lag, f):
         i = tick - lag
 
-        @pl.when((i >= 0) & (i < chunks))
+        @pl.when((i >= 0) & (i < n_wide))
         def _():
-            f(i)
-
-    def core_step(i):
+            f(i, CHUNK)
+
+        @pl.when((i >= n_wide) & (i < chunks))
+        def _():
+            f(i, PIECE)
+
+    def core_step(i, w):
         f, s, first, second, slot = places(i)
-        core_copy(i).wait()
+        core_copy(i, w).wait()
         for a in range(2):
             for b in range(2):
-                part[slot, at.core, a, b] = plus(part[slot, at.core, a, b], from_core[i % CORE_RING, a, b])
-        first_copy(i).start()
-
-    def first_step(i):
+                part[slot, at.core, a, b, :, :w] = plus(part[slot, at.core, a, b, :, :w], from_core[i % CORE_RING, a, b, :, :w])
+        first_copy(i, w).start()
+
+    def first_step(i, w):
         f, s, first, second, slot = places(i)
-        first_copy(i).wait()
+        first_copy(i, w).wait()
         for b in range(2):
-            part[slot, at.core, f, b] = plus(part[slot, at.core, f, b], from_first[i % LINK_RING, b])
-        second_copy(i).start()
-
-    def second_step(i):
+            part[slot, at.core, f, b, :, :w] = plus(part[slot, at.core, f, b, :, :w], from_first[i % LINK_RING, b, :, :w])
+        second_copy(i, w).start()
+
+    def second_step(i, w):
         f, s, first, second, slot = places(i)
-        second_copy(i).wait()
-        total_ref[i] = plus(part[slot, at.core, f, s], from_second[i % LINK_RING])
+        second_copy(i, w).wait()
+        total_ref[i, :, :w] = plus(part[slot, at.core, f, s, :, :w], from_second[i % LINK_RING, :, :w])
 
         @pl.when(at.inner == 0)
         def _():
-            out_copy(i).start()
-
-    def near_step(i):
+            out_copy(i, w).start()
+
+    def near_step(i, w):
         @pl.when(at.inner == 1)
         def _():
-            out_copy(i).wait_recv()
-            total_ref[i] = plus(total_ref[i], from_near[i % LINK_RING])
-            far_copy(i).start()
-
-    def far_step(i):
+            out_copy(i, w).wait_recv()
+            total_ref[i, :, :w] = plus(total_ref[i, :, :w], from_near[i % LINK_RING, :, :w])
+            far_copy(i, w).start()
+
+    def far_step(i, w):
         @pl.when(at.inner == 1)
         def _():
-            far_copy(i).wait()
-            total_ref[i] = plus(total_ref[i], from_far[i % LINK_RING])
-            out_copy(i).start()
+            far_copy(i, w).wait()
+            total_ref[i, :, :w] = plus(total_ref[i, :, :w], from_far[i % LINK_RING, :, :w])
+            out_copy(i, w).start()
 
         @pl.when(at.inner == 0)
         def _():
-            out_copy(i).wait_send()
-
-    def back_step(i):
+            out_copy(i, w).wait_send()
+
+    def back_step(i, w):
         @pl.when(at.inner == 0)
         def _():
-            out_copy(i).wait_recv()
-            total_ref[i] = from_near[i % LINK_RING]
+            out_copy(i, w).wait_recv()
+            total_ref[i, :, :w] = from_near[i % LINK_RING, :, :w]
 
         @pl.when(at.inner == 1)
         def _():
-            out_copy(i).wait_send()
+            out_copy(i, w).wait_send()
 
     when(LAGS["core"], core_step)
     when(LAGS["first"], first_step)
@@ -634,57 +681,32 @@
     when(LAGS["back"], back_step)
 
     each = range(GROUP)
-    low = lax.broadcasted_iota(jnp.int32, (rows, PAIR), 1) < HEAD_DIM
 
     def unit(b):
         span = (b + 1) * rows
         mine = slice(b * rows, span)
-
-        def both(ref, h):
-            t = ref[h, mine, :]
-            zero = jnp.zeros_like(t)
-            return jnp.concatenate([jnp.where(low, t, zero), jnp.where(low, zero, t)], axis=0)
-
-        q2 = [both(q_ref, h) for h in each]
-        g2 = [both(gc_ref, h) for h in each]
-        k = [k_ref[h, :span, :] for h in each]
-        v = [v_ref[h, :span, :] for h in each]
-        s_at = lax.broadcasted_iota(jnp.int32, (rows, span), 1)
-        t_at = b * rows + lax.broadcasted_iota(jnp.int32, (rows, span), 0)
-        allowed = (s_at >= begin_ref[mine, :]) & (s_at <= t_at)
-        allowed = jnp.concatenate([allowed, allowed], axis=0)
-        scores = [jnp.where(allowed, nt(q2[h], k[h]), EXCLUDED) for h in each]
-        dp = [nt(g2[h], v[h]) for h in each]
-        e = [jnp.exp(scores[h] - jnp.max(scores[h], axis=1, keepdims=True)) for h in each]
-        p = [e[h] * (1.0 / jnp.sum(e[h], axis=1, keepdims=True)) for h in each]
-        p16 = [p[h].astype(BF16) for h in each]
-        c2 = [nn(p16[h], v[h]) for h in each]
-        for h in each:
-            dv_acc[h, :span, :] += tn(p16[h], g2[h])
-        w = [p[h] * dp[h] for h in each]
-        ds16 = [(w[h] - p[h] * jnp.sum(w[h], axis=1, keepdims=True)).astype(BF16) for h in each]
-        d2 = [nn(ds16[h], k[h]) for h in each]
-        for h in each:
-            dk_acc[h, :span, :] += tn(ds16[h], q2[h])
+        context, dq, dk, dv = attend([q_ref[h, mine, :] for h in each], [k_ref[h, :span, :] for h in each],
+                                     [v_ref[h, :span, :] for h in each], [gc_ref[h, mine, :] for h in each],
+                                     begin_ref[mine, :], b * rows)
         for h in each:
             cols = slice(h * PAIR, (h + 1) * PAIR)
-            context = jnp.where(low, c2[h][:rows], c2[h][rows:]).astype(BF16)
-            ctx[g, mine, cols] = context
-            left_rest[1, pl.ds(pl.multiple_of(g * PIECE + h * PAIR, PAIR), PAIR), mine] = context.T
-            dq = jnp.where(low, d2[h][:rows], d2[h][rows:]) * (HEAD_DIM ** -0.5)
-            rhs[3 * g, mine, cols] = (dq * cos_ref[mine, :] - turned(dq) * sin_ref[mine, :]).astype(BF16)
-
-    @pl.when((tick < busy) & (spot == 0))
+            dk_acc[h, :span, :] += dk[h]
+            dv_acc[h, :span, :] += dv[h]
+            ctx[g, mine, cols] = context[h]
+            left_rest[1, pl.ds(pl.multiple_of(g * PIECE + h * PAIR, PAIR), PAIR), mine] = context[h].T
+            rhs[3 * g, mine, cols] = (dq[h] * cos_ref[mine, :] - turned(dq[h]) * sin_ref[mine, :]).astype(BF16)
+
+    @pl.when(attending & (spot == 0))
     def _():
         dk_acc[...] = jnp.zeros_like(dk_acc)
         dv_acc[...] = jnp.zeros_like(dv_acc)
 
     for b in range(per_group):
-        @pl.when((tick < busy) & (spot == b))
+        @pl.when(attending & (spot == b))
         def _():
             unit(b)
 
-    @pl.when((tick < busy) & (spot == per_group - 1))
+    @pl.when(attending & (spot == per_group - 1))
     def _():
         for h in each:
             cols = slice(h * PAIR, (h + 1) * PAIR)
@@ -717,25 +739,38 @@
         gl = jnp.concatenate([rhs[3 * groups + j, here, :] for j in range(groups)], axis=1)
         ig_ref[...] = (gl.astype(F32) + dx).astype(BF16)
 
+    def lines(ref):
+        return [ref[:, j : j + width] for j in range(0, ref.shape[1], width)]
+
+    early = Everywhere(at, dp_e, rows_e, e_send, e_recv)
+    late = Everywhere(at, dp_l, rows_l, l_send, l_recv)
+    row = jnp.full((1, width), count_ref[0].astype(F32), F32)
+
+    @pl.when(tick == 1)
+    def _():
+        early.begin(lines(bup_ref) + lines(bout_ref) + lines(gain2_ref) + lines(shift2_ref) + [row])
+
+    @pl.when(tick == 4)
+    def _():
+        early.turn()
+
+    @pl.when(tick == 7)
+    def _():
+        vec_ref[0] = early.end()
+
     begin = busy + row_ticks
 
     @pl.when(tick == begin)
     def _():
-        held_v[0] = jnp.zeros(held_v.shape[1:], F32)
-        held_v[0, 0:1, :] = bup_ref[...]
-        held_v[0, 1:2, : 3 * width] = bqkv[...]
-        held_v[0, 1:2, 3 * width :] = bout_ref[...]
-        held_v[0, 2:3, :width] = gain1[...]
-        held_v[0, 2:3, width : 2 * width] = shift1[...]
-        held_v[0, 2:3, 2 * width : 3 * width] = gain2_ref[...]
-        held_v[0, 2:3, 3 * width :] = shift2_ref[...]
-        held_v[0, 3:4, :] = jnp.full((1, held_v.shape[2]), count_ref[0].astype(F32), F32)
-
-    Everywhere(at, held_v, come_v, v_s, v_r).hop(tick - begin, 1)
-
-    @pl.when(tick == begin + 6)
-    def _():
-        vec_ref[...] = held_v[5]
+        late.begin(lines(gain1) + lines(shift1) + lines(bqkv) + [jnp.zeros((3, width), F32)])
+
+    @pl.when(tick == begin + 2)
+    def _():
+        late.turn()
+
+    @pl.when(tick == begin + 4)
+    def _():
+        vec_ref[1] = late.end()
 
 
 def back(count, segment, mlp, q, k, v, gc, x, base, t2, cosine, sine, g1, gain2, shift2, bup, bout, n2t, glt, n1t, gl, wout, wqkv,
@@ -744,12 +779,12 @@
     ff = bup.shape[1]
     block = width // 8
     groups = width // PIECE
-    chunks = (2 * ff + 4 * width) // CHUNK
-    period = length // rows + 1
+    n_mlp, pieces = 2 * ff // CHUNK, 4 * groups
+    chunks = n_mlp + pieces // 3 + pieces - 2 * (pieces // 3)
+    row_ticks = length // rows
+    period = row_ticks + 1
     busy = groups * period
-    row_ticks = length // rows
-    ticks = max(chunks + LAGS["back"], busy + row_ticks + 7)
-    n_mlp = 2 * ff // CHUNK
+    ticks = max(chunks + LAGS["back"], busy + row_ticks + 5)
 
     def row(cols):
         return pl.BlockSpec((rows, cols), lambda t: (jnp.clip(t - busy, 0, row_ticks - 1), 0))
@@ -758,30 +793,29 @@
         return pl.BlockSpec(a.shape, lambda t: (0,) * a.ndim, pipeline_mode=pl.Buffered(1))
 
     def mlp_cols(t):
-        return (0, jnp.minimum((period - 1) * (t // period) + jnp.minimum(t % period, period - 2), n_mlp - 1))
+        return (0, jnp.minimum(row_ticks * (t // period) + jnp.minimum(t % period, row_ticks - 1), n_mlp - 1))
 
     heads = pl.BlockSpec((GROUP, length, PAIR), lambda t: (jnp.minimum(t // period, groups - 1), 0, 0))
     s = jax.ShapeDtypeStruct
     dma = pltpu.SemaphoreType.DMA
-    hops = Everywhere.HOPS
     loaded = (n2t, glt, n1t, gl, wout, wqkv)
     return pl.pallas_call(
         functools.partial(back_body, rows=rows, row_ticks=row_ticks),
         grid=(ticks,),
         in_specs=[pl.BlockSpec(memory_space=pltpu.SMEM), whole(segment), pl.BlockSpec((length, CHUNK), mlp_cols)]
         + [heads] * 4 + [row(width)] * 3
-        + [whole(a) for a in (cosine, sine, g1, gain2, shift2, bup, bout)] + [pl.BlockSpec(memory_space=pl.ANY)] * 6,
+        + [whole(a) for a in (cosine, sine, g1, gain2, shift2, bup, bout)] + [pl.BlockSpec(memory_space=pl.ANY)] * len(loaded),
         out_specs=[row(width), row(width),
                    pl.BlockSpec((chunks, block, CHUNK), lambda t: (0, 0, 0), pipeline_mode=pl.Buffered(1)),
-                   pl.BlockSpec((8, ff), lambda t: (0, 0), pipeline_mode=pl.Buffered(1))],
-        out_shape=[s((length, width), BF16), s((length, width), BF16), s((chunks, block, CHUNK), BF16), s((8, ff), F32)],
+                   pl.BlockSpec((2, 8, width), lambda t: (0, 0, 0), pipeline_mode=pl.Buffered(1))],
+        out_shape=[s((length, width), BF16), s((length, width), BF16), s((chunks, block, CHUNK), BF16), s((2, 8, width), F32)],
         scratch_shapes=[
             pltpu.VMEM((2, width, length), BF16),
             pltpu.VMEM((2, width, length), BF16),
             pltpu.VMEM((4 * groups, length, PIECE), BF16),
             pltpu.VMEM(wout.shape, BF16),
             pltpu.VMEM(wqkv.shape, BF16),
-            dma((6,)),
+            dma((len(loaded),)),
             pltpu.VMEM((groups, length, PIECE), BF16),
             pltpu.VMEM((GROUP, length, PAIR), F32),
             pltpu.VMEM((GROUP, length, PAIR), F32),
@@ -793,8 +827,9 @@
             pltpu.VMEM((LINK_RING, block, CHUNK), BF16),
             pltpu.VMEM((LINK_RING, block, CHUNK), BF16),
         ] + [dma((chunks,))] * 10 + [
-            pltpu.VMEM((hops, 8, ff), F32), pltpu.VMEM((hops, 8, ff), F32),
-            dma((hops,)), dma((hops,)),
+            pltpu.VMEM((8, 8, width), F32), pltpu.VMEM((4, 8, width), F32),
+            pltpu.VMEM((8, 8, width), F32), pltpu.VMEM((4, 8, width), F32),
+            dma((12,)), dma((12,)), dma((12,)), dma((12,)),
             pltpu.VMEM((1, width), F32), pltpu.VMEM((1, width), F32), pltpu.VMEM((1, 3 * width), F32),
         ],
         compiler_params=pltpu.CompilerParams(vmem_limit_bytes=60 * 2**20, collective_id=0, has_side_effects=True),
@@ -803,17 +838,21 @@
 
 
 def finish_body(out_hbm, ig_hbm, total_ref, vec_ref, out_to, ig_to, up_ref, down_ref, low_ref, qkv_ref,
-                gain1_ref, shift1_ref, bqkv_ref, bout_ref, gain2_ref, shift2_ref, bup_ref, bdown_ref, sem):
-    copies = [pltpu.make_async_copy(out_hbm, out_to, sem.at[0]), pltpu.make_async_copy(ig_hbm, ig_to, sem.at[1])]
-    for copy in copies:
-        copy.start()
+                gain1_ref, shift1_ref, bqkv_ref, bout_ref, gain2_ref, shift2_ref, bup_ref, bdown_ref, held, sem):
+    takes = [pltpu.make_async_copy(a, held.at[j], sem.at[j]) for j, a in enumerate((out_hbm, ig_hbm))]
+    copies = [pltpu.make_async_copy(held.at[j], a, sem.at[2 + j]) for j, a in enumerate((out_to, ig_to))]
+    for take in takes:
+        take.start()
     width, ff = gain1_ref.shape[0], bup_ref.shape[0]
-    factor = 1.0 / vec_ref[3:4, 0:1]
+    factor = 1.0 / vec_ref[0, 7:8, 0:1]
     groups = width // PIECE
     n_up = ff // CHUNK
+    for take, copy in zip(takes, copies):
+        take.wait()
+        copy.start()
     for i in range(total_ref.shape[0]):
         grad = total_ref[i].astype(F32) * factor
-        kind, *what = chunk_columns(i, groups, 2 * n_up // groups)
+        kind, *what = chunk_columns(i, 2 * n_up, 4 * groups, 2 * n_up // groups)
         if kind == "mlp":
             ref, j = (up_ref, what[0]) if what[0] < n_up else (down_ref, what[0] - n_up)
             ref[:, j * CHUNK : (j + 1) * CHUNK] = grad
@@ -821,20 +860,23 @@
         for e, s in enumerate(what):
             ref, col = (qkv_ref, (s % 3) * width + (s // 3) * PIECE) if s < 3 * groups else (low_ref, (s - 3 * groups) * PIECE)
             ref[:, col : col + PIECE] = grad[:, e * PIECE : (e + 1) * PIECE]
-    vec = vec_ref[...] * factor
-    bup_ref[...] = vec[0]
-    bqkv_ref[...] = vec[1, : 3 * width]
-    bout_ref[...] = vec[1, 3 * width :]
-    bdown_ref[...] = vec[1, 3 * width :]
-    for j, ref in enumerate((gain1_ref, shift1_ref, gain2_ref, shift2_ref)):
-        ref[...] = vec[2, j * width : (j + 1) * width]
+    first, second = vec_ref[0] * factor, vec_ref[1] * factor
+    for j in range(ff // width):
+        bup_ref[j * width : (j + 1) * width] = first[j]
+    j = ff // width
+    for ref, line in ((bout_ref, first[j]), (bdown_ref, first[j]), (gain2_ref, first[j + 1]), (shift2_ref, first[j + 2]),
+                      (gain1_ref, second[0]), (shift1_ref, second[1])):
+        ref[...] = line
+    for j in range(3):
+        bqkv_ref[j * width : (j + 1) * width] = second[2 + j]
     for copy in copies:
         copy.wait()
 
 
-def finish(out, ig, total, vec):
+def finish(out, ig, total, vec, ff):
     length, width = out.shape
-    block, ff = total.shape[1], vec.shape[1]
+    block = total.shape[1]
+
     s = jax.ShapeDtypeStruct
     hbm, vmem = pl.BlockSpec(memory_space=pltpu.HBM), pl.BlockSpec(memory_space=pltpu.VMEM)
     vectors = (width, width, 3 * width, width, width, width, ff, width)
@@ -844,8 +886,8 @@
         out_specs=[hbm, hbm] + [vmem] * 12,
         out_shape=[s(out.shape, BF16), s(ig.shape, BF16), s((block, ff), F32), s((block, ff), F32), s((block, width), F32),
                    s((block, 3 * width), F32)] + [s((n,), F32) for n in vectors],
-        scratch_shapes=[pltpu.SemaphoreType.DMA((2,))],
-        compiler_params=pltpu.CompilerParams(vmem_limit_bytes=40 * 2**20),
+        scratch_shapes=[pltpu.VMEM((2, length, width), BF16), pltpu.SemaphoreType.DMA((4,))],
+        compiler_params=pltpu.CompilerParams(vmem_limit_bytes=60 * 2**20),
         name="finish",
     )(out, ig, total, vec)
 
@@ -865,20 +907,22 @@
     t = grad_one * g1 + t2
     dx = r * (t - jnp.mean(t, axis=1, keepdims=True) - n * jnp.mean(t * n, axis=1, keepdims=True))
     input_grad = (low.astype(F32) + dx).astype(BF16)
-    packed = jnp.concatenate([bup[0], jnp.sum(flat, axis=0, dtype=F32), bout[0], jnp.sum(grad_one * n, axis=0),
-                              jnp.sum(grad_one, axis=0), gain2[0], shift2[0], jnp.full(ff, count[0].astype(F32))])
+    packed = jnp.concatenate([bup[0], bout[0], gain2[0], shift2[0], jnp.full(width, count[0].astype(F32)),
+                              jnp.sum(grad_one * n, axis=0), jnp.sum(grad_one, axis=0), jnp.sum(flat, axis=0, dtype=F32),
+                              jnp.zeros(3 * width, F32)])
     packed = lax.psum(packed, ("dp", "rows"))
     mlp_part = jnp.concatenate([nn(n2t, mlp[:, :ff]), nn(glt, mlp[:, ff:])], axis=1)
     rest = [nn(n1t, gu[s % 3, :, (s // 3) * PIECE : (s // 3 + 1) * PIECE]) for s in range(3 * width // PIECE)]
     rest = jnp.concatenate(rest + [nn(ctxt, low)], axis=1)
-    columns = []
-    for i in range((mlp_part.shape[1] + rest.shape[1]) // CHUNK):
-        kind, j, *_ = chunk_columns(i, width // PIECE, 2 * ff // CHUNK * PIECE // width)
-        begin = j * (CHUNK if kind == "mlp" else PIECE)
-        columns.append((mlp_part if kind == "mlp" else rest)[:, begin : begin + CHUNK])
+    columns, n_mlp, pieces = [], 2 * ff // CHUNK, 4 * width // PIECE
+    for i in range(n_mlp + pieces // 3 + pieces - 2 * (pieces // 3)):
+        kind, *what = chunk_columns(i, n_mlp, pieces, n_mlp * PIECE // width)
+        held = mlp_part if kind == "mlp" else rest
+        begin, size = (what[0] * CHUNK, CHUNK) if kind == "mlp" else (what[0] * PIECE, len(what) * PIECE)
+        columns.append(jnp.pad(held[:, begin : begin + size], ((0, 0), (0, CHUNK - size))))
     part = jnp.stack(columns, axis=1).astype(BF16)
     grads = lax.psum(lax.psum_scatter(part, "dp", scatter_dimension=0, tiled=True), "rows")
-    return out, input_grad, jnp.swapaxes(grads, 0, 1), packed.reshape(4, -1)
+    return out, input_grad, jnp.swapaxes(grads, 0, 1), packed.reshape(2, 8, width)
 
 
 def shards(tokens, segment_ids, true_counts, regroup, cotangent, ln1_gain, ln1_bias, qkv_weight, qkv_bias, out_weight,
@@ -893,7 +937,7 @@
     out, input_grad, total, vec = last(true_counts, segment_ids, mlp, q, k, v, gc, arrived, base, t2, cosine, sine, ln1_gain, gain2,
                                        shift2, bias_up, bias_out, n2t, glt, n1t, gl, out_weight, qkv_weight)
     (out, input_grad, up, down, low, qkv, gain1, shift1, bias_qkv, bias_out, gain2, shift2, bias_up, bias_down) = finish(
-        out, input_grad, total, vec)
+        out, input_grad, total, vec, up_weight.shape[1])
     return (out, input_grad, gain1, shift1, qkv, bias_qkv, low, bias_out, gain2, shift2, up, bias_up, down.T, bias_down)
 
 

time: 214 us -> 209 us (0.977)
  local copies, waits for them, and re-layouts: 5.18 us -> 0 us
    unnamed x8 -> x0, local copies, waits for them, and re-layouts: 5.18 us -> none
    pallas_call x1, Pallas kernels: 116 us -> 112 us  [back(): pl.pallas_call(functools.partial(back_body, rows=rows, row_ticks=row_tick...]
    pallas_call x1, Pallas kernels: 3.48 us -> 6.46 us  [finish(): pl.pallas_call(finish_body, in_specs=[hbm, hbm, vmem, vmem], out_specs=[h...]
where the time goes in v6:
time: 209 us
  Pallas kernels  206 us (99%)
  between operations  2.12 us (1%)
    pallas_call x1, Pallas kernels, back(): pl.pallas_call(functools.partial(back_body, rows=rows, row_ticks=row_tick...  112 us
    pallas_call x1, Pallas kernels, front(): pl.pallas_call(functools.partial(front_body, tile=tile), grid=(chunks,),...  87.8 us
    pallas_call x1, Pallas kernels, finish(): pl.pallas_call(finish_body, in_specs=[hbm, hbm, vmem, vmem], out_specs=[h...  6.46 us

profile of v6, /device:TPU:0, one launch (start us, length us, event | category | flops | bytes accessed | tf_op | source)
XLA Modules:
  0.0 208.6 jit_solution(1587845756330290541)
XLA Ops:
  1.9 87.8 %front.1 = (bf16[1024,768]{1,0:T(8,128)(2,1)}, bf16[6,1024,128]{2,1,0:T(8,128)(2,1)}, bf16[6,1024,128]{2,1,0:T(8,128)(2,1)}, bf16[6,1024,128]{2,1,0:T(8,128)(2,1...) custom-call(s32[1]{0:T(128)S(6)} %copy.33.count_ref, ...), custom_call_target="tpu_custom_call" | custom-call | tf_op jit(solution)/shard_map/front/pallas_call | solution.py:299
  89.8 112.2 %back.1 = (bf16[1024,768]{1,0:T(8,128)(2,1)}, bf16[1024,768]{1,0:T(8,128)(2,1)}, bf16[20,96,512]{2,1,0:T(8,128)(2,1)}, f32[2,8,768]{2,1,0:T(8,128)}) custom-call(s32[1]{0:T(128)S(6)} %copy.33.count_ref, s32[1024]{0:T(1024)} %seg_ref.1, bf16[1024,6144]{1,0:T(8,128)(2,1)} %get-tuple-element.48.mlp_ref, bf16[6,1024,128]{2,1,0:T(8,128)(2,1)} %get-tuple-element.49.q_ref, ...), custom_call_target="tpu_custom_call" | custom-call | tf_op jit(solution)/shard_map/back/pallas_call | solution.py:802
  201.9 6.5 %finish.1 = (bf16[1024,768]{1,0:T(8,128)(2,1)}, bf16[1024,768]{1,0:T(8,128)(2,1)}, f32[96,3072]{1,0:T(8,128)}, f32[96,3072]{1,0:T(8,128)}, f32[96,768]{1,0:T(8,1...) custom-call(bf16[1024,768]{1,0:T(8,128)(2,1)} %get-tuple-element.64., ...), custom_call_target="tpu_custom_call" | custom-call | tf_op jit(solution)/shard_map/finish/pallas_call | solution.py:883

commit v7 on v6

--- a/solution.py
+++ b/solution.py
@@ -95,12 +95,12 @@
     return context, dq, dk, dv
 
 
-def front_body(count_ref, want_ref, own_ref, cot_ref, cos_ref, sin_ref, g1_vec, b1_vec, bqkv_vec, bout_vec, g2_vec, b2_vec,
-               bup_vec, bdown_vec, wqkv_hbm, wout_hbm, wup_hbm, wdown_hbm,
+def front_body(count_ref, want_ref, seg_ref, cos_ref, sin_ref, g1_vec, b1_vec, bqkv_vec, bout_vec, g2_vec, b2_vec,
+               bup_vec, bdown_vec, own_hbm, cot_hbm, wqkv_hbm, wout_hbm, wup_hbm, wdown_hbm,
                x_ref, q_ref, k_ref, v_ref, gc_ref, n1t_ref, n2t_ref, glt_ref, gl_ref, mlp_ref, base_ref, t2_ref,
-               gain2_ref, shift2_ref, bup_out, bout_out,
+               gain2_ref, shift2_ref, bup_out, bout_out, begin_ref,
                wqkv_ref, wout_ref, wup_ref, wdown_ref, wants, from_near, from_half, to_inner, to_end,
-               g1_ref, b1_ref, bqkv_ref, bout_ref, g2_ref, b2_ref, bup_ref, bdown_ref, gl_all, ga_all, gc_all, w_sem, want_send, want_recv, near_send, near_recv, inner_send, end_send, half_recv, *, tile):
+               g1_ref, b1_ref, bqkv_ref, bout_ref, g2_ref, b2_ref, bup_ref, bdown_ref, own_ref, cot_ref, gl_all, ga_all, gc_all, w_sem, want_send, want_recv, near_send, near_recv, inner_send, end_send, half_recv, *, tile):
     step = pl.program_id(0)
     steps = pl.num_programs(0)
     length, width = cot_ref.shape
@@ -115,7 +115,7 @@
     near = z + 1 - 2 * (z % 2)
     other_inner, other_end = 3 - z, 6 - 3 * z
     loads = [pltpu.make_async_copy(src, dst, w_sem.at[j]) for j, (src, dst) in enumerate(
-        ((wdown_hbm, wdown_ref), (wout_hbm, wout_ref), (wqkv_hbm, wqkv_ref), (wup_hbm, wup_ref)))]
+        ((cot_hbm, cot_ref), (own_hbm, own_ref), (wdown_hbm, wdown_ref), (wout_hbm, wout_ref), (wqkv_hbm, wqkv_ref), (wup_hbm, wup_ref)))]
 
     def span(i):
         return pl.ds(pl.multiple_of(i * rows, rows), rows)
@@ -128,7 +128,7 @@
         return remote(wants.at[0], wants.at[j], want_send.at[j], want_recv.at[j], (d, to))
 
     def near_copy(i):
-        return remote(own_ref.at[bit(i)], from_near.at[bit(i)], near_send.at[i], near_recv.at[i], (d, near))
+        return remote(own_hbm.at[bit(i)], from_near.at[bit(i)], near_send.at[i], near_recv.at[i], (d, near))
 
     def inner_copy(i):
         return remote(to_inner.at[bit(i)], from_half.at[bit(i)], inner_send.at[i], half_recv.at[i], (d, other_inner))
@@ -155,6 +155,8 @@
         barrier = pltpu.get_barrier_semaphore()
         for j in (1, 2, 3):
             pl.semaphore_signal(barrier, inc=1, device_id=(d, lax.rem(z + j, 4)), device_id_type=MESH)
+        for load in loads:
+            load.start()
         wants[0] = jnp.full(wants.shape[1:], want_ref[0] % 4, jnp.int32)
         pl.semaphore_wait(barrier, 3)
         for j in (1, 2, 3):
@@ -165,14 +167,13 @@
             return carry
 
         lax.fori_loop(0, parts, hand, 0)
-        for load in loads:
-            load.start()
         for vec, ref in ((g1_vec, g1_ref), (b1_vec, b1_ref), (bqkv_vec, bqkv_ref), (bout_vec, bout_ref), (g2_vec, g2_ref),
                          (b2_vec, b2_ref), (bup_vec, bup_ref), (bdown_vec, bdown_ref)):
             ref[...] = vec[...].reshape(1, -1)
         gain2_ref[...] = jnp.zeros_like(gain2_ref)
         shift2_ref[...] = jnp.zeros_like(shift2_ref)
         bup_out[...] = jnp.zeros_like(bup_out)
+        loads[0].wait()
         place = lax.broadcasted_iota(jnp.int32, (length, 1), 0)
         masked = jnp.where(place < count_ref[0], cot_ref[...].astype(F32), 0.0)
         gl_all[...] = masked.astype(BF16)
@@ -182,22 +183,27 @@
             ga_all[f] = nt(gl_all[...], wdown_ref[f * tile : (f + 1) * tile, :])
 
         tiles = ff // tile
-        loads[0].wait()
-        for f in range(2):
-            active(f)
+        loads[1].wait()
         for j in (1, 2, 3):
             want_copy(j).wait()
         relay(0)
         relay(1)
-        for f in range(2, tiles - 1):
+        loads[2].wait()
+        for f in range(tiles - 2):
             active(f)
         relay(2)
         relay(3)
-        active(tiles - 1)
-        loads[1].wait()
+        for f in range(tiles - 2, tiles):
+            active(f)
+        wide = jnp.broadcast_to(seg_ref[...].reshape(1, -1), (8, length)).astype(F32)
+        tall = wide.T[:, :1]
+        for b in range(0, length, PAIR):
+            earlier = jnp.where(wide[:1] < tall[b : b + PAIR], 1.0, 0.0)
+            begin_ref[b : b + PAIR, :] = jnp.sum(earlier, axis=1, keepdims=True).astype(jnp.int32)
+        loads[3].wait()
         for p in range(pairs):
             gc_all[p] = nt(gl_all[...], wout_ref[p * PAIR : (p + 1) * PAIR, :]).astype(BF16)
-        for load in loads[2:]:
+        for load in loads[4:]:
             load.wait()
 
     @pl.when((step > 0) & (step + 1 < chunks))
@@ -274,7 +280,7 @@
         lax.fori_loop(0, parts, done, 0)
 
 
-def front(count, want, own, cot, cosine, sine, g1, b1, wqkv, bqkv, wout, bout, g2, b2, wup, bup, wdown, bdown, rows=128, tile=512):
+def front(count, want, segment, own, cot, cosine, sine, g1, b1, wqkv, bqkv, wout, bout, g2, b2, wup, bup, wdown, bdown, rows=128, tile=512):
     length, width = own.shape
     ff = wup.shape[1]
     pairs = width // PAIR
@@ -299,22 +305,22 @@
     return pl.pallas_call(
         functools.partial(front_body, tile=tile),
         grid=(chunks,),
-        in_specs=[pl.BlockSpec(memory_space=pltpu.SMEM), pl.BlockSpec(memory_space=pltpu.SMEM), whole(own), whole(cot), row(PAIR), row(PAIR)]
-        + [whole(a) for a in vectors] + [pl.BlockSpec(memory_space=pl.ANY)] * 4,
+        in_specs=[pl.BlockSpec(memory_space=pltpu.SMEM), pl.BlockSpec(memory_space=pltpu.SMEM), whole(segment), row(PAIR), row(PAIR)]
+        + [whole(a) for a in vectors] + [pl.BlockSpec(memory_space=pl.ANY)] * 6,
         out_specs=[row(width)] + [heads] * 4 + [down] * 3
         + [pl.BlockSpec((width // PIECE, rows, PIECE), lambda i: (0, i, 0)), row(2 * ff)] + [row(width)] * 2
-        + [vec(width), vec(width), vec(ff), vec(width)],
+        + [vec(width), vec(width), vec(ff), vec(width)] + [pl.BlockSpec((length, 1), lambda i: (0, 0))],
         out_shape=[s((length, width), BF16)] + [s((pairs, length, PAIR), BF16)] * 4 + [s((width, length), BF16)] * 3
         + [s((width // PIECE, length, PIECE), BF16), s((length, 2 * ff), BF16)]
-        + [s((length, width), F32)] * 2 + [s((1, width), F32), s((1, width), F32), s((1, ff), F32), s((1, width), F32)],
+        + [s((length, width), F32)] * 2 + [s((1, width), F32), s((1, width), F32), s((1, ff), F32), s((1, width), F32)] + [s((length, 1), jnp.int32)],
         scratch_shapes=[pltpu.VMEM(w.shape, BF16) for w in weights]
         + [pltpu.VMEM((4, 8, 128), jnp.int32)] + [pltpu.VMEM((length, width), BF16)] * 4
         + [pltpu.VMEM((1, v.shape[0]), F32) for v in vectors]
-        + [pltpu.VMEM((length, width), BF16), pltpu.VMEM((ff // tile, length, tile), F32), pltpu.VMEM((pairs, length, PAIR), BF16)]
-        + [dma((4,)), dma((4,)), dma((4,))] + [dma((2 * chunks,))] * 5,
+        + [pltpu.VMEM((length, width), BF16)] * 3 + [pltpu.VMEM((ff // tile, length, tile), F32), pltpu.VMEM((pairs, length, PAIR), BF16)]
+        + [dma((6,)), dma((4,)), dma((4,))] + [dma((2 * chunks,))] * 5,
         compiler_params=pltpu.CompilerParams(vmem_limit_bytes=60 * 2**20, collective_id=1, has_side_effects=True),
         name="front",
-    )(count, want, own, cot, cosine, sine, *vectors, *weights)
+    )(count, want, segment, cosine, sine, *vectors, own, cot, *weights)
 
 
 def attention_body(q_ref, k_ref, v_ref, gc_ref, seg_ref, cos_ref, sin_ref,
@@ -474,7 +480,7 @@
         return total
 
 
-LAGS = dict(core=1, first=3, second=5, z=7, mid=9, back=10)
+LAGS = dict(core=1, first=3, second=5, z=7, mid=9, back=11)
 RING, CORE_RING, LINK_RING = 7, 6, 8
 
 
@@ -488,17 +494,17 @@
     return ("rest", 2 * j, 2 * j + 1) if j < wide else ("rest", j + wide)
 
 
-def back_body(count_ref, seg_ref, mlp_ref, q_ref, k_ref, v_ref, gc_ref, x_ref, base_ref, t2_ref, cos_ref, sin_ref, g1_ref,
+def back_body(count_ref, begin_ref, mlp_ref, q_ref, k_ref, v_ref, gc_ref, x_ref, base_ref, t2_ref, cos_ref, sin_ref, g1_ref,
               gain2_ref, shift2_ref, bup_ref, bout_ref, n2t_hbm, glt_hbm, n1t_hbm, gl_hbm, wout_hbm, wqkv_hbm,
               out_ref, ig_ref, total_ref, vec_ref,
-              left_mlp, left_rest, rhs, wout_ref, wqkv_ref, load_sem, ctx, dk_acc, dv_acc, begin_ref,
+              left_mlp, left_rest, rhs, wout_ref, wqkv_ref, load_sem, ctx, dk_acc, dv_acc,
               part, from_core, from_first, from_second, from_near, from_far,
               c_send, c_recv, f_send, f_recv, s_send, s_recv, n_send, n_recv, m_send, m_recv,
               dp_e, rows_e, dp_l, rows_l, e_send, e_recv, l_send, l_recv, gain1, shift1, bqkv, *, rows, row_ticks):
     tick = pl.program_id(0)
     at = Line()
     chunks, block = total_ref.shape[0], total_ref.shape[1]
-    length, width = seg_ref.shape[0], wout_ref.shape[0]
+    length, width = begin_ref.shape[0], wout_ref.shape[0]
     groups = width // PIECE
     per_group = length // rows
     n_mlp, pieces = 2 * bup_ref.shape[1] // CHUNK, 4 * groups
@@ -523,11 +529,6 @@
         pl.semaphore_wait(barrier, 10)
         for load in later_need:
             load.start()
-        wide = jnp.broadcast_to(seg_ref[...].reshape(1, -1), (8, length)).astype(F32)
-        tall = wide.T[:, :1]
-        for b in range(0, length, PAIR):
-            earlier = jnp.where(wide[:1] < tall[b : b + PAIR], 1.0, 0.0)
-            begin_ref[b : b + PAIR, :] = jnp.sum(earlier, axis=1, keepdims=True).astype(jnp.int32)
         gain1[...] = jnp.zeros_like(gain1)
         shift1[...] = jnp.zeros_like(shift1)
         bqkv[...] = jnp.zeros_like(bqkv)
@@ -572,7 +573,7 @@
         return remote(total_ref.at[i, :, lanes], from_far.at[i % LINK_RING, :, lanes], m_send.at[i], m_recv.at[i], at.far)
 
     def plus(a, b):
-        return (a.astype(F32) + b.astype(F32)).astype(BF16)
+        return a + b
 
     def put(h, half, cols, rows_of):
         even = 1 - tick % 2
@@ -714,10 +715,12 @@
             rhs[3 * g + 1, :, cols] = (dk * cos_ref[...] - turned(dk) * sin_ref[...]).astype(BF16)
             rhs[3 * g + 2, :, cols] = dv_acc[h].astype(BF16)
 
-    @pl.when((tick >= busy) & (tick < busy + row_ticks))
+    row_at = chunks - 2
+
+    @pl.when((tick >= row_at) & (tick < row_at + row_ticks))
     def _():
         n_rows = x_ref.shape[0]
-        here = pl.ds(pl.multiple_of((tick - busy) * n_rows, n_rows), n_rows)
+        here = pl.ds(pl.multiple_of((tick - row_at) * n_rows, n_rows), n_rows)
         attn = base_ref[...]
         for j in range(groups):
             attn = attn + nn(ctx[j, here, :], wout_ref[j * PIECE : (j + 1) * PIECE, :])
@@ -758,7 +761,7 @@
     def _():
         vec_ref[0] = early.end()
 
-    begin = busy + row_ticks
+    begin = row_at + row_ticks
 
     @pl.when(tick == begin)
     def _():
@@ -773,7 +776,7 @@
         vec_ref[1] = late.end()
 
 
-def back(count, segment, mlp, q, k, v, gc, x, base, t2, cosine, sine, g1, gain2, shift2, bup, bout, n2t, glt, n1t, gl, wout, wqkv,
+def back(count, begins, mlp, q, k, v, gc, x, base, t2, cosine, sine, g1, gain2, shift2, bup, bout, n2t, glt, n1t, gl, wout, wqkv,
          rows=256):
     length, width = x.shape
     ff = bup.shape[1]
@@ -784,10 +787,10 @@
     row_ticks = length // rows
     period = row_ticks + 1
     busy = groups * period
-    ticks = max(chunks + LAGS["back"], busy + row_ticks + 5)
+    ticks = max(chunks + LAGS["back"], chunks - 2 + row_ticks + 5)
 
     def row(cols):
-        return pl.BlockSpec((rows, cols), lambda t: (jnp.clip(t - busy, 0, row_ticks - 1), 0))
+        return pl.BlockSpec((rows, cols), lambda t: (jnp.clip(t - (chunks - 2), 0, row_ticks - 1), 0))
 
     def whole(a):
         return pl.BlockSpec(a.shape, lambda t: (0,) * a.ndim, pipeline_mode=pl.Buffered(1))
@@ -802,7 +805,7 @@
     return pl.pallas_call(
         functools.partial(back_body, rows=rows, row_ticks=row_ticks),
         grid=(ticks,),
-        in_specs=[pl.BlockSpec(memory_space=pltpu.SMEM), whole(segment), pl.BlockSpec((length, CHUNK), mlp_cols)]
+        in_specs=[pl.BlockSpec(memory_space=pltpu.SMEM), whole(begins), pl.BlockSpec((length, CHUNK), mlp_cols)]
         + [heads] * 4 + [row(width)] * 3
         + [whole(a) for a in (cosine, sine, g1, gain2, shift2, bup, bout)] + [pl.BlockSpec(memory_space=pl.ANY)] * len(loaded),
         out_specs=[row(width), row(width),
@@ -819,7 +822,6 @@
             pltpu.VMEM((groups, length, PIECE), BF16),
             pltpu.VMEM((GROUP, length, PAIR), F32),
             pltpu.VMEM((GROUP, length, PAIR), F32),
-            pltpu.VMEM((length, 1), jnp.int32),
             pltpu.VMEM((RING, 2, 2, 2, block, CHUNK), BF16),
             pltpu.VMEM((CORE_RING, 2, 2, block, CHUNK), BF16),
             pltpu.VMEM((LINK_RING, 2, block, CHUNK), BF16),
@@ -834,32 +836,53 @@
         ],
         compiler_params=pltpu.CompilerParams(vmem_limit_bytes=60 * 2**20, collective_id=0, has_side_effects=True),
         name="back",
-    )(count, segment, mlp, q, k, v, gc, x, base, t2, cosine, sine, g1, gain2, shift2, bup, bout, *loaded)
-
-
-def finish_body(out_hbm, ig_hbm, total_ref, vec_ref, out_to, ig_to, up_ref, down_ref, low_ref, qkv_ref,
-                gain1_ref, shift1_ref, bqkv_ref, bout_ref, gain2_ref, shift2_ref, bup_ref, bdown_ref, held, sem):
-    takes = [pltpu.make_async_copy(a, held.at[j], sem.at[j]) for j, a in enumerate((out_hbm, ig_hbm))]
-    copies = [pltpu.make_async_copy(held.at[j], a, sem.at[2 + j]) for j, a in enumerate((out_to, ig_to))]
+    )(count, begins, mlp, q, k, v, gc, x, base, t2, cosine, sine, g1, gain2, shift2, bup, bout, *loaded)
+
+
+def finish_body(out_hbm, ig_hbm, total_hbm, vec_ref, out_to, ig_to, up_to, down_to, low_to, qkv_to,
+                gain1_ref, shift1_ref, bqkv_ref, bout_ref, gain2_ref, shift2_ref, bup_ref, bdown_ref,
+                held, total_ref, up_ref, down_ref, low_ref, qkv_ref, sem):
+    load = pltpu.make_async_copy(total_hbm, total_ref, sem.at[0])
+    load.start()
+    takes = [pltpu.make_async_copy(a, held.at[j], sem.at[1 + j]) for j, a in enumerate((out_hbm, ig_hbm))]
+    copies = [pltpu.make_async_copy(held.at[j], a, sem.at[3 + j]) for j, a in enumerate((out_to, ig_to))]
     for take in takes:
         take.start()
     width, ff = gain1_ref.shape[0], bup_ref.shape[0]
     factor = 1.0 / vec_ref[0, 7:8, 0:1]
     groups = width // PIECE
     n_up = ff // CHUNK
+    load.wait()
+
+    def put(kinds):
+        for i in range(total_ref.shape[0]):
+            kind, *what = chunk_columns(i, 2 * n_up, 4 * groups, 2 * n_up // groups)
+            if kind not in kinds or (kind == "mlp" and what[0] // n_up != kinds[kind]):
+                continue
+            if kind == "mlp":
+                ref, j = (up_ref, down_ref)[kinds[kind]], what[0] % n_up
+                ref[:, j * CHUNK : (j + 1) * CHUNK] = total_ref[i].astype(F32) * factor
+                continue
+            for e, s in enumerate(what):
+                ref, col = (qkv_ref, (s % 3) * width + (s // 3) * PIECE) if s < 3 * groups else (low_ref, (s - 3 * groups) * PIECE)
+                ref[:, col : col + PIECE] = total_ref[i, :, e * PIECE : (e + 1) * PIECE].astype(F32) * factor
+
+    results = []
+
+    def send(ref, to):
+        results.append(pltpu.make_async_copy(ref, to, sem.at[5 + len(results)]))
+        results[-1].start()
+
+    put({"mlp": 0})
+    send(up_ref, up_to)
     for take, copy in zip(takes, copies):
         take.wait()
         copy.start()
-    for i in range(total_ref.shape[0]):
-        grad = total_ref[i].astype(F32) * factor
-        kind, *what = chunk_columns(i, 2 * n_up, 4 * groups, 2 * n_up // groups)
-        if kind == "mlp":
-            ref, j = (up_ref, what[0]) if what[0] < n_up else (down_ref, what[0] - n_up)
-            ref[:, j * CHUNK : (j + 1) * CHUNK] = grad
-            continue
-        for e, s in enumerate(what):
-            ref, col = (qkv_ref, (s % 3) * width + (s // 3) * PIECE) if s < 3 * groups else (low_ref, (s - 3 * groups) * PIECE)
-            ref[:, col : col + PIECE] = grad[:, e * PIECE : (e + 1) * PIECE]
+    put({"mlp": 1})
+    send(down_ref, down_to)
+    put({"rest": 0})
+    send(low_ref, low_to)
+    send(qkv_ref, qkv_to)
     first, second = vec_ref[0] * factor, vec_ref[1] * factor
     for j in range(ff // width):
         bup_ref[j * width : (j + 1) * width] = first[j]
@@ -869,30 +892,30 @@
         ref[...] = line
     for j in range(3):
         bqkv_ref[j * width : (j + 1) * width] = second[2 + j]
-    for copy in copies:
+    for copy in copies + results:
         copy.wait()
 
 
 def finish(out, ig, total, vec, ff):
     length, width = out.shape
     block = total.shape[1]
-
     s = jax.ShapeDtypeStruct
     hbm, vmem = pl.BlockSpec(memory_space=pltpu.HBM), pl.BlockSpec(memory_space=pltpu.VMEM)
     vectors = (width, width, 3 * width, width, width, width, ff, width)
+    grads = [(block, ff), (block, ff), (block, width), (block, 3 * width)]
     return pl.pallas_call(
         finish_body,
-        in_specs=[hbm, hbm, vmem, vmem],
-        out_specs=[hbm, hbm] + [vmem] * 12,
-        out_shape=[s(out.shape, BF16), s(ig.shape, BF16), s((block, ff), F32), s((block, ff), F32), s((block, width), F32),
-                   s((block, 3 * width), F32)] + [s((n,), F32) for n in vectors],
-        scratch_shapes=[pltpu.VMEM((2, length, width), BF16), pltpu.SemaphoreType.DMA((4,))],
+        in_specs=[hbm, hbm, hbm, vmem],
+        out_specs=[hbm] * 6 + [vmem] * 8,
+        out_shape=[s(out.shape, BF16), s(ig.shape, BF16)] + [s(shape, F32) for shape in grads] + [s((n,), F32) for n in vectors],
+        scratch_shapes=[pltpu.VMEM((2, length, width), BF16), pltpu.VMEM(total.shape, BF16)]
+        + [pltpu.VMEM(shape, F32) for shape in grads] + [pltpu.SemaphoreType.DMA((9,))],
         compiler_params=pltpu.CompilerParams(vmem_limit_bytes=60 * 2**20),
         name="finish",
     )(out, ig, total, vec)
 
 
-def by_collectives(count, segment, mlp, q, k, v, gc, x, base, t2, cosine, sine, g1, gain2, shift2, bup, bout, n2t, glt, n1t, gl,
+def by_collectives(segment, count, begins, mlp, q, k, v, gc, x, base, t2, cosine, sine, g1, gain2, shift2, bup, bout, n2t, glt, n1t, gl,
                    wout, wqkv):
     width, ff = x.shape[1], bup.shape[1]
     ctx, ctxt, gu = attention(q, k, v, gc, segment, cosine, sine)
@@ -930,11 +953,11 @@
     length, width = cotangent.shape
     ff = up_weight.shape[1]
     cosine, sine = (jnp.asarray(t) for t in rotary_tables(length))
-    (arrived, q, k, v, gc, n1t, n2t, glt, gl, mlp, base, t2, gain2, shift2, bias_up, bias_out) = front(
-        true_counts, regroup, tokens, cotangent, cosine, sine, ln1_gain, ln1_bias, qkv_weight, qkv_bias, out_weight, out_bias,
+    (arrived, q, k, v, gc, n1t, n2t, glt, gl, mlp, base, t2, gain2, shift2, bias_up, bias_out, begins) = front(
+        true_counts, regroup, segment_ids, tokens, cotangent, cosine, sine, ln1_gain, ln1_bias, qkv_weight, qkv_bias, out_weight, out_bias,
         ln2_gain, ln2_bias, up_weight, up_bias, down_weight, down_bias)
-    last = back if (lax.axis_size("dp"), lax.axis_size("rows")) == (8, 4) else by_collectives
-    out, input_grad, total, vec = last(true_counts, segment_ids, mlp, q, k, v, gc, arrived, base, t2, cosine, sine, ln1_gain, gain2,
+    last = back if (lax.axis_size("dp"), lax.axis_size("rows")) == (8, 4) else functools.partial(by_collectives, segment_ids)
+    out, input_grad, total, vec = last(true_counts, begins, mlp, q, k, v, gc, arrived, base, t2, cosine, sine, ln1_gain, gain2,
                                        shift2, bias_up, bias_out, n2t, glt, n1t, gl, out_weight, qkv_weight)
     (out, input_grad, up, down, low, qkv, gain1, shift1, bias_qkv, bias_out, gain2, shift2, bias_up, bias_down) = finish(
         out, input_grad, total, vec, up_weight.shape[1])

time: 209 us -> 204 us (0.976)
  Pallas kernels: 206 us -> 201 us
    pallas_call x1, Pallas kernels: 112 us -> 109 us  [back(): pl.pallas_call(functools.partial(back_body, rows=rows, row_ticks=row_tick...]
where the time goes in v7:
time: 204 us; the launch traced here: 203 us
  Pallas kernels  201 us (99%)
  between operations  2.12 us (1%)
    pallas_call x1, Pallas kernels, back(): pl.pallas_call(functools.partial(back_body, rows=rows, row_ticks=row_tick...  109 us
    pallas_call x1, Pallas kernels, front(): pl.pallas_call(functools.partial(front_body, tile=tile), grid=(chunks,),...  85.9 us
    pallas_call x1, Pallas kernels, finish(): pl.pallas_call(finish_body, in_specs=[hbm, hbm, hbm, vmem], out_specs=[hb...  5.98 us

profile of v7, /device:TPU:0, one launch (start us, length us, event | category | flops | bytes accessed | tf_op | source)
XLA Modules:
  0.0 203.5 jit_solution(6983308383061833473)
XLA Ops:
  1.9 85.9 %front.1 = (bf16[1024,768]{1,0:T(8,128)(2,1)}, bf16[6,1024,128]{2,1,0:T(8,128)(2,1)}, bf16[6,1024,128]{2,1,0:T(8,128)(2,1)}, bf16[6,1024,128]{2,1,0:T(8,128)(2,1...) custom-call(s32[1]{0:T(128)S(6)} %copy.33.count_ref, ...), custom_call_target="tpu_custom_call" | custom-call | tf_op jit(solution)/shard_map/front/pallas_call | solution.py:305
  87.9 109.4 %back.1 = (bf16[1024,768]{1,0:T(8,128)(2,1)}, bf16[1024,768]{1,0:T(8,128)(2,1)}, bf16[20,96,512]{2,1,0:T(8,128)(2,1)}, f32[2,8,768]{2,1,0:T(8,128)}) custom-call(s32[1]{0:T(128)S(6)} %copy.33.count_ref, s32[1024,1]{1,0:T(8,128)} %get-tuple-element.49.begin_ref, bf16[1024,6144]{1,0:T(8,128)(2,1)} %get-tuple-element.50.mlp_ref, ...), custom_call_target="tpu_custom_call" | custom-call | tf_op jit(solution)/shard_map/back/pallas_call | solution.py:805
  197.3 6.0 %finish.1 = (bf16[1024,768]{1,0:T(8,128)(2,1)}, bf16[1024,768]{1,0:T(8,128)(2,1)}, f32[96,3072]{1,0:T(8,128)}, f32[96,3072]{1,0:T(8,128)}, f32[96,768]{1,0:T(8,1...) custom-call(bf16[1024,768]{1,0:T(8,128)(2,1)} %get-tuple-element.66., ...), custom_call_target="tpu_custom_call" | custom-call | tf_op jit(solution)/shard_map/finish/pallas_call | solution.py:906

commit v8 on v7

--- a/solution.py
+++ b/solution.py
@@ -67,19 +67,23 @@
 
 
 def attend(q, k, v, gc, begins, t_first):
-    each, rows, span = range(len(q)), q[0].shape[0], k[0].shape[0]
+    each, rows = range(len(q)), q[0].shape[0]
     low = lax.broadcasted_iota(jnp.int32, (rows, PAIR), 1) < HEAD_DIM
 
     def both(t):
         zero = jnp.zeros_like(t)
         return jnp.concatenate([jnp.where(low, t, zero), jnp.where(low, zero, t)], axis=0)
 
+    def allowed(h):
+        span = k[h].shape[0]
+        s_at = lax.broadcasted_iota(jnp.int32, (rows, span), 1)
+        t_at = t_first[h] + lax.broadcasted_iota(jnp.int32, (rows, span), 0)
+        seen = (s_at >= begins[h]) & (s_at <= t_at)
+        return jnp.concatenate([seen, seen], axis=0)
+
+    seen = {t_first[h]: allowed(h) for h in each}
     q2, g2 = [both(t) for t in q], [both(t) for t in gc]
-    s_at = lax.broadcasted_iota(jnp.int32, (rows, span), 1)
-    t_at = t_first + lax.broadcasted_iota(jnp.int32, (rows, span), 0)
-    allowed = (s_at >= begins) & (s_at <= t_at)
-    allowed = jnp.concatenate([allowed, allowed], axis=0)
-    scores = [jnp.where(allowed, nt(q2[h], k[h]), EXCLUDED) for h in each]
+    scores = [jnp.where(seen[t_first[h]], nt(q2[h], k[h]), EXCLUDED) for h in each]
     dp = [nt(g2[h], v[h]) for h in each]
     e = [jnp.exp(scores[h] - jnp.max(scores[h], axis=1, keepdims=True)) for h in each]
     p = [e[h] * (1.0 / jnp.sum(e[h], axis=1, keepdims=True)) for h in each]
@@ -684,18 +688,18 @@
     each = range(GROUP)
 
     def unit(b):
-        span = (b + 1) * rows
-        mine = slice(b * rows, span)
-        context, dq, dk, dv = attend([q_ref[h, mine, :] for h in each], [k_ref[h, :span, :] for h in each],
-                                     [v_ref[h, :span, :] for h in each], [gc_ref[h, mine, :] for h in each],
-                                     begin_ref[mine, :], b * rows)
-        for h in each:
-            cols = slice(h * PAIR, (h + 1) * PAIR)
-            dk_acc[h, :span, :] += dk[h]
-            dv_acc[h, :span, :] += dv[h]
-            ctx[g, mine, cols] = context[h]
-            left_rest[1, pl.ds(pl.multiple_of(g * PIECE + h * PAIR, PAIR), PAIR), mine] = context[h].T
-            rhs[3 * g, mine, cols] = (dq[h] * cos_ref[mine, :] - turned(dq[h]) * sin_ref[mine, :]).astype(BF16)
+        part = rows // 2
+        blocks = [(h, b * rows + j * part) for j in range(2) for h in each]
+        context, dq, dk, dv = attend([q_ref[h, t : t + part, :] for h, t in blocks], [k_ref[h, : t + part, :] for h, t in blocks],
+                                     [v_ref[h, : t + part, :] for h, t in blocks], [gc_ref[h, t : t + part, :] for h, t in blocks],
+                                     [begin_ref[t : t + part, :] for h, t in blocks], [t for h, t in blocks])
+        for i, (h, t) in enumerate(blocks):
+            cols, mine = slice(h * PAIR, (h + 1) * PAIR), slice(t, t + part)
+            dk_acc[h, : t + part, :] += dk[i]
+            dv_acc[h, : t + part, :] += dv[i]
+            ctx[g, mine, cols] = context[i]
+            left_rest[1, pl.ds(pl.multiple_of(g * PIECE + h * PAIR, PAIR), PAIR), mine] = context[i].T
+            rhs[3 * g, mine, cols] = (dq[i] * cos_ref[mine, :] - turned(dq[i]) * sin_ref[mine, :]).astype(BF16)
 
     @pl.when(attending & (spot == 0))
     def _():

time: 204 us -> 202 us (level)
  no operation moved by 1% of the time
where the time goes in v8:
time: 202 us
  Pallas kernels  200 us (99%)
  between operations  2.12 us (1%)
    pallas_call x1, Pallas kernels, back(): pl.pallas_call(functools.partial(back_body, rows=rows, row_ticks=row_tick...  108 us
    pallas_call x1, Pallas kernels, front(): pl.pallas_call(functools.partial(front_body, tile=tile), grid=(chunks,),...  85.9 us
    pallas_call x1, Pallas kernels, finish(): pl.pallas_call(finish_body, in_specs=[hbm, hbm, hbm, vmem], out_specs=[hb...  5.98 us

profile of v8, /device:TPU:0, one launch (start us, length us, event | category | flops | bytes accessed | tf_op | source)
XLA Modules:
  0.0 202.0 jit_solution(4994302862479553914)
XLA Ops:
  1.9 85.9 %front.1 = (bf16[1024,768]{1,0:T(8,128)(2,1)}, bf16[6,1024,128]{2,1,0:T(8,128)(2,1)}, bf16[6,1024,128]{2,1,0:T(8,128)(2,1)}, bf16[6,1024,128]{2,1,0:T(8,128)(2,1...) custom-call(s32[1]{0:T(128)S(6)} %copy.33.count_ref, ...), custom_call_target="tpu_custom_call" | custom-call | tf_op jit(solution)/shard_map/front/pallas_call | solution.py:309
  87.9 107.9 %back.1 = (bf16[1024,768]{1,0:T(8,128)(2,1)}, bf16[1024,768]{1,0:T(8,128)(2,1)}, bf16[20,96,512]{2,1,0:T(8,128)(2,1)}, f32[2,8,768]{2,1,0:T(8,128)}) custom-call(s32[1]{0:T(128)S(6)} %copy.33.count_ref, s32[1024,1]{1,0:T(8,128)} %get-tuple-element.49.begin_ref, bf16[1024,6144]{1,0:T(8,128)(2,1)} %get-tuple-element.50.mlp_ref, ...), custom_call_target="tpu_custom_call" | custom-call | tf_op jit(solution)/shard_map/back/pallas_call | solution.py:809
  195.8 6.0 %finish.1 = (bf16[1024,768]{1,0:T(8,128)(2,1)}, bf16[1024,768]{1,0:T(8,128)(2,1)}, f32[96,3072]{1,0:T(8,128)}, f32[96,3072]{1,0:T(8,128)}, f32[96,768]{1,0:T(8,1...) custom-call(bf16[1024,768]{1,0:T(8,128)(2,1)} %get-tuple-element.66., ...), custom_call_target="tpu_custom_call" | custom-call | tf_op jit(solution)/shard_map/finish/pallas_call | solution.py:910

commit v9 on v8

--- a/solution.py
+++ b/solution.py
@@ -284,7 +284,7 @@
         lax.fori_loop(0, parts, done, 0)
 
 
-def front(count, want, segment, own, cot, cosine, sine, g1, b1, wqkv, bqkv, wout, bout, g2, b2, wup, bup, wdown, bdown, rows=128, tile=512):
+def front(count, want, segment, own, cot, cosine, sine, g1, b1, wqkv, bqkv, wout, bout, g2, b2, wup, bup, wdown, bdown, rows=128, tile=768):
     length, width = own.shape
     ff = wup.shape[1]
     pairs = width // PAIR
@@ -579,28 +579,22 @@
     def plus(a, b):
         return a + b
 
-    def put(h, half, cols, rows_of):
+    def put(cols, rows_of):
         even = 1 - tick % 2
-        for j in range(4):
-            d = h * 4 + j
-            c, x, y = d % 2, (d // 2) % 2, d // 4
+        for j in range(8):
+            c, x, y = j % 2, (j // 2) % 2, j // 4
             a = x * even + y * (1 - even)
             b = y * even + x * (1 - even)
             part[tick % RING, c, a, b, :, cols] = rows_of[j * block : (j + 1) * block].astype(BF16)
 
-    half = width // 2
-
     @pl.when(attending)
     def _():
         left = (per_group * g + spot) // (n_mlp // 2)
-        for h in range(2):
-            put(h, half, slice(0, CHUNK), nn(left_mlp[left, h * half : (h + 1) * half, :], mlp_ref[...]))
+        put(slice(0, CHUNK), nn(left_mlp[left], mlp_ref[...]))
         core_copy(tick, CHUNK).start()
 
     def rest(s, e):
-        for h in range(2):
-            put(h, half, slice(e * PIECE, (e + 1) * PIECE),
-                nn(left_rest[s // (3 * groups), h * half : (h + 1) * half, :], rhs[s]))
+        put(slice(e * PIECE, (e + 1) * PIECE), nn(left_rest[s // (3 * groups)], rhs[s]))
 
     @pl.when((tick < n_wide) & jnp.logical_not(attending))
     def _():

time: 202 us -> 202 us (level)
  no operation moved by 1% of the time
where the time goes in v9:
time: 202 us; the launch traced here: 201 us
  Pallas kernels  199 us (99%)
  between operations  2.12 us (1%)
    pallas_call x1, Pallas kernels, back(): pl.pallas_call(functools.partial(back_body, rows=rows, row_ticks=row_tick...  108 us
    pallas_call x1, Pallas kernels, front(): pl.pallas_call(functools.partial(front_body, tile=tile), grid=(chunks,),...  85.3 us
    pallas_call x1, Pallas kernels, finish(): pl.pallas_call(finish_body, in_specs=[hbm, hbm, hbm, vmem], out_specs=[hb...  5.98 us

profile of v9, /device:TPU:0, one launch (start us, length us, event | category | flops | bytes accessed | tf_op | source)
XLA Modules:
  0.0 201.4 jit_solution(8673430987948313094)
XLA Ops:
  1.9 85.3 %front.1 = (bf16[1024,768]{1,0:T(8,128)(2,1)}, bf16[6,1024,128]{2,1,0:T(8,128)(2,1)}, bf16[6,1024,128]{2,1,0:T(8,128)(2,1)}, bf16[6,1024,128]{2,1,0:T(8,128)(2,1...) custom-call(s32[1]{0:T(128)S(6)} %copy.33.count_ref, ...), custom_call_target="tpu_custom_call" | custom-call | tf_op jit(solution)/shard_map/front/pallas_call | solution.py:309
  87.2 108.0 %back.1 = (bf16[1024,768]{1,0:T(8,128)(2,1)}, bf16[1024,768]{1,0:T(8,128)(2,1)}, bf16[20,96,512]{2,1,0:T(8,128)(2,1)}, f32[2,8,768]{2,1,0:T(8,128)}) custom-call(s32[1]{0:T(128)S(6)} %copy.33.count_ref, s32[1024,1]{1,0:T(8,128)} %get-tuple-element.49.begin_ref, bf16[1024,6144]{1,0:T(8,128)(2,1)} %get-tuple-element.50.mlp_ref, ...), custom_call_target="tpu_custom_call" | custom-call | tf_op jit(solution)/shard_map/back/pallas_call | solution.py:803
  195.2 6.0 %finish.1 = (bf16[1024,768]{1,0:T(8,128)(2,1)}, bf16[1024,768]{1,0:T(8,128)(2,1)}, f32[96,3072]{1,0:T(8,128)}, f32[96,3072]{1,0:T(8,128)}, f32[96,768]{1,0:T(8,1...) custom-call(bf16[1024,768]{1,0:T(8,128)(2,1)} %get-tuple-element.66., ...), custom_call_target="tpu_custom_call" | custom-call | tf_op jit(solution)/shard_map/finish/pallas_call | solution.py:904
